TPU v7x, 128 devices: a whole 4x4x4 slice. The times are simulated.
128 devices in a mesh: aux: 16 (over z, y), bas: 8 (over x, core).
Axes of the slice: x: 4, y: 4, z: 4, core: 2. Of those that a mesh axis runs over, the one named last changes fastest.
Arguments:
- tiles: bfloat16 [16384, 4, 32, 128], P(('aux', 'bas')), may hold values from -6 to 6
- tile_owner: int32 [16384, 1], replicated, may hold values from 0 to 127; in each aligned block of 128 rows (0 to 127, 128 to 255, ...) at most 2 rows name the same one
- pair_rows: int32 [16384], replicated, may hold values from 0 to 639
- pair_cols: int32 [16384], replicated, may hold values from 0 to 159
- orbitals: bfloat16 [32, 20480], replicated, may hold values from -0.5 to 0.5
- support: int32 [32, 160], replicated, may hold values 0 or 1
Outputs:
- exchange: float32 [20480, 20480], P('aux', 'bas')
Inputs may be any that keep to these rules, and one draw needn't show every extreme that they name: tile_owner[t, 0] is the device that half-transforms tile t, numbered aux index times 8 plus bas index; the integrals of tile t belong to auxiliary block tile_owner[t, 0] // 8. Among the 128 rows of one device no value appears more than 2 times, and some value appears exactly 2 times.
All inputs are finite; a program needn't handle non-finite values.
Results may differ from a plain program's by a relative error of at most 0.0075.
Values may be sent and summed in bfloat16 or wider, within the bound.
No kernel may reach another device: no remote copies, remote signals or barrier semaphores. Data moves between devices by JAX's collectives and lax.ppermute only.
A program may use at most 128 MiB of HBM per device.

v0:
```python
import jax
import jax.numpy as jnp
from jax import lax
from jax.sharding import PartitionSpec as P

NBAS = 20480


def from_root(shard, axis, root):
    mine = lax.axis_index(axis) == root
    return lax.psum(jnp.where(mine, shard, jnp.zeros_like(shard)), axis)


def masked_blocks(orbitals, support):
    orbital_count, basis_count = orbitals.shape
    block_count = support.shape[1]
    block_width = basis_count // block_count
    kept = jnp.repeat(support, block_width, axis=1) == 1
    coefficient = jnp.where(kept, orbitals, jnp.zeros_like(orbitals))
    return coefficient.reshape(orbital_count, block_count, block_width).transpose(1, 0, 2)


def half_transform(tile_block, chosen):
    leading = tile_block.shape[:-3]
    aux_count, tile_rows, tile_cols = tile_block.shape[-3:]
    orbital_count = chosen.shape[-2]
    product = jnp.einsum("kpmn,kin->kmpi", tile_block, chosen, preferred_element_type=jnp.float32)
    return product.reshape(leading + (tile_rows, aux_count * orbital_count)).astype(jnp.bfloat16)


def slot_ranks(owners, tiles_here):
    positions = jnp.arange(tiles_here, dtype=jnp.int32)
    matching = owners[:, :, None] == owners[:, None, :]
    earlier = positions[None, :] < positions[:, None]
    return jnp.sum(jnp.logical_and(matching, earlier[None]), axis=2)


def shards(tiles, tile_owner, pair_rows, pair_cols, orbitals, support):
    aux_count = lax.axis_size("aux")
    bas_count = lax.axis_size("bas")
    devices = aux_count * bas_count
    tiles_here = tiles.shape[0]
    capacity = max(2, 2 * tiles_here // devices)
    slot_count = devices * capacity
    aux_place = lax.axis_index("aux")
    bas_place = lax.axis_index("bas")
    myself = aux_place * bas_count + bas_place
    owners = tile_owner[:, 0].reshape(devices, tiles_here)
    rows_all = pair_rows.reshape(devices, tiles_here)
    cols_all = pair_cols.reshape(devices, tiles_here)
    ranks = slot_ranks(owners, tiles_here)
    coefficient = masked_blocks(orbitals, support)
    my_owner = lax.dynamic_index_in_dim(owners, myself, 0, keepdims=False)
    my_rank = lax.dynamic_index_in_dim(ranks, myself, 0, keepdims=False)
    target = my_owner * capacity + my_rank
    slot_index = jnp.arange(slot_count, dtype=jnp.int32)
    slot_hits = target[None, :] == slot_index[:, None]
    filled = jnp.any(slot_hits, axis=1)
    source = jnp.sum(
        jnp.where(slot_hits, jnp.arange(tiles_here, dtype=jnp.int32)[None, :], 0), axis=1
    )
    owned = owners == myself
    which_slot = jnp.arange(capacity, dtype=jnp.int32)
    picked = jnp.logical_and(owned[:, None, :], ranks[:, None, :] == which_slot[None, :, None])
    live_slot = jnp.any(picked, axis=2).reshape(slot_count)
    slot_rows = jnp.sum(jnp.where(picked, rows_all[:, None, :], 0), axis=2).reshape(slot_count)
    slot_cols = jnp.sum(jnp.where(picked, cols_all[:, None, :], 0), axis=2).reshape(slot_count)
    outgoing = jnp.where(filled[:, None, None, None], tiles[source], jnp.zeros((), jnp.bfloat16))
    arrived = lax.all_to_all(
        outgoing.reshape((devices, capacity) + outgoing.shape[1:]),
        ("aux", "bas"),
        split_axis=0,
        concat_axis=0,
        tiled=True,
    )
    arrived = arrived.reshape((slot_count,) + outgoing.shape[1:])
    halves = half_transform(arrived, coefficient[slot_cols])
    tile_rows = halves.shape[1]
    width = halves.shape[2]
    flat_halves = halves.reshape(slot_count, tile_rows * width)
    block_ids = jnp.arange(NBAS // bas_count * lax.axis_size("bas") // tile_rows, dtype=jnp.int32)
    onehot = jnp.logical_and(slot_rows[None, :] == block_ids[:, None], live_slot[None, :]).astype(
        jnp.bfloat16
    )
    summed = jnp.dot(onehot, flat_halves, preferred_element_type=jnp.float32)
    local_rows = lax.psum_scatter(
        summed.reshape(NBAS // bas_count * lax.axis_size("bas"), width).astype(jnp.bfloat16),
        "bas",
        scatter_dimension=0,
        tiled=True,
    )
    columns = lax.all_gather(local_rows, "aux", axis=1, tiled=True)
    group_ratio = aux_count // bas_count
    band_rows = NBAS // aux_count
    own_part = lax.dynamic_slice_in_dim(columns, aux_place % group_ratio * band_rows, band_rows, 0)
    row_data = from_root(own_part, "bas", aux_place // group_ratio)
    factor = 1.0 / columns.shape[1]
    result_block = lax.dot_general(
        row_data, columns, (((1,), (1,)), ((), ())), preferred_element_type=jnp.float32
    )
    return result_block * factor


def solution(mesh):
    in_specs = (P(("aux", "bas"), None, None, None), P(), P(), P(), P(), P())
    out_specs = P("aux", "bas")
    return jax.shard_map(shards, mesh=mesh, in_specs=in_specs, out_specs=out_specs, check_vma=False)
```

profile of v0, /device:TPU:0, one launch (start us, length us, event | category | flops | bytes accessed | tf_op | source)
XLA Modules:
  0.0 433.3 jit_solution(1781522440067708799)
XLA Ops:
  6.6 0.9 broadcast_compare_fusion
  7.4 6.3 %convert_reduce_fusion = s32[128,128]{1,0:T(8,128)S(1)} fusion(s32[128,128]{1,0:T(8,128)} %bitcast.39, pred[128,128]{1,0:T(8,128)(4,1)S(1)} %iota_compare_fusion.3), kind=kLoop, calls=%fused_computation.4 | loop fusion | flops 8372224 | bytes 147456 | tf_op jit(solution)/shard_map/reduce_sum | solution.py:35
  13.7 0.7 fusion.11
  14.4 0.1 fusion.6
  14.5 0.1 select_reduce_fusion
  14.7 0.2 broadcast_in_dim.77
  14.8 1.0 select_reduce_fusion.2
  15.8 0.1 copy.13
  16.0 0.1 reshape.89
  16.1 10.8 %gather_fusion.1 = bf16[256,4,32,128]{3,2,1,0:T(8,128)(2,1)} fusion(bf16[128,4,32,128]{3,2,1,0:T(8,128)(2,1)} %param.6, s32[1024]{0:T(1024)S(1)} %pad_clamp_fusion), kind=kCustom, calls=%fused_computation.1 | custom fusion | bytes 16778240 | tf_op jit(solution)/shard_map/gather | solution.py:68
  26.9 7.4 %broadcast_select_fusion = bf16[128,2,4,32,128]{4,3,2,1,0:T(8,128)(2,1)} fusion(bf16[128,2,4,32,128]{4,3,2,1,0:T(8,128)(2,1)} %bitcast.35, pred[128,2]{1,0:T(8,128)(4,1)S(1)} %broadcast_in_dim.77), kind=kLoop, calls=%fused_computation.5 | loop fusion | flops 4194304 | bytes 16777472 | tf_op jit(solution)/shard_map/jit(_where)/select_n | solution.py:68
  34.4 0.0 copy-start.1
  34.4 0.0 copy-start
  34.4 11.7 %all-to-all-start = ((bf16[128,2,4,32,128]{4,3,2,1,0:T(8,128)(2,1)}), bf16[128,2,4,32,128]{4,3,2,1,0:T(8,128)(2,1)}, u32[]{:S(2)}, u32[]{:S(2)}) async-start(bf16[128,2,4,32,128]{4,3,2,1,0:T(8,128)(2,1)} %broadcast_select_fusion), calls=%async_computation | async-start | bytes 16777216 | tf_op jit(solution)/shard_map/all_to_all | solution.py:69
  46.1 0.2 reduce-scatter.2.cloned.1.call-start
  46.3 0.1 fusion.8
  46.4 0.1 copy.11
  46.5 0.2 and.43
  46.7 0.1 copy.10
  46.8 0.1 eq.90
  47.0 0.0 copy-done.1
  47.0 1.0 broadcast_in_dim.73
  48.0 0.0 copy-done
  48.0 0.5 bitcast_bitcast_fusion
  48.5 1.0 gather_fusion
  49.5 95.0 %all-to-all-done = bf16[128,2,4,32,128]{4,3,2,1,0:T(8,128)(2,1)} async-done(((bf16[128,2,4,32,128]{4,3,2,1,0:T(8,128)(2,1)}), bf16[128,2,4,32,128]{4,3,2,1,0:T(8,128)(2,1)}, u32[]{:S(2)}, u32[]{:S(2)}) %all-to-all-start) | async-done | bytes 8388640 | tf_op jit(solution)/shard_map/all_to_all | solution.py:69
  144.5 19.4 %convert_bitcast_fusion = bf16[256,32,4,32]{1,3,2,0:T(8,128)(2,1)} fusion(bf16[256,4,32,128]{3,2,1,0:T(8,128)(2,1)} %bitcast.11, bf16[256,32,128]{2,1,0:T(8,128)(2,1)S(1)} %gather_fusion), kind=kOutput, calls=%fused_computation.3 | convolution fusion | flops 269484032 | bytes 12582912 | tf_op jit(solution)/shard_map/kpmn,kin->kmpi/dot_general | solution.py:27
  163.9 11.1 %copy.14 = bf16[256,32,4,32]{0,3,2,1:T(8,128)(2,1)S(1)} copy(bf16[256,32,4,32]{1,3,2,0:T(8,128)(2,1)} %convert_bitcast_fusion) | data formatting | bytes 4194304 | tf_op jit(solution)/shard_map/convert_element_type | solution.py:28
  175.0 3.9 convolution_convert_fusion
  178.9 8.9 %convert_element_type.25 = bf16[20480,128]{1,0:T(8,128)(2,1)} reshape(bf16[640,4096]{1,0:T(8,128)(2,1)} %convolution_convert_fusion) | data formatting | bytes 10485760 | tf_op jit(solution)/shard_map/convert_element_type | solution.py:87
  187.8 0.0 reduce-scatter.2.cloned.1.call-update
  187.8 0.0 all-gather.2.cloned.1.call-start
  187.9 44.6 %reduce-scatter.2.cloned.1.call-done = bf16[2560,128]{1,0:T(8,128)(2,1)} async-done(((bf16[20480,128]{1,0:T(8,128)(2,1)}), bf16[2560,128]{1,0:T(8,128)(2,1)}) %reduce-scatter.2.cloned.1.call-update) | async-done | bytes 655376 | tf_op jit(solution)/shard_map/reduce_scatter | solution.py:86
  232.5 0.0 all-gather.2.cloned.1.call-update
  232.5 0.3 all-reduce.2.cloned.1.call-start
  232.8 90.5 %all-gather.2.cloned.1.call-done = bf16[2560,2048]{1,0:T(8,128)(2,1)} async-done(((bf16[2560,128]{1,0:T(8,128)(2,1)}), bf16[2560,2048]{1,0:T(8,128)(2,1)}) %all-gather.2.cloned.1.call-update) | async-done | bytes 10485776 | tf_op jit(solution)/shard_map/all_gather | solution.py:92
  323.4 6.6 %dynamic-slice_select_fusion = bf16[1280,2048]{1,0:T(8,128)(2,1)} fusion(bf16[2560,2048]{1,0:T(8,128)(2,1)} %all-gather.2.cloned.1.call-done, s32[]{:T(128)S(6)} %select_n.78, pred[]{:T(512)S(6)} %eq.81), kind=kLoop, calls=%fused_computation.7 | loop fusion | flops 2621440 | bytes 10485765 | tf_op jit(solution)/shard_map/jit(_where)/select_n | solution.py:11
  330.0 0.0 all-reduce.2.cloned.1.call-update
  330.0 75.9 %all-reduce.2.cloned.1.call-done = bf16[1280,2048]{1,0:T(8,128)(2,1)} async-done(((bf16[1280,2048]{1,0:T(8,128)(2,1)}), bf16[1280,2048]{1,0:T(8,128)(2,1)}) %all-reduce.2.cloned.1.call-update) | async-done | bytes 5242896 | tf_op jit(solution)/shard_map/psum | solution.py:11
  405.9 20.9 %convolution_multiply_fusion = f32[1280,2560]{1,0:T(8,128)} fusion(bf16[1280,2048]{1,0:T(8,128)(2,1)} %all-reduce.2.cloned.1.call-done, bf16[2560,2048]{1,0:T(8,128)(2,1)} %all-gather.2.cloned.1.call-done), kind=kOutput, calls=%fused_computation.2 | convolution fusion | flops 13425049600 | bytes 28835840 | tf_op jit(solution)/shard_map/dot_general | solution.py:98
  (5 shorter events, 0.0 us)
Async XLA Ops:
  34.4 12.6 %copy-start.1 = (s32[32,160]{1,0:T(8,128)S(1)}, s32[32,160]{1,0:T(8,128)}, u32[]{:S(2)}) copy-start(s32[32,160]{1,0:T(8,128)} %param.11) | copy-start | bytes 61444
  34.4 13.6 %copy-start = (bf16[32,20480]{1,0:T(8,128)(2,1)S(1)}, bf16[32,20480]{1,0:T(8,128)(2,1)}, u32[]{:S(2)}) copy-start(bf16[32,20480]{1,0:T(8,128)(2,1)} %param.10) | copy-start | bytes 3932164
  34.4 110.1 %all-to-all-start = ((bf16[128,2,4,32,128]{4,3,2,1,0:T(8,128)(2,1)}), bf16[128,2,4,32,128]{4,3,2,1,0:T(8,128)(2,1)}, u32[]{:S(2)}, u32[]{:S(2)}) async-start(bf16[128,2,4,32,128]{4,3,2,1,0:T(8,128)(2,1)} %broadcast_select_fusion), calls=%async_computation | async-start | bytes 16777216 | tf_op jit(solution)/shard_map/all_to_all | solution.py:69
  46.1 186.5 %reduce-scatter.2.cloned.1.call-start = ((), (), s32[]{:S(2)}) async-start(), calls=%async_computation.2 | async-start | bytes 5898240 | tf_op jit(solution)/shard_map/reduce_scatter | solution.py:86
  187.8 135.5 %all-gather.2.cloned.1.call-start = ((), (), s32[]{:S(2)}) async-start(), calls=%async_computation.3 | async-start | bytes 11141120 | tf_op jit(solution)/shard_map/all_gather | solution.py:92
  232.5 173.4 %all-reduce.2.cloned.1.call-start = ((), (), s32[]{:S(2)}) async-start(), calls=%async_computation.4 | async-start | bytes 10485760 | tf_op jit(solution)/shard_map/psum | solution.py:11
Sparse Core Ops, SparseCore 0:
  188.0 44.5 reduce-scatter.1
  234.6 88.6 all-gather.1
  330.1 75.7 all-reduce.1
where the time goes:
time: 435 us; the launch traced here: 433 us
  waiting for transfers between devices  306 us (70%)
  matrix products  44.2 us (10%)
  local copies, waits for them, and re-layouts  33.8 us (8%)
  other arithmetic  23.8 us (5%)
  between operations  13.3 us (3%)
  starting transfers between devices  12.2 us (3%)
    all_to_all x1, waiting for transfers between devices, shards(): lax.all_to_all(outgoing.reshape((devices, capacity) + outgoing.shape[1:])...  95 us
    all_gather x1, waiting for transfers between devices, shards(): columns = lax.all_gather(local_rows, 'aux', axis=1, tiled=True)  90.5 us
    psum x1, waiting for transfers between devices, from_root(): return lax.psum(jnp.where(mine, shard, jnp.zeros_like(shard)), axis)  75.9 us
    reduce_scatter x1, waiting for transfers between devices, shards(): lax.psum_scatter(summed.reshape(NBAS // bas_count * lax.axis_size('bas'),...  44.6 us
    dot_general x1, matrix products, shards(): lax.dot_general(row_data, columns, (((1,), (1,)), ((), ())), preferred_el...  20.9 us
    dot_general x1, matrix products, half_transform(): jnp.einsum('kpmn,kin->kmpi', tile_block, chosen, preferred_element_type=j...  19.4 us
    all_to_all x1, starting transfers between devices, shards(): lax.all_to_all(outgoing.reshape((devices, capacity) + outgoing.shape[1:])...  11.7 us
    convert_element_type x1, local copies, waits for them, and re-layouts, half_transform(): product.reshape(leading + (tile_rows, aux_count * orbital_count))  11.1 us
  transfers between devices with their start and end apart: 4, of which 4 were waited for; matrix products, arithmetic and copies ran while one was open for 1% of the time, Pallas kernels for 0%

commit v1 on v0

v1 whole, which is shorter than its diff:
```python
import jax
import jax.numpy as jnp
from jax import lax
from jax.experimental import pallas as pl
from jax.experimental.pallas import tpu as pltpu
from jax.sharding import Mesh, PartitionSpec as P

NBAS = 20480
AUX_AXES = ("z", "y")
BAS_AXES = ("x", "core")
ALL_AXES = AUX_AXES + BAS_AXES
TILE_STEP = 32
COL_STEP = 256
SWAP = [(0, 1), (1, 0)]
VMEM_LIMIT = 56 * 1024 * 1024


def half_kernel(self_ref, owner_ref, col_ref, tiles_ref, orbital_ref, support_ref, out_ref, count_ref, kept_ref):
    step = pl.program_id(0)
    aux_here, tile_rows, tile_cols = tiles_ref.shape[1:]
    orbital_count = orbital_ref.shape[0]
    width = aux_here * orbital_count
    block_count = count_ref.shape[0]
    per_block = out_ref.shape[0] // block_count

    @pl.when(step == 0)
    def _():
        for block in range(block_count):
            count_ref[block] = 0
        orbital = lax.broadcasted_iota(jnp.int32, (orbital_count, width), 0)
        column = lax.broadcasted_iota(jnp.int32, (orbital_count, width), 1)
        spread = (lax.rem(column, orbital_count) == orbital).astype(jnp.float32)
        kept_ref[...] = lax.dot_general(
            (support_ref[...] == 1).astype(jnp.float32),
            spread,
            (((0,), (0,)), ((), ())),
            preferred_element_type=jnp.float32,
        )

    row = lax.bitwise_and(self_ref[0], 7)
    lane = lax.broadcasted_iota(jnp.int32, (tile_rows, width), 1)
    for index in range(tiles_ref.shape[0]):
        tile = step * tiles_ref.shape[0] + index
        block = lax.shift_right_logical(owner_ref[row, tile], 3)
        rank = count_ref[block]
        count_ref[block] = rank + 1
        col = col_ref[row, tile]
        chosen = orbital_ref[:, pl.ds(pl.multiple_of(col * tile_cols, tile_cols), tile_cols)]
        product = lax.dot_general(
            tiles_ref[index].reshape(aux_here * tile_rows, tile_cols),
            jnp.concatenate([chosen] * aux_here, axis=0),
            (((1,), (1,)), ((), ())),
            preferred_element_type=jnp.float32,
        )
        half = product[:tile_rows]
        for aux in range(1, aux_here):
            part = product[aux * tile_rows : (aux + 1) * tile_rows]
            half = jnp.where(lane >= aux * orbital_count, part, half)
        kept = kept_ref[pl.ds(col, 1), :] > 0.5
        out_ref[block * per_block + rank] = jnp.where(kept, half, 0.0).astype(out_ref.dtype)


def half_slots(myself, tiles, owners, cols, orbitals, support, block_count, per_block):
    count, aux_here, tile_rows, tile_cols = tiles.shape
    width = aux_here * orbitals.shape[0]
    index_spec = pl.BlockSpec((8, count), lambda i, self_ref: (self_ref[0] // 8, 0), memory_space=pltpu.SMEM)
    return pl.pallas_call(
        half_kernel,
        grid_spec=pltpu.PrefetchScalarGridSpec(
            num_scalar_prefetch=1,
            grid=(count // TILE_STEP,),
            in_specs=[
                index_spec,
                index_spec,
                pl.BlockSpec((TILE_STEP, aux_here, tile_rows, tile_cols), lambda i, _: (i, 0, 0, 0)),
                pl.BlockSpec(orbitals.shape, lambda i, _: (0, 0)),
                pl.BlockSpec(support.shape, lambda i, _: (0, 0)),
            ],
            out_specs=pl.BlockSpec((block_count * per_block, tile_rows, width), lambda i, _: (0, 0, 0)),
            scratch_shapes=[
                pltpu.SMEM((block_count,), jnp.int32),
                pltpu.VMEM((support.shape[1], width), jnp.float32),
            ],
        ),
        out_shape=jax.ShapeDtypeStruct((block_count * per_block, tile_rows, width), jnp.bfloat16),
        compiler_params=pltpu.CompilerParams(vmem_limit_bytes=VMEM_LIMIT),
        name="half_transform",
    )(myself, owners, cols, tiles, orbitals, support)


def sum_kernel(count_ref, list_ref, own_ref, other_ref, *refs):
    out_refs, total_ref = refs[:-1], refs[-1]
    total_ref[...] = jnp.zeros_like(total_ref)
    for side, slots_ref in enumerate((own_ref, other_ref)):

        def add(index, carry, side=side, slots_ref=slots_ref):
            entry = list_ref[side, index]
            slot = lax.shift_right_logical(entry, 9)
            place = lax.bitwise_and(entry, 511)
            total_ref[place] += slots_ref[slot].astype(jnp.float32)
            return carry

        lax.fori_loop(0, count_ref[side], add, 0)
    first = 0
    for out_ref in out_refs:
        blocks = out_ref.shape[0]
        out_ref[...] = total_ref[pl.ds(first, blocks)].astype(out_ref.dtype)
        first += blocks


def sum_slots(counts, entries, own, other, part):
    tile_shape = own.shape[1:]
    sizes = [part] + [part // 2] * 6
    places = 4 * part
    outs = pl.pallas_call(
        sum_kernel,
        in_specs=[
            pl.BlockSpec(memory_space=pltpu.SMEM),
            pl.BlockSpec(memory_space=pltpu.SMEM),
            pl.BlockSpec(memory_space=pltpu.VMEM),
            pl.BlockSpec(memory_space=pltpu.VMEM),
        ],
        out_specs=[pl.BlockSpec(memory_space=pltpu.VMEM)] * len(sizes),
        out_shape=[jax.ShapeDtypeStruct((size,) + tile_shape, jnp.bfloat16) for size in sizes],
        scratch_shapes=[pltpu.VMEM((places,) + tile_shape, jnp.float32)],
        compiler_params=pltpu.CompilerParams(vmem_limit_bytes=VMEM_LIMIT),
        name="sum_slots",
    )(counts, entries, own, other)
    return outs


def slot_entries(owners, rows, block, x_place, core, slots_per_source, rows_per_part):
    sides, sources, tiles_here = owners.shape
    hit = lax.shift_right_logical(owners, 3) == block
    mine = jnp.logical_and(hit, (rows // rows_per_part) % 2 == core)
    before = jnp.triu(jnp.ones((tiles_here, tiles_here), jnp.bfloat16), 1)
    flags = jnp.stack([hit, mine]).astype(jnp.bfloat16)
    ahead = jnp.einsum("fkst,tu->fksu", flags, before, preferred_element_type=jnp.float32).astype(jnp.int32)
    slot = jnp.arange(sources, dtype=jnp.int32)[None, :, None] * slots_per_source + ahead[0]
    part = (rows // (2 * rows_per_part) - x_place) & 3
    place = part * rows_per_part + rows % rows_per_part
    mine_counts = jnp.sum(mine.astype(jnp.int32), axis=2)
    earlier = jnp.cumsum(mine_counts, axis=1) - mine_counts
    position = jnp.where(mine, ahead[1] + earlier[:, :, None], -1).reshape(sides, 1, sources * tiles_here)
    packed = (slot * 512 + place).reshape(sides, 1, sources * tiles_here)
    wanted = jnp.arange(sources * slots_per_source, dtype=jnp.int32)[None, :, None]
    entries = jnp.sum(jnp.where(position == wanted, packed, 0), axis=2)
    return jnp.sum(mine_counts, axis=1), entries


def shift(value, axis, by):
    return lax.ppermute(value, axis, [(i, (i + by) % 4) for i in range(4)])


def reduce_over_x(own, p1a, p1b, p2a, p2b, p3a, p3b):
    def add(*values):
        total = sum(value.astype(jnp.float32) for value in values).astype(jnp.bfloat16)
        return total.reshape(-1, total.shape[-1])

    far_a, far_b = shift(p2a, "x", 1), shift(p2b, "x", -1)
    low_b, high_a = shift(p1b, "x", 1), shift(p3a, "x", -1)
    low_a = shift(add(p1a, far_a).reshape(p1a.shape), "x", 1)
    high_b = shift(add(p3b, far_b).reshape(p3b.shape), "x", -1)
    low, high = jnp.concatenate([low_a, low_b]), jnp.concatenate([high_a, high_b])
    return add(own, low, high)


def device(z, y, x, core):
    return ((z * 4 + y) * 4 + x) * 2 + core


def shift_turned(value, second, by):
    pairs = []
    for z in range(4):
        for y in range(4):
            for x in range(4):
                for core in range(2):
                    along_z = (core == 0) != second
                    to_z, to_y = ((z + by) % 4, y) if along_z else (z, (y + by) % 4)
                    pairs.append((device(z, y, x, core), device(to_z, to_y, x, core)))
    return lax.ppermute(value, ALL_AXES, pairs)


def spread_pairs(turn):
    along_x, along_zy = [], []
    for zg in range(4):
        for yg in range(4):
            for z in range(4):
                for high in range(2):
                    y = 2 * high + (yg // 2 ^ turn)
                    x = (zg + y + z) % 4
                    along_x.append((device(zg, yg, z, high), device(zg, yg, x, high)))
                    along_zy.append((device(zg, yg, x, high), device(z, y, x, yg % 2)))
    return along_x, along_zy


def gather_both(local):
    stage = lax.optimization_barrier
    middle = local.shape[0] // 2
    turned = lax.axis_index("y") // 2 == 1
    halves = local[:middle], local[middle:]
    pairs = [spread_pairs(turn) for turn in range(2)]

    low, high = shift_turned(local, False, 1), shift_turned(local, False, -1)
    rows = [lax.ppermute(jnp.where(turned, halves[1 - t], halves[t]), ALL_AXES, pairs[t][0]) for t in range(2)]
    low, high, rows = stage((low, high, rows))

    far_a, far_b = shift_turned(high[:middle], False, -1), shift_turned(low[middle:], False, 1)
    rows = [lax.ppermute(rows[t], ALL_AXES, pairs[t][1]) for t in range(2)]
    near = jnp.stack([local, low])
    far = jnp.stack([high, jnp.concatenate([far_a, far_b])])
    rows = jnp.stack(rows)
    near, far, rows = stage((near, far, rows))

    near_low, near_high = shift_turned(near, True, 1), shift_turned(near, True, -1)
    rows_low, rows_high = shift(rows, "x", 1), shift(rows, "x", -1)
    far, near_low, near_high, rows_low, rows_high = stage((far, near_low, near_high, rows_low, rows_high))

    far_low, far_high = shift_turned(far, True, 1), shift_turned(far, True, -1)
    rows_far = jnp.stack([shift(rows_high[0], "x", -1), shift(rows_low[1], "x", 1)])
    near_high, far_low, far_high, rows_far = stage((near_high, far_low, far_high, rows_far))

    near_far, far_far = shift_turned(near_high, True, -1), shift_turned(far_low, True, 1)
    rows_near, rows_far = jnp.stack([rows, rows_low]), jnp.stack([rows_high, rows_far])
    rows = [rows_near, rows_far, lax.ppermute(rows_near, "core", SWAP), lax.ppermute(rows_far, "core", SWAP)]
    return [near, far, near_low, far_low, near_high, far_high, near_far, far_far], rows


def exchange_kernel(at_ref, *refs, factor):
    row_refs, col_refs, (out_ref, row_data) = refs[:4], refs[4:-2], refs[-2:]
    width = row_refs[0].shape[-1]

    @pl.when(pl.program_id(0) == 0)
    def _():
        z_place, y_place, x_place, core = (at_ref[i] for i in range(4))

        def order(offset):
            odd = lax.bitwise_and(offset, 1)
            half = lax.shift_right_logical(offset, 1)
            return jnp.where(odd == 1, 2 - half, offset + half)

        for core_from, pair in ((core, row_refs[:2]), (1 - core, row_refs[2:])):
            for index, offset in enumerate((0, -1, 1, 2)):
                for turn in range(2):
                    zg = lax.bitwise_and(x_place + offset - y_place - z_place, 3)
                    yg = 2 * lax.bitwise_xor(lax.bitwise_and(y_place, 1), turn) + core_from
                    z_at = order(lax.bitwise_and(zg - z_place, 3))
                    y_at = order(lax.bitwise_and(yg - y_place, 3))
                    place = jnp.where(core == 0, 4 * y_at + z_at, 4 * z_at + y_at)
                    columns = pl.ds(pl.multiple_of(place * width, width), width)
                    row_data[:, columns] = pair[index // 2][index % 2, turn]

    columns = jnp.concatenate([col_ref[i] for col_ref in col_refs for i in range(2)], axis=1)
    out_ref[...] = (
        lax.dot_general(
            row_data[...], columns, (((1,), (1,)), ((), ())), preferred_element_type=jnp.float32
        )
        * factor
    )


def exchange_block(at, row_parts, pieces):
    offsets, turns, rows, width = row_parts[0].shape
    col_count = pieces[0].shape[1]
    depth = 2 * len(pieces) * width
    return pl.pallas_call(
        lambda *refs: exchange_kernel(*refs, factor=1.0 / depth),
        grid=(col_count // COL_STEP,),
        in_specs=[pl.BlockSpec(memory_space=pltpu.SMEM)]
        + [pl.BlockSpec(row_parts[0].shape, lambda j: (0, 0, 0, 0))] * len(row_parts)
        + [pl.BlockSpec((2, COL_STEP, width), lambda j: (0, j, 0))] * len(pieces),
        out_specs=pl.BlockSpec((rows, COL_STEP), lambda j: (0, j)),
        out_shape=jax.ShapeDtypeStruct((rows, col_count), jnp.float32),
        scratch_shapes=[pltpu.VMEM((rows, depth), jnp.bfloat16)],
        compiler_params=pltpu.CompilerParams(vmem_limit_bytes=VMEM_LIMIT),
        name="exchange",
    )(at, *row_parts, *pieces)


def shards(tiles, tile_owner, pair_rows, pair_cols, orbitals, support):
    tiles_here, _, tile_rows, _ = tiles.shape
    aux_count = lax.axis_size(AUX_AXES)
    bas_count = lax.axis_size(BAS_AXES)
    x_count = lax.axis_size("x")
    block = lax.axis_index(AUX_AXES)
    at = [lax.axis_index(axis) for axis in ALL_AXES]
    x_place, core = at[2:]
    myself = block * bas_count + lax.axis_index(BAS_AXES)
    slots_per_source = 2 * bas_count
    rows_per_part = NBAS // tile_rows // bas_count

    owner_flat = tile_owner[:, 0]
    by_device = (aux_count * bas_count, tiles_here)
    outgoing = half_slots(
        myself[None].astype(jnp.int32),
        tiles,
        owner_flat.reshape(by_device),
        pair_cols.reshape(by_device),
        orbitals,
        support,
        aux_count,
        slots_per_source,
    )
    own = lax.all_to_all(outgoing, AUX_AXES, split_axis=0, concat_axis=0, tiled=True)

    def sources(flat):
        near = lax.dynamic_index_in_dim(flat.reshape(aux_count, x_count, 2, tiles_here), x_place, 1, keepdims=False)
        return jnp.where(core == 0, near, near[:, ::-1]).transpose(1, 0, 2)

    counts, entries = slot_entries(
        sources(owner_flat), sources(pair_rows), block, x_place, core, slots_per_source, rows_per_part
    )
    other = lax.ppermute(own, "core", SWAP)
    local = reduce_over_x(*sum_slots(counts, entries, own, other, rows_per_part))
    pieces, row_parts = gather_both(local)
    return exchange_block(jnp.stack(at).astype(jnp.int32), row_parts, pieces)


def solution(mesh):
    fine = Mesh(mesh.devices.reshape(4, 4, 4, 2), ALL_AXES)
    in_specs = (P(ALL_AXES, None, None, None), P(), P(), P(), P(), P())
    out_specs = P(AUX_AXES, BAS_AXES)
    return jax.shard_map(shards, mesh=fine, in_specs=in_specs, out_specs=out_specs, check_vma=False)
```

time: 435 us -> 201 us (0.46)
  waiting for transfers between devices: 306 us -> 72.1 us
  matrix products: 44.2 us -> 0.13 us
  blocking collectives: 0 us -> 36.5 us
  starting transfers between devices: 12.2 us -> 48.3 us
  Pallas kernels: 0 us -> 34.9 us
  local copies, waits for them, and re-layouts: 33.8 us -> 2.81 us
  other arithmetic: 23.8 us -> 5.77 us
  between operations: 13.3 us -> 0.31 us
    all_to_all x1 -> x0, waiting for transfers between devices: 95 us -> none  [shards(): lax.all_to_all(outgoing.reshape((devices, capacity) + outgoing.shape[1:])...]
    all_gather x1 -> x0, waiting for transfers between devices: 90.5 us -> none  [shards(): columns = lax.all_gather(local_rows, 'aux', axis=1, tiled=True)]
    psum x1 -> x0, waiting for transfers between devices: 75.9 us -> none  [from_root(): return lax.psum(jnp.where(mine, shard, jnp.zeros_like(shard)), axis)]
    ppermute x0 -> x27, waiting for transfers between devices: none -> 72.1 us  [the longest x10 33.5 us: shift(): return lax.ppermute(value, axis, [(i, (i + by) % 4) for i in range(4)])]
    ppermute x0 -> x27, starting transfers between devices: none -> 48.3 us  [the longest x10 20.6 us: shift(): return lax.ppermute(value, axis, [(i, (i + by) % 4) for i in range(4)])]
    reduce_scatter x1 -> x0, waiting for transfers between devices: 44.6 us -> none  [shards(): lax.psum_scatter(summed.reshape(NBAS // bas_count * lax.axis_size('bas'),...]
    dot_general x3 -> x1, matrix products: 44.2 us -> 0.13 us  [slot_entries(): jnp.einsum('fkst,tu->fksu', flags, before, preferred_element_type=jnp.flo...]
    all_to_all x0 -> x1, blocking collectives: none -> 36.5 us  [shards(): lax.all_to_all(outgoing, AUX_AXES, split_axis=0, concat_axis=0, tiled=True)]
  transfers between devices with their start and end apart: 4 -> 27, of which waited for: 4 -> 15; matrix products, arithmetic and copies ran while one was open for 1% -> 3% of each run, Pallas kernels for 0% -> 0%
where the time goes in v1:
time: 201 us
  waiting for transfers between devices  72.1 us (36%)
  starting transfers between devices  48.3 us (24%)
  blocking collectives  36.5 us (18%)
  Pallas kernels  34.9 us (17%)
  other arithmetic  5.77 us (3%)
  local copies, waits for them, and re-layouts  2.81 us (1%)
    all_to_all x1, blocking collectives, shards(): lax.all_to_all(outgoing, AUX_AXES, split_axis=0, concat_axis=0, tiled=True)  36.5 us
    ppermute x10, waiting for transfers between devices, shift(): return lax.ppermute(value, axis, [(i, (i + by) % 4) for i in range(4)])  33.5 us
    ppermute x10, waiting for transfers between devices, shift_turned(): return lax.ppermute(value, ALL_AXES, pairs)  24.2 us
    pallas_call x1, Pallas kernels, exchange_block(): pl.pallas_call(lambda *refs: exchange_kernel(*refs, factor=1.0 / depth),...  22.1 us
    ppermute x10, starting transfers between devices, shift(): return lax.ppermute(value, axis, [(i, (i + by) % 4) for i in range(4)])  20.6 us
    ppermute x10, starting transfers between devices, shift_turned(): return lax.ppermute(value, ALL_AXES, pairs)  18.4 us
    ppermute x2, waiting for transfers between devices, gather_both(): lax.ppermute(jnp.where(turned, halves[1 - t], halves[t]), ALL_AXES, pairs...  7.58 us
    pallas_call x1, Pallas kernels, half_slots(): pl.pallas_call(half_kernel, grid_spec=pltpu.PrefetchScalarGridSpec(num_sc...  7.2 us
  transfers between devices with their start and end apart: 27, of which 15 were waited for; matrix products, arithmetic and copies ran while one was open for 3% of the time, Pallas kernels for 0%

profile of v1, /device:TPU:0, one launch (start us, length us, event | category | flops | bytes accessed | tf_op | source)
XLA Modules:
  0.0 200.8 jit_solution(7406109829735475574)
XLA Ops:
  0.0 7.2 %half_transform.1 = bf16[256,32,128]{2,1,0:T(8,128)(2,1)} custom-call(s32[1]{0:T(128)} %bitcast.20.self_ref, s32[128,128]{1,0:T(8,128)} %bitcast.123, s32[128,128]{1,0:T(8,128)} %bitcast.125, bf16[128,4,32,128]{3,2,1,0:T(8,128)(2,1)} %tiles_ref.1, bf16[32,20480]{1,0:T(8,128)(2,1)} %orbital_ref.1, s32[32,160]{1,0:T(8,128)} %support_ref.1), custom_call_target="tpu_custom_call" | custom-call | tf_op jit(solution)/shard_map/half_transform/pallas_call | solution.py:67
  7.2 36.5 %all_to_all.5.own_ref = bf16[256,32,128]{2,1,0:T(8,128)(2,1)S(1)} all-to-all(bf16[256,32,128]{2,1,0:T(8,128)(2,1)} %half_transform.1), channel_id=1, replica_groups=mesh['z'=4,'y'=4,'x'=4,'core'=2] {'z','y'}, dimensions={0} | all-to-all | bytes 4194304 | tf_op jit(solution)/shard_map/all_to_all | solution.py:304
  43.7 0.0 collective-permute-start
  43.8 0.8 constant_dynamic-slice_fusion.1
  44.5 0.7 convert_reduce_fusion
  45.2 0.2 reduce_window_sum.11
  45.4 0.1 convolution_convert_fusion
  45.6 0.1 fusion.20
  45.7 1.1 select_reduce_fusion.list_ref
  46.8 1.2 collective-permute-done.other_ref
  48.0 5.5 %sum_slots.1 = (bf16[80,32,128]{2,1,0:T(8,128)(2,1)}, bf16[40,32,128]{2,1,0:T(8,128)(2,1)}, bf16[40,32,128]{2,1,0:T(8,128)(2,1)}, bf16[40,32,128]{2,1,0:T(8,128)...) custom-call(s32[2]{0:T(128)} %get-tuple-element.52.count_ref, ...), custom_call_target="tpu_custom_call" | custom-call | tf_op jit(solution)/shard_map/sum_slots/pallas_call | solution.py:115
  53.6 1.3 collective-permute-start.1
  54.8 2.0 collective-permute-start.5
  56.8 0.1 collective-permute-start.3
  56.8 3.2 %collective-permute-start.4 = (bf16[40,32,128]{2,1,0:T(8,128)(2,1)}, bf16[40,32,128]{2,1,0:T(8,128)(2,1)S(1)}, u32[]{:S(2)}, u32[]{:S(2)}) collective-permute-start(bf16[40,32,128]{2,1,0:T(8,128)(2,1)} %get-tuple-element.32), channel_id=1, source_target_pairs={{0,6},{2,0},{4,2},{6,4},{1,7},{3,1},{5,3},{7,5},{8,14},{10,8},{12,... | collective-permute-start | bytes 983048 | tf_op jit(solution)/shard_map/ppermute | solution.py:152
  60.0 5.5 %collective-permute-done.1 = bf16[40,32,128]{2,1,0:T(8,128)(2,1)S(1)} collective-permute-done((bf16[40,32,128]{2,1,0:T(8,128)(2,1)}, bf16[40,32,128]{2,1,0:T(8,128)(2,1)S(1)}, u32[]{:S(2)}, u32[]{:S(2)}) %collective-permute-start.1) | collective-permute-done | bytes 327712 | tf_op jit(solution)/shard_map/ppermute | solution.py:152
  65.6 1.1 add_convert_fusion.2
  66.6 0.1 collective-permute-start.2
  66.7 0.0 collective-permute-done.5
  66.7 1.1 add_convert_fusion.1
  67.8 3.3 %collective-permute-start.6 = (bf16[40,32,128]{2,1,0:T(8,128)(2,1)S(1)}, bf16[40,32,128]{2,1,0:T(8,128)(2,1)S(1)}, u32[]{:S(2)}, u32[]{:S(2)}) collective-permute-start(bf16[40,32,128]{2,1,0:T(8,128)(2,1)S(1)} %add_convert_fusion.1), channel_id=1, source_target_pairs={{0,6},{2,0},{4,2},{6,4},{1,7},{3,1},{5,3},{7,5},{8,14},{10,8},{12,... | collective-permute-start | bytes 983048 | tf_op jit(solution)/shard_map/ppermute | solution.py:152
  71.1 1.5 collective-permute-done.3
  72.6 0.0 collective-permute-done.4
  72.6 6.0 %collective-permute-done.2 = bf16[40,32,128]{2,1,0:T(8,128)(2,1)S(1)} collective-permute-done((bf16[40,32,128]{2,1,0:T(8,128)(2,1)S(1)}, bf16[40,32,128]{2,1,0:T(8,128)(2,1)S(1)}, u32[]{:S(2)}, u32[]{:S(2)}) %collective-permute-start.2) | collective-permute-done | bytes 327712 | tf_op jit(solution)/shard_map/ppermute | solution.py:152
  78.6 0.1 collective-permute-done.6
  78.8 0.3 add_convert_fusion
  79.0 0.9 collective-permute-start.8
  79.9 1.2 collective-permute-start.7
  81.2 0.7 collective-permute-start.9
  81.8 3.4 %collective-permute-start.10 = (bf16[1280,128]{1,0:T(8,128)(2,1)S(1)}, bf16[1280,128]{1,0:T(8,128)(2,1)S(1)}, u32[]{:S(2)}, u32[]{:S(2)}) collective-permute-start(bf16[1280,128]{1,0:T(8,128)(2,1)S(1)} %bitcast.121), channel_id=1, source_target_pairs={{0,2},{1,7},{2,4},{3,1},{4,6},{5,3},{6,0},{7,5},{8,10},{9,15},{10,... | collective-permute-start | bytes 983048 | tf_op jit(solution)/shard_map/ppermute | solution.py:205
  85.3 7.6 %collective-permute-done.10 = bf16[1280,128]{1,0:T(8,128)(2,1)S(1)} collective-permute-done((bf16[1280,128]{1,0:T(8,128)(2,1)S(1)}, bf16[1280,128]{1,0:T(8,128)(2,1)S(1)}, u32[]{:S(2)}, u32[]{:S(2)}) %collective-permute-start.10) | collective-permute-done | bytes 327712 | tf_op jit(solution)/shard_map/ppermute | solution.py:205
  92.9 2.8 %collective-permute-start.11 = (bf16[1280,128]{1,0:T(8,128)(2,1)S(1)}, bf16[1280,128]{1,0:T(8,128)(2,1)S(1)}, u32[]{:S(2)}, u32[]{:S(2)}) collective-permute-start(bf16[1280,128]{1,0:T(8,128)(2,1)S(1)} %slice.30), channel_id=1, source_target_pairs={{0,96},{1,25},{2,98},{3,27},{4,100},{5,29},{6,102},{7,31},{8,104},... | collective-permute-start | bytes 983048 | tf_op jit(solution)/shard_map/ppermute | solution.py:181
  95.7 0.5 collective-permute-start.12
  96.2 0.7 collective-permute-start.13
  96.9 4.2 %collective-permute-start.14 = (bf16[1280,128]{1,0:T(8,128)(2,1)S(1)}, bf16[1280,128]{1,0:T(8,128)(2,1)S(1)}, u32[]{:S(2)}, u32[]{:S(2)}) collective-permute-start(bf16[1280,128]{1,0:T(8,128)(2,1)S(1)} %collective-permute-done.10), channel_id=1, source_target_pairs={{2,10},{7,30},{4,44},{1,56},{6,78},{3,90},{0,104},{5,124},{10,11},... | collective-permute-start | bytes 983048 | tf_op jit(solution)/shard_map/ppermute | solution.py:209
  101.1 0.1 pad_maximum_fusion.refs_5_
  101.2 2.7 %collective-permute-done.12 = bf16[1280,128]{1,0:T(8,128)(2,1)S(1)} collective-permute-done((bf16[1280,128]{1,0:T(8,128)(2,1)S(1)}, bf16[1280,128]{1,0:T(8,128)(2,1)S(1)}, u32[]{:S(2)}, u32[]{:S(2)}) %collective-permute-start.12) | collective-permute-done | bytes 327712 | tf_op jit(solution)/shard_map/ppermute | solution.py:181
  104.0 0.1 pad_maximum_fusion.1.refs_6_
  104.1 5.6 %collective-permute-done.14 = bf16[1280,128]{1,0:T(8,128)(2,1)S(1)} collective-permute-done((bf16[1280,128]{1,0:T(8,128)(2,1)S(1)}, bf16[1280,128]{1,0:T(8,128)(2,1)S(1)}, u32[]{:S(2)}, u32[]{:S(2)}) %collective-permute-start.14) | collective-permute-done | bytes 327712 | tf_op jit(solution)/shard_map/ppermute | solution.py:209
  109.7 0.1 pad_maximum_fusion.4
  109.8 3.6 %collective-permute-start.16 = (bf16[2,2560,128]{2,1,0:T(8,128)(2,1)S(1)}, bf16[2,2560,128]{2,1,0:T(8,128)(2,1)S(1)}, u32[]{:S(2)}, u32[]{:S(2)}) collective-permute-start(bf16[2,2560,128]{2,1,0:T(8,128)(2,1)S(1)} %pad_maximum_fusion.refs_5_), channel_id=1, source_target_pairs={{0,24},{1,97},{2,26},{3,99},{4,28},{5,101},{6,30},{7,103},{8,0},{9... | collective-permute-start | bytes 3932168 | tf_op jit(solution)/shard_map/ppermute | solution.py:181
  113.4 2.2 %collective-permute-start.15 = (bf16[2,2560,128]{2,1,0:T(8,128)(2,1)S(1)}, bf16[2,2560,128]{2,1,0:T(8,128)(2,1)S(1)}, u32[]{:S(2)}, u32[]{:S(2)}) collective-permute-start(bf16[2,2560,128]{2,1,0:T(8,128)(2,1)S(1)} %pad_maximum_fusion.refs_5_), channel_id=1, source_target_pairs={{0,8},{1,33},{2,10},{3,35},{4,12},{5,37},{6,14},{7,39},{8,16},{9,4... | collective-permute-start | bytes 3932168 | tf_op jit(solution)/shard_map/ppermute | solution.py:181
  115.7 8.1 %collective-permute-start.18 = (bf16[2,1280,128]{2,1,0:T(8,128)(2,1)S(1)}, bf16[2,1280,128]{2,1,0:T(8,128)(2,1)S(1)}, u32[]{:S(2)}, u32[]{:S(2)}) collective-permute-start(bf16[2,1280,128]{2,1,0:T(8,128)(2,1)S(1)} %pad_maximum_fusion.4), channel_id=1, source_target_pairs={{0,6},{2,0},{4,2},{6,4},{1,7},{3,1},{5,3},{7,5},{8,14},{10,8},{12,... | collective-permute-start | bytes 1966088 | tf_op jit(solution)/shard_map/ppermute | solution.py:152
  123.8 9.1 %collective-permute-done.18 = bf16[2,1280,128]{2,1,0:T(8,128)(2,1)S(1)} collective-permute-done((bf16[2,1280,128]{2,1,0:T(8,128)(2,1)S(1)}, bf16[2,1280,128]{2,1,0:T(8,128)(2,1)S(1)}, u32[]{:S(2)}, u32[]{:S(2)}) %collective-permute-start.18) | collective-permute-done | bytes 655392 | tf_op jit(solution)/shard_map/ppermute | solution.py:152
  132.9 3.3 %collective-permute-done.17 = bf16[2,1280,128]{2,1,0:T(8,128)(2,1)S(1)} collective-permute-done((bf16[2,1280,128]{2,1,0:T(8,128)(2,1)S(1)}, bf16[2,1280,128]{2,1,0:T(8,128)(2,1)S(1)}, u32[]{:S(2)}, u32[]{:S(2)}) %collective-permute-start.17) | collective-permute-done | bytes 655392 | tf_op jit(solution)/shard_map/ppermute | solution.py:152
  136.2 2.7 %collective-permute-start.20 = (bf16[2,2560,128]{2,1,0:T(8,128)(2,1)S(1)}, bf16[2,2560,128]{2,1,0:T(8,128)(2,1)S(1)}, u32[]{:S(2)}, u32[]{:S(2)}) collective-permute-start(bf16[2,2560,128]{2,1,0:T(8,128)(2,1)S(1)} %pad_maximum_fusion.1.refs_6_), channel_id=1, source_target_pairs={{0,24},{1,97},{2,26},{3,99},{4,28},{5,101},{6,30},{7,103},{8,0},{9... | collective-permute-start | bytes 3932168 | tf_op jit(solution)/shard_map/ppermute | solution.py:181
  138.9 1.3 collective-permute-start.19
  140.2 2.6 %collective-permute-start.21 = (bf16[1280,128]{1,0:T(8,128)(2,1)S(1)}, bf16[1280,128]{1,0:T(8,128)(2,1)S(1)}, u32[]{:S(2)}, u32[]{:S(2)}) collective-permute-start(bf16[1280,128]{1,0:T(8,128)(2,1)S(1)} %slice_bitcast_fusion.1), channel_id=1, source_target_pairs={{0,6},{2,0},{4,2},{6,4},{1,7},{3,1},{5,3},{7,5},{8,14},{10,8},{12,... | collective-permute-start | bytes 983048 | tf_op jit(solution)/shard_map/ppermute | solution.py:152
  142.8 0.1 pad_maximum_fusion.2.refs_1_
  143.0 0.3 collective-permute-start.23
  143.3 4.2 %collective-permute-done.21 = bf16[1280,128]{1,0:T(8,128)(2,1)S(1)} collective-permute-done((bf16[1280,128]{1,0:T(8,128)(2,1)S(1)}, bf16[1280,128]{1,0:T(8,128)(2,1)S(1)}, u32[]{:S(2)}, u32[]{:S(2)}) %collective-permute-start.21) | collective-permute-done | bytes 327712 | tf_op jit(solution)/shard_map/ppermute | solution.py:152
  147.4 3.7 %collective-permute-done.22 = bf16[1280,128]{1,0:T(8,128)(2,1)S(1)} collective-permute-done((bf16[1280,128]{1,0:T(8,128)(2,1)S(1)}, bf16[1280,128]{1,0:T(8,128)(2,1)S(1)}, u32[]{:S(2)}, u32[]{:S(2)}) %collective-permute-start.22) | collective-permute-done | bytes 327712 | tf_op jit(solution)/shard_map/ppermute | solution.py:152
  151.1 0.1 pad_maximum_fusion.5
  151.2 4.5 %collective-permute-done.20.refs_10_ = bf16[2,2560,128]{2,1,0:T(8,128)(2,1)S(1)} collective-permute-done((bf16[2,2560,128]{2,1,0:T(8,128)(2,1)S(1)}, bf16[2,2560,128]{2,1,0:T(8,128)(2,1)S(1)}, u32[]{:S(2)}, u32[]{:S(2)}) %collective-permute-start.20) | collective-permute-done | bytes 1310752 | tf_op jit(solution)/shard_map/ppermute | solution.py:181
  155.7 2.0 collective-permute-done.19.refs_8_
  157.7 0.1 pad_maximum_fusion.3.refs_2_
  157.8 0.1 collective-permute-start.24
  157.9 0.8 copy-done.9
  158.7 0.4 collective-permute-start.26
  159.2 2.8 %collective-permute-start.25 = (bf16[2,2560,128]{2,1,0:T(8,128)(2,1)S(1)}, bf16[2,2560,128]{2,1,0:T(8,128)(2,1)}, u32[]{:S(2)}, u32[]{:S(2)}) collective-permute-start(bf16[2,2560,128]{2,1,0:T(8,128)(2,1)S(1)} %collective-permute-done.16.refs_9_), channel_id=1, source_target_pairs={{0,24},{1,97},{2,26},{3,99},{4,28},{5,101},{6,30},{7,103},{8,0},{9... | collective-permute-start | bytes 3932168 | tf_op jit(solution)/shard_map/ppermute | solution.py:181
  162.0 0.6 pad_add_fusion.refs_0_
  162.6 15.0 %collective-permute-done.26.refs_12_ = bf16[2,2560,128]{2,1,0:T(8,128)(2,1)S(1)} collective-permute-done((bf16[2,2560,128]{2,1,0:T(8,128)(2,1)S(1)}, bf16[2,2560,128]{2,1,0:T(8,128)(2,1)S(1)}, u32[]{:S(2)}, u32[]{:S(2)}) %collective-permute-start.26) | collective-permute-done | bytes 1310752 | tf_op jit(solution)/shard_map/ppermute | solution.py:181
  177.6 1.1 copy-done.12
  178.6 22.1 %exchange.1 = f32[1280,2560]{1,0:T(8,128)} custom-call(s32[4]{0:T(128)} %pad_add_fusion.refs_0_, bf16[2,2,1280,128]{3,2,1,0:T(8,128)(2,1)} %copy-done.4, bf16[2,2,1280,128]{3,2,1,0:T(8,128)(2,1)} %copy-done.5, bf16[2,2,1280,128]{3,2,1,0:T(8,128)(2,1)} %copy-done.10, bf16[2,2,1280,128]{3,2,1,0:T(8,128)(2,1)} %copy-done.11, bf16[2,2560,128]{2,1,0:T(8,128)(2,1)} %copy-done.2, ...), custom_call_target="tpu_custom_call" | custom-call | tf_op jit(solution)/shard_map/exchange/pallas_call | solution.py:266
  (50 shorter events, 0.3 us)
Async XLA Ops:
  0.0 43.7 %copy-start = (s32[16384]{0:T(1024)S(1)}, s32[16384]{0:T(1024)}, u32[]{:S(2)}) copy-start(s32[16384]{0:T(1024)} %param.8) | copy-start | bytes 196612
  43.7 4.3 %copy-start.1 = (bf16[256,32,128]{2,1,0:T(8,128)(2,1)}, bf16[256,32,128]{2,1,0:T(8,128)(2,1)S(1)}, u32[]{:S(2)}) copy-start(bf16[256,32,128]{2,1,0:T(8,128)(2,1)S(1)} %all_to_all.5.own_ref) | copy-start | bytes 6291460
  43.7 4.3 %collective-permute-start = (bf16[256,32,128]{2,1,0:T(8,128)(2,1)S(1)}, bf16[256,32,128]{2,1,0:T(8,128)(2,1)}, u32[]{:S(2)}, u32[]{:S(2)}) collective-permute-start(bf16[256,32,128]{2,1,0:T(8,128)(2,1)S(1)} %all_to_all.5.own_ref), channel_id=1, source_target_pairs={{0,1},{1,0},{2,3},{3,2},{4,5},{5,4},{6,7},{7,6},{8,9},{9,8},{10,11... | collective-permute-start | bytes 6291464 | tf_op jit(solution)/shard_map/ppermute | solution.py:313
  53.6 25.2 %copy-start.13 = (bf16[80,32,128]{2,1,0:T(8,128)(2,1)S(1)}, bf16[80,32,128]{2,1,0:T(8,128)(2,1)}, u32[]{:S(2)}) copy-start(bf16[80,32,128]{2,1,0:T(8,128)(2,1)} %get-tuple-element.28) | copy-start | bytes 1966084
  53.6 12.0 %collective-permute-start.1 = (bf16[40,32,128]{2,1,0:T(8,128)(2,1)}, bf16[40,32,128]{2,1,0:T(8,128)(2,1)S(1)}, u32[]{:S(2)}, u32[]{:S(2)}) collective-permute-start(bf16[40,32,128]{2,1,0:T(8,128)(2,1)} %get-tuple-element.30), channel_id=1, source_target_pairs={{0,2},{2,4},{4,6},{6,0},{1,3},{3,5},{5,7},{7,1},{8,10},{10,12},{12... | collective-permute-start | bytes 983048 | tf_op jit(solution)/shard_map/ppermute | solution.py:152
  54.8 11.9 %collective-permute-start.5 = (bf16[40,32,128]{2,1,0:T(8,128)(2,1)}, bf16[40,32,128]{2,1,0:T(8,128)(2,1)S(1)}, u32[]{:S(2)}, u32[]{:S(2)}) collective-permute-start(bf16[40,32,128]{2,1,0:T(8,128)(2,1)} %get-tuple-element.34), channel_id=1, source_target_pairs={{0,6},{2,0},{4,2},{6,4},{1,7},{3,1},{5,3},{7,5},{8,14},{10,8},{12,... | collective-permute-start | bytes 983048 | tf_op jit(solution)/shard_map/ppermute | solution.py:152
  56.8 15.8 %collective-permute-start.3 = (bf16[40,32,128]{2,1,0:T(8,128)(2,1)}, bf16[40,32,128]{2,1,0:T(8,128)(2,1)S(1)}, u32[]{:S(2)}, u32[]{:S(2)}) collective-permute-start(bf16[40,32,128]{2,1,0:T(8,128)(2,1)} %get-tuple-element.31), channel_id=1, source_target_pairs={{0,2},{2,4},{4,6},{6,0},{1,3},{3,5},{5,7},{7,1},{8,10},{10,12},{12... | collective-permute-start | bytes 983048 | tf_op jit(solution)/shard_map/ppermute | solution.py:152
  56.8 15.8 %collective-permute-start.4 = (bf16[40,32,128]{2,1,0:T(8,128)(2,1)}, bf16[40,32,128]{2,1,0:T(8,128)(2,1)S(1)}, u32[]{:S(2)}, u32[]{:S(2)}) collective-permute-start(bf16[40,32,128]{2,1,0:T(8,128)(2,1)} %get-tuple-element.32), channel_id=1, source_target_pairs={{0,6},{2,0},{4,2},{6,4},{1,7},{3,1},{5,3},{7,5},{8,14},{10,8},{12,... | collective-permute-start | bytes 983048 | tf_op jit(solution)/shard_map/ppermute | solution.py:152
  66.6 12.0 %collective-permute-start.2 = (bf16[40,32,128]{2,1,0:T(8,128)(2,1)S(1)}, bf16[40,32,128]{2,1,0:T(8,128)(2,1)S(1)}, u32[]{:S(2)}, u32[]{:S(2)}) collective-permute-start(bf16[40,32,128]{2,1,0:T(8,128)(2,1)S(1)} %add_convert_fusion.2), channel_id=1, source_target_pairs={{0,2},{2,4},{4,6},{6,0},{1,3},{3,5},{5,7},{7,1},{8,10},{10,12},{12... | collective-permute-start | bytes 983048 | tf_op jit(solution)/shard_map/ppermute | solution.py:152
  67.8 11.0 %collective-permute-start.6 = (bf16[40,32,128]{2,1,0:T(8,128)(2,1)S(1)}, bf16[40,32,128]{2,1,0:T(8,128)(2,1)S(1)}, u32[]{:S(2)}, u32[]{:S(2)}) collective-permute-start(bf16[40,32,128]{2,1,0:T(8,128)(2,1)S(1)} %add_convert_fusion.1), channel_id=1, source_target_pairs={{0,6},{2,0},{4,2},{6,4},{1,7},{3,1},{5,3},{7,5},{8,14},{10,8},{12,... | collective-permute-start | bytes 983048 | tf_op jit(solution)/shard_map/ppermute | solution.py:152
  79.0 13.8 %collective-permute-start.8 = (bf16[2560,128]{1,0:T(8,128)(2,1)S(1)}, bf16[2560,128]{1,0:T(8,128)(2,1)S(1)}, u32[]{:S(2)}, u32[]{:S(2)}) collective-permute-start(bf16[2560,128]{1,0:T(8,128)(2,1)S(1)} %bitcast.108), channel_id=1, source_target_pairs={{0,96},{1,25},{2,98},{3,27},{4,100},{5,29},{6,102},{7,31},{8,104},... | collective-permute-start | bytes 1966088 | tf_op jit(solution)/shard_map/ppermute | solution.py:181
  79.9 13.0 %collective-permute-start.7 = (bf16[2560,128]{1,0:T(8,128)(2,1)S(1)}, bf16[2560,128]{1,0:T(8,128)(2,1)S(1)}, u32[]{:S(2)}, u32[]{:S(2)}) collective-permute-start(bf16[2560,128]{1,0:T(8,128)(2,1)S(1)} %bitcast.109), channel_id=1, source_target_pairs={{0,32},{1,9},{2,34},{3,11},{4,36},{5,13},{6,38},{7,15},{8,40},{9,1... | collective-permute-start | bytes 1966088 | tf_op jit(solution)/shard_map/ppermute | solution.py:181
  81.2 4.1 %collective-permute-start.9 = (bf16[1280,128]{1,0:T(8,128)(2,1)S(1)}, bf16[1280,128]{1,0:T(8,128)(2,1)S(1)}, u32[]{:S(2)}, u32[]{:S(2)}) collective-permute-start(bf16[1280,128]{1,0:T(8,128)(2,1)S(1)} %bitcast.122), channel_id=1, source_target_pairs={{0,0},{1,5},{2,2},{3,7},{4,4},{5,1},{6,6},{7,3},{8,8},{9,13},{10,1... | collective-permute-start | bytes 983048 | tf_op jit(solution)/shard_map/ppermute | solution.py:205
  81.8 11.0 %collective-permute-start.10 = (bf16[1280,128]{1,0:T(8,128)(2,1)S(1)}, bf16[1280,128]{1,0:T(8,128)(2,1)S(1)}, u32[]{:S(2)}, u32[]{:S(2)}) collective-permute-start(bf16[1280,128]{1,0:T(8,128)(2,1)S(1)} %bitcast.121), channel_id=1, source_target_pairs={{0,2},{1,7},{2,4},{3,1},{4,6},{5,3},{6,0},{7,5},{8,10},{9,15},{10,... | collective-permute-start | bytes 983048 | tf_op jit(solution)/shard_map/ppermute | solution.py:205
  92.9 8.3 %collective-permute-start.11 = (bf16[1280,128]{1,0:T(8,128)(2,1)S(1)}, bf16[1280,128]{1,0:T(8,128)(2,1)S(1)}, u32[]{:S(2)}, u32[]{:S(2)}) collective-permute-start(bf16[1280,128]{1,0:T(8,128)(2,1)S(1)} %slice.30), channel_id=1, source_target_pairs={{0,96},{1,25},{2,98},{3,27},{4,100},{5,29},{6,102},{7,31},{8,104},... | collective-permute-start | bytes 983048 | tf_op jit(solution)/shard_map/ppermute | solution.py:181
  95.7 8.3 %collective-permute-start.12 = (bf16[1280,128]{1,0:T(8,128)(2,1)S(1)}, bf16[1280,128]{1,0:T(8,128)(2,1)S(1)}, u32[]{:S(2)}, u32[]{:S(2)}) collective-permute-start(bf16[1280,128]{1,0:T(8,128)(2,1)S(1)} %slice.31), channel_id=1, source_target_pairs={{0,32},{1,9},{2,34},{3,11},{4,36},{5,13},{6,38},{7,15},{8,40},{9,1... | collective-permute-start | bytes 983048 | tf_op jit(solution)/shard_map/ppermute | solution.py:181
  96.2 7.9 %collective-permute-start.13 = (bf16[1280,128]{1,0:T(8,128)(2,1)S(1)}, bf16[1280,128]{1,0:T(8,128)(2,1)S(1)}, u32[]{:S(2)}, u32[]{:S(2)}) collective-permute-start(bf16[1280,128]{1,0:T(8,128)(2,1)S(1)} %collective-permute-done.9), channel_id=1, source_target_pairs={{0,0},{5,20},{2,34},{7,54},{4,68},{1,80},{6,102},{3,114},{8,1},{13... | collective-permute-start | bytes 983048 | tf_op jit(solution)/shard_map/ppermute | solution.py:209
  96.9 12.9 %collective-permute-start.14 = (bf16[1280,128]{1,0:T(8,128)(2,1)S(1)}, bf16[1280,128]{1,0:T(8,128)(2,1)S(1)}, u32[]{:S(2)}, u32[]{:S(2)}) collective-permute-start(bf16[1280,128]{1,0:T(8,128)(2,1)S(1)} %collective-permute-done.10), channel_id=1, source_target_pairs={{2,10},{7,30},{4,44},{1,56},{6,78},{3,90},{0,104},{5,124},{10,11},... | collective-permute-start | bytes 983048 | tf_op jit(solution)/shard_map/ppermute | solution.py:209
  101.2 12.2 %copy-start.2 = (bf16[2,2560,128]{2,1,0:T(8,128)(2,1)}, bf16[2,2560,128]{2,1,0:T(8,128)(2,1)S(1)}, u32[]{:S(2)}) copy-start(bf16[2,2560,128]{2,1,0:T(8,128)(2,1)S(1)} %pad_maximum_fusion.refs_5_) | copy-start | bytes 3932164
  104.1 36.1 %copy-start.3 = (bf16[2,2560,128]{2,1,0:T(8,128)(2,1)}, bf16[2,2560,128]{2,1,0:T(8,128)(2,1)S(1)}, u32[]{:S(2)}) copy-start(bf16[2,2560,128]{2,1,0:T(8,128)(2,1)S(1)} %pad_maximum_fusion.1.refs_6_) | copy-start | bytes 3932164
  109.8 26.4 %collective-permute-start.16 = (bf16[2,2560,128]{2,1,0:T(8,128)(2,1)S(1)}, bf16[2,2560,128]{2,1,0:T(8,128)(2,1)S(1)}, u32[]{:S(2)}, u32[]{:S(2)}) collective-permute-start(bf16[2,2560,128]{2,1,0:T(8,128)(2,1)S(1)} %pad_maximum_fusion.refs_5_), channel_id=1, source_target_pairs={{0,24},{1,97},{2,26},{3,99},{4,28},{5,101},{6,30},{7,103},{8,0},{9... | collective-permute-start | bytes 3932168 | tf_op jit(solution)/shard_map/ppermute | solution.py:181
  113.4 22.8 %collective-permute-start.15 = (bf16[2,2560,128]{2,1,0:T(8,128)(2,1)S(1)}, bf16[2,2560,128]{2,1,0:T(8,128)(2,1)S(1)}, u32[]{:S(2)}, u32[]{:S(2)}) collective-permute-start(bf16[2,2560,128]{2,1,0:T(8,128)(2,1)S(1)} %pad_maximum_fusion.refs_5_), channel_id=1, source_target_pairs={{0,8},{1,33},{2,10},{3,35},{4,12},{5,37},{6,14},{7,39},{8,16},{9,4... | collective-permute-start | bytes 3932168 | tf_op jit(solution)/shard_map/ppermute | solution.py:181
  115.7 17.2 %collective-permute-start.18 = (bf16[2,1280,128]{2,1,0:T(8,128)(2,1)S(1)}, bf16[2,1280,128]{2,1,0:T(8,128)(2,1)S(1)}, u32[]{:S(2)}, u32[]{:S(2)}) collective-permute-start(bf16[2,1280,128]{2,1,0:T(8,128)(2,1)S(1)} %pad_maximum_fusion.4), channel_id=1, source_target_pairs={{0,6},{2,0},{4,2},{6,4},{1,7},{3,1},{5,3},{7,5},{8,14},{10,8},{12,... | collective-permute-start | bytes 1966088 | tf_op jit(solution)/shard_map/ppermute | solution.py:152
  123.8 12.4 %collective-permute-start.17 = (bf16[2,1280,128]{2,1,0:T(8,128)(2,1)S(1)}, bf16[2,1280,128]{2,1,0:T(8,128)(2,1)S(1)}, u32[]{:S(2)}, u32[]{:S(2)}) collective-permute-start(bf16[2,1280,128]{2,1,0:T(8,128)(2,1)S(1)} %pad_maximum_fusion.4), channel_id=1, source_target_pairs={{0,2},{2,4},{4,6},{6,0},{1,3},{3,5},{5,7},{7,1},{8,10},{10,12},{12... | collective-permute-start | bytes 1966088 | tf_op jit(solution)/shard_map/ppermute | solution.py:152
  136.2 23.0 %copy-start.6 = (bf16[2,2560,128]{2,1,0:T(8,128)(2,1)}, bf16[2,2560,128]{2,1,0:T(8,128)(2,1)S(1)}, u32[]{:S(2)}) copy-start(bf16[2,2560,128]{2,1,0:T(8,128)(2,1)S(1)} %collective-permute-done.16.refs_9_) | copy-start | bytes 3932164
  136.2 6.8 %copy-start.7 = (bf16[2,2560,128]{2,1,0:T(8,128)(2,1)}, bf16[2,2560,128]{2,1,0:T(8,128)(2,1)S(1)}, u32[]{:S(2)}) copy-start(bf16[2,2560,128]{2,1,0:T(8,128)(2,1)S(1)} %collective-permute-done.15.refs_7_) | copy-start | bytes 3932164
  136.2 19.5 %collective-permute-start.20 = (bf16[2,2560,128]{2,1,0:T(8,128)(2,1)S(1)}, bf16[2,2560,128]{2,1,0:T(8,128)(2,1)S(1)}, u32[]{:S(2)}, u32[]{:S(2)}) collective-permute-start(bf16[2,2560,128]{2,1,0:T(8,128)(2,1)S(1)} %pad_maximum_fusion.1.refs_6_), channel_id=1, source_target_pairs={{0,24},{1,97},{2,26},{3,99},{4,28},{5,101},{6,30},{7,103},{8,0},{9... | collective-permute-start | bytes 3932168 | tf_op jit(solution)/shard_map/ppermute | solution.py:181
  138.9 18.8 %collective-permute-start.19 = (bf16[2,2560,128]{2,1,0:T(8,128)(2,1)S(1)}, bf16[2,2560,128]{2,1,0:T(8,128)(2,1)S(1)}, u32[]{:S(2)}, u32[]{:S(2)}) collective-permute-start(bf16[2,2560,128]{2,1,0:T(8,128)(2,1)S(1)} %pad_maximum_fusion.1.refs_6_), channel_id=1, source_target_pairs={{0,8},{1,33},{2,10},{3,35},{4,12},{5,37},{6,14},{7,39},{8,16},{9,4... | collective-permute-start | bytes 3932168 | tf_op jit(solution)/shard_map/ppermute | solution.py:181
  140.2 7.2 %collective-permute-start.21 = (bf16[1280,128]{1,0:T(8,128)(2,1)S(1)}, bf16[1280,128]{1,0:T(8,128)(2,1)S(1)}, u32[]{:S(2)}, u32[]{:S(2)}) collective-permute-start(bf16[1280,128]{1,0:T(8,128)(2,1)S(1)} %slice_bitcast_fusion.1), channel_id=1, source_target_pairs={{0,6},{2,0},{4,2},{6,4},{1,7},{3,1},{5,3},{7,5},{8,14},{10,8},{12,... | collective-permute-start | bytes 983048 | tf_op jit(solution)/shard_map/ppermute | solution.py:152
  142.8 8.3 %collective-permute-start.22 = (bf16[1280,128]{1,0:T(8,128)(2,1)S(1)}, bf16[1280,128]{1,0:T(8,128)(2,1)S(1)}, u32[]{:S(2)}, u32[]{:S(2)}) collective-permute-start(bf16[1280,128]{1,0:T(8,128)(2,1)S(1)} %slice_bitcast_fusion), channel_id=1, source_target_pairs={{0,2},{2,4},{4,6},{6,0},{1,3},{3,5},{5,7},{7,1},{8,10},{10,12},{12... | collective-permute-start | bytes 983048 | tf_op jit(solution)/shard_map/ppermute | solution.py:152
  143.0 14.8 %copy-start.4 = (bf16[2,2,1280,128]{3,2,1,0:T(8,128)(2,1)}, bf16[2,2,1280,128]{3,2,1,0:T(8,128)(2,1)S(1)}, u32[]{:S(2)}) copy-start(bf16[2,2,1280,128]{3,2,1,0:T(8,128)(2,1)S(1)} %pad_maximum_fusion.2.refs_1_) | copy-start | bytes 3932164
  143.0 19.6 %collective-permute-start.23 = (bf16[2,2,1280,128]{3,2,1,0:T(8,128)(2,1)S(1)}, bf16[2,2,1280,128]{3,2,1,0:T(8,128)(2,1)S(1)}, u32[]{:S(2)}, u32[]{:S(2)}) collective-permute-start(bf16[2,2,1280,128]{3,2,1,0:T(8,128)(2,1)S(1)} %pad_maximum_fusion.2.refs_1_), channel_id=1, source_target_pairs={{0,1},{1,0},{2,3},{3,2},{4,5},{5,4},{6,7},{7,6},{8,9},{9,8},{10,11... | collective-permute-start | bytes 3932168 | tf_op jit(solution)/shard_map/ppermute | solution.py:225
  155.7 2.1 %copy-start.8 = (bf16[2,2560,128]{2,1,0:T(8,128)(2,1)}, bf16[2,2560,128]{2,1,0:T(8,128)(2,1)S(1)}, u32[]{:S(2)}) copy-start(bf16[2,2560,128]{2,1,0:T(8,128)(2,1)S(1)} %collective-permute-done.20.refs_10_) | copy-start | bytes 3932164
  157.7 1.1 copy-start.9
  157.8 19.8 %copy-start.5 = (bf16[2,2,1280,128]{3,2,1,0:T(8,128)(2,1)}, bf16[2,2,1280,128]{3,2,1,0:T(8,128)(2,1)S(1)}, u32[]{:S(2)}) copy-start(bf16[2,2,1280,128]{3,2,1,0:T(8,128)(2,1)S(1)} %pad_maximum_fusion.3.refs_2_) | copy-start | bytes 3932164
  157.8 4.7 %collective-permute-start.24 = (bf16[2,2,1280,128]{3,2,1,0:T(8,128)(2,1)S(1)}, bf16[2,2,1280,128]{3,2,1,0:T(8,128)(2,1)S(1)}, u32[]{:S(2)}, u32[]{:S(2)}) collective-permute-start(bf16[2,2,1280,128]{3,2,1,0:T(8,128)(2,1)S(1)} %pad_maximum_fusion.3.refs_2_), channel_id=1, source_target_pairs={{0,1},{1,0},{2,3},{3,2},{4,5},{5,4},{6,7},{7,6},{8,9},{9,8},{10,11... | collective-permute-start | bytes 3932168 | tf_op jit(solution)/shard_map/ppermute | solution.py:225
  158.7 18.8 %collective-permute-start.26 = (bf16[2,2560,128]{2,1,0:T(8,128)(2,1)S(1)}, bf16[2,2560,128]{2,1,0:T(8,128)(2,1)S(1)}, u32[]{:S(2)}, u32[]{:S(2)}) collective-permute-start(bf16[2,2560,128]{2,1,0:T(8,128)(2,1)S(1)} %collective-permute-done.19.refs_8_), channel_id=1, source_target_pairs={{0,8},{1,33},{2,10},{3,35},{4,12},{5,37},{6,14},{7,39},{8,16},{9,4... | collective-permute-start | bytes 3932168 | tf_op jit(solution)/shard_map/ppermute | solution.py:181
  159.2 18.4 %collective-permute-start.25 = (bf16[2,2560,128]{2,1,0:T(8,128)(2,1)S(1)}, bf16[2,2560,128]{2,1,0:T(8,128)(2,1)}, u32[]{:S(2)}, u32[]{:S(2)}) collective-permute-start(bf16[2,2560,128]{2,1,0:T(8,128)(2,1)S(1)} %collective-permute-done.16.refs_9_), channel_id=1, source_target_pairs={{0,24},{1,97},{2,26},{3,99},{4,28},{5,101},{6,30},{7,103},{8,0},{9... | collective-permute-start | bytes 3932168 | tf_op jit(solution)/shard_map/ppermute | solution.py:181
  162.5 15.0 %copy-start.10 = (bf16[2,2,1280,128]{3,2,1,0:T(8,128)(2,1)}, bf16[2,2,1280,128]{3,2,1,0:T(8,128)(2,1)S(1)}, u32[]{:S(2)}) copy-start(bf16[2,2,1280,128]{3,2,1,0:T(8,128)(2,1)S(1)} %collective-permute-done.23.refs_3_) | copy-start | bytes 3932164
  162.6 15.0 %copy-start.11 = (bf16[2,2,1280,128]{3,2,1,0:T(8,128)(2,1)}, bf16[2,2,1280,128]{3,2,1,0:T(8,128)(2,1)S(1)}, u32[]{:S(2)}) copy-start(bf16[2,2,1280,128]{3,2,1,0:T(8,128)(2,1)S(1)} %collective-permute-done.24.refs_4_) | copy-start | bytes 3932164
  177.6 1.1 copy-start.12

commit v2 on v1

--- a/solution.py
+++ b/solution.py
@@ -208,18 +208,14 @@
     far_a, far_b = shift_turned(high[:middle], False, -1), shift_turned(low[middle:], False, 1)
     rows = [lax.ppermute(rows[t], ALL_AXES, pairs[t][1]) for t in range(2)]
     near = jnp.stack([local, low])
+    near_low, near_high = shift_turned(near, True, 1), shift_turned(near, True, -1)
     far = jnp.stack([high, jnp.concatenate([far_a, far_b])])
     rows = jnp.stack(rows)
-    near, far, rows = stage((near, far, rows))
-
-    near_low, near_high = shift_turned(near, True, 1), shift_turned(near, True, -1)
+    far, rows = stage((far, rows))
+
     rows_low, rows_high = shift(rows, "x", 1), shift(rows, "x", -1)
-    far, near_low, near_high, rows_low, rows_high = stage((far, near_low, near_high, rows_low, rows_high))
-
     far_low, far_high = shift_turned(far, True, 1), shift_turned(far, True, -1)
     rows_far = jnp.stack([shift(rows_high[0], "x", -1), shift(rows_low[1], "x", 1)])
-    near_high, far_low, far_high, rows_far = stage((near_high, far_low, far_high, rows_far))
-
     near_far, far_far = shift_turned(near_high, True, -1), shift_turned(far_low, True, 1)
     rows_near, rows_far = jnp.stack([rows, rows_low]), jnp.stack([rows_high, rows_far])
     rows = [rows_near, rows_far, lax.ppermute(rows_near, "core", SWAP), lax.ppermute(rows_far, "core", SWAP)]

time: 201 us -> 198 us (0.985)
  starting transfers between devices: 48.3 us -> 42.1 us
  waiting for transfers between devices: 72.1 us -> 74.5 us
    ppermute x10, waiting for transfers between devices: 24.2 us -> 39.1 us  [shift_turned(): return lax.ppermute(value, ALL_AXES, pairs)]
    ppermute x10, waiting for transfers between devices: 33.5 us -> 26.5 us  [shift(): return lax.ppermute(value, axis, [(i, (i + by) % 4) for i in range(4)])]
    ppermute x2, waiting for transfers between devices: 5.59 us -> 0.01 us  [gather_both(): rows = [lax.ppermute(rows[t], ALL_AXES, pairs[t][1]) for t in range(2)]]
    ppermute x10, starting transfers between devices: 18.4 us -> 14.8 us  [shift_turned(): return lax.ppermute(value, ALL_AXES, pairs)]
  transfers between devices with their start and end apart: 27 -> 27, of which waited for: 15 -> 14; matrix products, arithmetic and copies ran while one was open for 3% -> 3% of each run, Pallas kernels for 0% -> 0%
where the time goes in v2:
time: 198 us; the launch traced here: 196 us
  waiting for transfers between devices  74.5 us (38%)
  starting transfers between devices  42.1 us (21%)
  blocking collectives  36.5 us (18%)
  Pallas kernels  34.8 us (18%)
  other arithmetic  5.77 us (3%)
    ppermute x10, waiting for transfers between devices, shift_turned(): return lax.ppermute(value, ALL_AXES, pairs)  39.1 us
    all_to_all x1, blocking collectives, shards(): lax.all_to_all(outgoing, AUX_AXES, split_axis=0, concat_axis=0, tiled=True)  36.5 us
    ppermute x10, waiting for transfers between devices, shift(): return lax.ppermute(value, axis, [(i, (i + by) % 4) for i in range(4)])  26.5 us
    pallas_call x1, Pallas kernels, exchange_block(): pl.pallas_call(lambda *refs: exchange_kernel(*refs, factor=1.0 / depth),...  22.1 us
    ppermute x10, starting transfers between devices, shift(): return lax.ppermute(value, axis, [(i, (i + by) % 4) for i in range(4)])  19.2 us
    ppermute x10, starting transfers between devices, shift_turned(): return lax.ppermute(value, ALL_AXES, pairs)  14.8 us
    ppermute x2, waiting for transfers between devices, gather_both(): lax.ppermute(jnp.where(turned, halves[1 - t], halves[t]), ALL_AXES, pairs...  7.75 us
    pallas_call x1, Pallas kernels, half_slots(): pl.pallas_call(half_kernel, grid_spec=pltpu.PrefetchScalarGridSpec(num_sc...  7.18 us
  transfers between devices with their start and end apart: 27, of which 14 were waited for; matrix products, arithmetic and copies ran while one was open for 3% of the time, Pallas kernels for 0%

profile of v2, /device:TPU:0, one launch (start us, length us, event | category | flops | bytes accessed | tf_op | source)
XLA Modules:
  0.0 196.1 jit_solution(11910225951286022024)
XLA Ops:
  0.0 7.2 %half_transform.1 = bf16[256,32,128]{2,1,0:T(8,128)(2,1)} custom-call(s32[1]{0:T(128)} %bitcast.20.self_ref, s32[128,128]{1,0:T(8,128)} %bitcast.123, s32[128,128]{1,0:T(8,128)} %bitcast.125, bf16[128,4,32,128]{3,2,1,0:T(8,128)(2,1)} %tiles_ref.1, bf16[32,20480]{1,0:T(8,128)(2,1)} %orbital_ref.1, s32[32,160]{1,0:T(8,128)} %support_ref.1), custom_call_target="tpu_custom_call" | custom-call | tf_op jit(solution)/shard_map/half_transform/pallas_call | solution.py:67
  7.2 36.5 %all_to_all.5.own_ref = bf16[256,32,128]{2,1,0:T(8,128)(2,1)S(1)} all-to-all(bf16[256,32,128]{2,1,0:T(8,128)(2,1)} %half_transform.1), channel_id=1, replica_groups=mesh['z'=4,'y'=4,'x'=4,'core'=2] {'z','y'}, dimensions={0} | all-to-all | bytes 4194304 | tf_op jit(solution)/shard_map/all_to_all | solution.py:300
  43.8 0.8 constant_dynamic-slice_fusion.1
  44.5 0.7 convert_reduce_fusion
  45.2 0.2 reduce_window_sum.11
  45.4 0.1 convolution_convert_fusion
  45.6 0.1 fusion.20
  45.7 1.1 select_reduce_fusion.list_ref
  46.8 1.2 collective-permute-done.other_ref
  48.0 5.5 %sum_slots.1 = (bf16[80,32,128]{2,1,0:T(8,128)(2,1)}, bf16[40,32,128]{2,1,0:T(8,128)(2,1)}, bf16[40,32,128]{2,1,0:T(8,128)(2,1)}, bf16[40,32,128]{2,1,0:T(8,128)...) custom-call(s32[2]{0:T(128)} %get-tuple-element.32.count_ref, ...), custom_call_target="tpu_custom_call" | custom-call | tf_op jit(solution)/shard_map/sum_slots/pallas_call | solution.py:115
  53.5 1.5 collective-permute-start.1
  55.0 1.8 collective-permute-start.5
  56.7 0.3 collective-permute-start.3
  57.0 3.0 %collective-permute-start.4 = (bf16[40,32,128]{2,1,0:T(8,128)(2,1)}, bf16[40,32,128]{2,1,0:T(8,128)(2,1)S(1)}, u32[]{:S(2)}, u32[]{:S(2)}) collective-permute-start(bf16[40,32,128]{2,1,0:T(8,128)(2,1)} %get-tuple-element.22), channel_id=1, source_target_pairs={{0,6},{2,0},{4,2},{6,4},{1,7},{3,1},{5,3},{7,5},{8,14},{10,8},{12,... | collective-permute-start | bytes 983048 | tf_op jit(solution)/shard_map/ppermute | solution.py:152
  60.0 5.5 %collective-permute-done.1 = bf16[40,32,128]{2,1,0:T(8,128)(2,1)S(1)} collective-permute-done((bf16[40,32,128]{2,1,0:T(8,128)(2,1)}, bf16[40,32,128]{2,1,0:T(8,128)(2,1)S(1)}, u32[]{:S(2)}, u32[]{:S(2)}) %collective-permute-start.1) | collective-permute-done | bytes 327712 | tf_op jit(solution)/shard_map/ppermute | solution.py:152
  65.5 1.1 add_convert_fusion.2
  66.5 0.3 collective-permute-start.2
  66.8 1.1 add_convert_fusion.1
  67.9 3.1 %collective-permute-start.6 = (bf16[40,32,128]{2,1,0:T(8,128)(2,1)S(1)}, bf16[40,32,128]{2,1,0:T(8,128)(2,1)S(1)}, u32[]{:S(2)}, u32[]{:S(2)}) collective-permute-start(bf16[40,32,128]{2,1,0:T(8,128)(2,1)S(1)} %add_convert_fusion.1), channel_id=1, source_target_pairs={{0,6},{2,0},{4,2},{6,4},{1,7},{3,1},{5,3},{7,5},{8,14},{10,8},{12,... | collective-permute-start | bytes 983048 | tf_op jit(solution)/shard_map/ppermute | solution.py:152
  71.0 1.5 collective-permute-done.3
  72.5 0.3 collective-permute-done.4
  72.8 5.9 %collective-permute-done.2 = bf16[40,32,128]{2,1,0:T(8,128)(2,1)S(1)} collective-permute-done((bf16[40,32,128]{2,1,0:T(8,128)(2,1)S(1)}, bf16[40,32,128]{2,1,0:T(8,128)(2,1)S(1)}, u32[]{:S(2)}, u32[]{:S(2)}) %collective-permute-start.2) | collective-permute-done | bytes 327712 | tf_op jit(solution)/shard_map/ppermute | solution.py:152
  78.7 0.1 collective-permute-done.6
  78.8 0.3 add_convert_fusion
  79.0 0.8 collective-permute-start.8
  79.8 1.3 collective-permute-start.7
  81.2 0.7 collective-permute-start.9
  81.9 3.3 %collective-permute-start.10 = (bf16[1280,128]{1,0:T(8,128)(2,1)S(1)}, bf16[1280,128]{1,0:T(8,128)(2,1)S(1)}, u32[]{:S(2)}, u32[]{:S(2)}) collective-permute-start(bf16[1280,128]{1,0:T(8,128)(2,1)S(1)} %bitcast.121), channel_id=1, source_target_pairs={{0,2},{1,7},{2,4},{3,1},{4,6},{5,3},{6,0},{7,5},{8,10},{9,15},{10,... | collective-permute-start | bytes 983048 | tf_op jit(solution)/shard_map/ppermute | solution.py:205
  85.1 0.0 collective-permute-done.9
  85.1 7.7 %collective-permute-done.10 = bf16[1280,128]{1,0:T(8,128)(2,1)S(1)} collective-permute-done((bf16[1280,128]{1,0:T(8,128)(2,1)S(1)}, bf16[1280,128]{1,0:T(8,128)(2,1)S(1)}, u32[]{:S(2)}, u32[]{:S(2)}) %collective-permute-start.10) | collective-permute-done | bytes 327712 | tf_op jit(solution)/shard_map/ppermute | solution.py:205
  92.9 0.0 collective-permute-done.8
  92.9 0.0 collective-permute-done.7
  93.0 3.2 %collective-permute-start.12 = (bf16[1280,128]{1,0:T(8,128)(2,1)S(1)}, bf16[1280,128]{1,0:T(8,128)(2,1)S(1)}, u32[]{:S(2)}, u32[]{:S(2)}) collective-permute-start(bf16[1280,128]{1,0:T(8,128)(2,1)S(1)} %slice.31), channel_id=1, source_target_pairs={{0,32},{1,9},{2,34},{3,11},{4,36},{5,13},{6,38},{7,15},{8,40},{9,1... | collective-permute-start | bytes 983048 | tf_op jit(solution)/shard_map/ppermute | solution.py:181
  96.1 0.1 collective-permute-start.11
  96.3 0.7 collective-permute-start.13
  96.9 2.9 %collective-permute-start.14 = (bf16[1280,128]{1,0:T(8,128)(2,1)S(1)}, bf16[1280,128]{1,0:T(8,128)(2,1)S(1)}, u32[]{:S(2)}, u32[]{:S(2)}) collective-permute-start(bf16[1280,128]{1,0:T(8,128)(2,1)S(1)} %collective-permute-done.10), channel_id=1, source_target_pairs={{2,10},{7,30},{4,44},{1,56},{6,78},{3,90},{0,104},{5,124},{10,11},... | collective-permute-start | bytes 983048 | tf_op jit(solution)/shard_map/ppermute | solution.py:209
  99.9 1.4 collective-permute-done.12
  101.3 12.5 %collective-permute-done.11 = bf16[1280,128]{1,0:T(8,128)(2,1)S(1)} collective-permute-done((bf16[1280,128]{1,0:T(8,128)(2,1)S(1)}, bf16[1280,128]{1,0:T(8,128)(2,1)S(1)}, u32[]{:S(2)}, u32[]{:S(2)}) %collective-permute-start.11) | collective-permute-done | bytes 327712 | tf_op jit(solution)/shard_map/ppermute | solution.py:181
  113.8 0.1 pad_maximum_fusion.refs_6_
  114.0 0.0 collective-permute-done.14
  114.0 0.1 pad_maximum_fusion.4
  114.0 5.5 %collective-permute-start.16 = (bf16[2,1280,128]{2,1,0:T(8,128)(2,1)S(1)}, bf16[2,1280,128]{2,1,0:T(8,128)(2,1)S(1)}, u32[]{:S(2)}, u32[]{:S(2)}) collective-permute-start(bf16[2,1280,128]{2,1,0:T(8,128)(2,1)S(1)} %pad_maximum_fusion.4), channel_id=1, source_target_pairs={{0,6},{2,0},{4,2},{6,4},{1,7},{3,1},{5,3},{7,5},{8,14},{10,8},{12,... | collective-permute-start | bytes 1966088 | tf_op jit(solution)/shard_map/ppermute | solution.py:152
  119.5 0.1 pad_maximum_fusion.3.refs_5_
  119.7 0.1 collective-permute-start.23
  119.8 2.0 %collective-permute-start.21 = (bf16[2,2560,128]{2,1,0:T(8,128)(2,1)S(1)}, bf16[2,2560,128]{2,1,0:T(8,128)(2,1)S(1)}, u32[]{:S(2)}, u32[]{:S(2)}) collective-permute-start(bf16[2,2560,128]{2,1,0:T(8,128)(2,1)S(1)} %pad_maximum_fusion.3.refs_5_), channel_id=1, source_target_pairs={{0,8},{1,33},{2,10},{3,35},{4,12},{5,37},{6,14},{7,39},{8,16},{9,4... | collective-permute-start | bytes 3932168 | tf_op jit(solution)/shard_map/ppermute | solution.py:181
  121.8 0.0 collective-permute-start.22
  121.8 8.8 %collective-permute-done.16 = bf16[2,1280,128]{2,1,0:T(8,128)(2,1)S(1)} collective-permute-done((bf16[2,1280,128]{2,1,0:T(8,128)(2,1)S(1)}, bf16[2,1280,128]{2,1,0:T(8,128)(2,1)S(1)}, u32[]{:S(2)}, u32[]{:S(2)}) %collective-permute-start.16) | collective-permute-done | bytes 655392 | tf_op jit(solution)/shard_map/ppermute | solution.py:152
  130.7 3.8 %collective-permute-start.17 = (bf16[1280,128]{1,0:T(8,128)(2,1)S(1)}, bf16[1280,128]{1,0:T(8,128)(2,1)S(1)}, u32[]{:S(2)}, u32[]{:S(2)}) collective-permute-start(bf16[1280,128]{1,0:T(8,128)(2,1)S(1)} %slice_bitcast_fusion.1), channel_id=1, source_target_pairs={{0,6},{2,0},{4,2},{6,4},{1,7},{3,1},{5,3},{7,5},{8,14},{10,8},{12,... | collective-permute-start | bytes 983048 | tf_op jit(solution)/shard_map/ppermute | solution.py:152
  134.5 0.1 collective-permute-start.18
  134.5 0.1 pad_maximum_fusion.1.refs_1_
  134.7 4.3 %collective-permute-done.17 = bf16[1280,128]{1,0:T(8,128)(2,1)S(1)} collective-permute-done((bf16[1280,128]{1,0:T(8,128)(2,1)S(1)}, bf16[1280,128]{1,0:T(8,128)(2,1)S(1)}, u32[]{:S(2)}, u32[]{:S(2)}) %collective-permute-start.17) | collective-permute-done | bytes 327712 | tf_op jit(solution)/shard_map/ppermute | solution.py:152
  139.0 4.0 %collective-permute-start.24 = (bf16[2,2560,128]{2,1,0:T(8,128)(2,1)S(1)}, bf16[2,2560,128]{2,1,0:T(8,128)(2,1)S(1)}, u32[]{:S(2)}, u32[]{:S(2)}) collective-permute-start(bf16[2,2560,128]{2,1,0:T(8,128)(2,1)S(1)} %pad_maximum_fusion.refs_6_), channel_id=1, source_target_pairs={{0,24},{1,97},{2,26},{3,99},{4,28},{5,101},{6,30},{7,103},{8,0},{9... | collective-permute-start | bytes 3932168 | tf_op jit(solution)/shard_map/ppermute | solution.py:181
  143.0 0.0 collective-permute-start.19
  143.1 0.1 maximum_bitcast_fusion.1
  143.1 0.1 pad_maximum_fusion.2.refs_2_
  143.3 0.6 collective-permute-start.20
  143.9 2.5 %collective-permute-start.25 = (bf16[2,2560,128]{2,1,0:T(8,128)(2,1)S(1)}, bf16[2,2560,128]{2,1,0:T(8,128)(2,1)S(1)}, u32[]{:S(2)}, u32[]{:S(2)}) collective-permute-start(bf16[2,2560,128]{2,1,0:T(8,128)(2,1)S(1)} %collective-permute-done.23.refs_9_), channel_id=1, source_target_pairs={{0,24},{1,97},{2,26},{3,99},{4,28},{5,101},{6,30},{7,103},{8,0},{9... | collective-permute-start | bytes 3932168 | tf_op jit(solution)/shard_map/ppermute | solution.py:181
  146.4 6.3 %collective-permute-done.22.refs_8_ = bf16[2,2560,128]{2,1,0:T(8,128)(2,1)S(1)} collective-permute-done((bf16[2,2560,128]{2,1,0:T(8,128)(2,1)S(1)}, bf16[2,2560,128]{2,1,0:T(8,128)(2,1)S(1)}, u32[]{:S(2)}, u32[]{:S(2)}) %collective-permute-start.22) | collective-permute-done | bytes 1310752 | tf_op jit(solution)/shard_map/ppermute | solution.py:181
  152.7 0.7 collective-permute-start.26
  153.4 0.6 pad_add_fusion.refs_0_
  154.0 4.8 %collective-permute-done.24.refs_10_ = bf16[2,2560,128]{2,1,0:T(8,128)(2,1)S(1)} collective-permute-done((bf16[2,2560,128]{2,1,0:T(8,128)(2,1)S(1)}, bf16[2,2560,128]{2,1,0:T(8,128)(2,1)S(1)}, u32[]{:S(2)}, u32[]{:S(2)}) %collective-permute-start.24) | collective-permute-done | bytes 1310752 | tf_op jit(solution)/shard_map/ppermute | solution.py:181
  158.8 14.0 %collective-permute-done.25.refs_11_ = bf16[2,2560,128]{2,1,0:T(8,128)(2,1)S(1)} collective-permute-done((bf16[2,2560,128]{2,1,0:T(8,128)(2,1)S(1)}, bf16[2,2560,128]{2,1,0:T(8,128)(2,1)S(1)}, u32[]{:S(2)}, u32[]{:S(2)}) %collective-permute-start.25) | collective-permute-done | bytes 1310752 | tf_op jit(solution)/shard_map/ppermute | solution.py:181
  172.9 1.0 copy-done.12
  174.0 22.1 %exchange.1 = f32[1280,2560]{1,0:T(8,128)} custom-call(s32[4]{0:T(128)} %pad_add_fusion.refs_0_, bf16[2,2,1280,128]{3,2,1,0:T(8,128)(2,1)} %copy-done.4, bf16[2,2,1280,128]{3,2,1,0:T(8,128)(2,1)} %copy-done.5, bf16[2,2,1280,128]{3,2,1,0:T(8,128)(2,1)} %copy-done.10, bf16[2,2,1280,128]{3,2,1,0:T(8,128)(2,1)} %copy-done.11, bf16[2,2560,128]{2,1,0:T(8,128)(2,1)} %copy-done.3, ...), custom_call_target="tpu_custom_call" | custom-call | tf_op jit(solution)/shard_map/exchange/pallas_call | solution.py:262
  (50 shorter events, 0.3 us)
Async XLA Ops:
  0.0 43.7 %copy-start = (s32[16384]{0:T(1024)S(1)}, s32[16384]{0:T(1024)}, u32[]{:S(2)}) copy-start(s32[16384]{0:T(1024)} %param.8) | copy-start | bytes 196612
  43.7 4.3 %copy-start.1 = (bf16[256,32,128]{2,1,0:T(8,128)(2,1)}, bf16[256,32,128]{2,1,0:T(8,128)(2,1)S(1)}, u32[]{:S(2)}) copy-start(bf16[256,32,128]{2,1,0:T(8,128)(2,1)S(1)} %all_to_all.5.own_ref) | copy-start | bytes 6291460
  43.7 4.3 %collective-permute-start = (bf16[256,32,128]{2,1,0:T(8,128)(2,1)S(1)}, bf16[256,32,128]{2,1,0:T(8,128)(2,1)}, u32[]{:S(2)}, u32[]{:S(2)}) collective-permute-start(bf16[256,32,128]{2,1,0:T(8,128)(2,1)S(1)} %all_to_all.5.own_ref), channel_id=1, source_target_pairs={{0,1},{1,0},{2,3},{3,2},{4,5},{5,4},{6,7},{7,6},{8,9},{9,8},{10,11... | collective-permute-start | bytes 6291464 | tf_op jit(solution)/shard_map/ppermute | solution.py:309
  53.5 25.3 %copy-start.13 = (bf16[80,32,128]{2,1,0:T(8,128)(2,1)S(1)}, bf16[80,32,128]{2,1,0:T(8,128)(2,1)}, u32[]{:S(2)}) copy-start(bf16[80,32,128]{2,1,0:T(8,128)(2,1)} %get-tuple-element.18) | copy-start | bytes 1966084
  53.5 12.0 %collective-permute-start.1 = (bf16[40,32,128]{2,1,0:T(8,128)(2,1)}, bf16[40,32,128]{2,1,0:T(8,128)(2,1)S(1)}, u32[]{:S(2)}, u32[]{:S(2)}) collective-permute-start(bf16[40,32,128]{2,1,0:T(8,128)(2,1)} %get-tuple-element.20), channel_id=1, source_target_pairs={{0,2},{2,4},{4,6},{6,0},{1,3},{3,5},{5,7},{7,1},{8,10},{10,12},{12... | collective-permute-start | bytes 983048 | tf_op jit(solution)/shard_map/ppermute | solution.py:152
  55.0 11.9 %collective-permute-start.5 = (bf16[40,32,128]{2,1,0:T(8,128)(2,1)}, bf16[40,32,128]{2,1,0:T(8,128)(2,1)S(1)}, u32[]{:S(2)}, u32[]{:S(2)}) collective-permute-start(bf16[40,32,128]{2,1,0:T(8,128)(2,1)} %get-tuple-element.24), channel_id=1, source_target_pairs={{0,6},{2,0},{4,2},{6,4},{1,7},{3,1},{5,3},{7,5},{8,14},{10,8},{12,... | collective-permute-start | bytes 983048 | tf_op jit(solution)/shard_map/ppermute | solution.py:152
  56.7 15.8 %collective-permute-start.3 = (bf16[40,32,128]{2,1,0:T(8,128)(2,1)}, bf16[40,32,128]{2,1,0:T(8,128)(2,1)S(1)}, u32[]{:S(2)}, u32[]{:S(2)}) collective-permute-start(bf16[40,32,128]{2,1,0:T(8,128)(2,1)} %get-tuple-element.21), channel_id=1, source_target_pairs={{0,2},{2,4},{4,6},{6,0},{1,3},{3,5},{5,7},{7,1},{8,10},{10,12},{12... | collective-permute-start | bytes 983048 | tf_op jit(solution)/shard_map/ppermute | solution.py:152
  57.0 15.8 %collective-permute-start.4 = (bf16[40,32,128]{2,1,0:T(8,128)(2,1)}, bf16[40,32,128]{2,1,0:T(8,128)(2,1)S(1)}, u32[]{:S(2)}, u32[]{:S(2)}) collective-permute-start(bf16[40,32,128]{2,1,0:T(8,128)(2,1)} %get-tuple-element.22), channel_id=1, source_target_pairs={{0,6},{2,0},{4,2},{6,4},{1,7},{3,1},{5,3},{7,5},{8,14},{10,8},{12,... | collective-permute-start | bytes 983048 | tf_op jit(solution)/shard_map/ppermute | solution.py:152
  66.5 12.2 %collective-permute-start.2 = (bf16[40,32,128]{2,1,0:T(8,128)(2,1)S(1)}, bf16[40,32,128]{2,1,0:T(8,128)(2,1)S(1)}, u32[]{:S(2)}, u32[]{:S(2)}) collective-permute-start(bf16[40,32,128]{2,1,0:T(8,128)(2,1)S(1)} %add_convert_fusion.2), channel_id=1, source_target_pairs={{0,2},{2,4},{4,6},{6,0},{1,3},{3,5},{5,7},{7,1},{8,10},{10,12},{12... | collective-permute-start | bytes 983048 | tf_op jit(solution)/shard_map/ppermute | solution.py:152
  67.9 10.9 %collective-permute-start.6 = (bf16[40,32,128]{2,1,0:T(8,128)(2,1)S(1)}, bf16[40,32,128]{2,1,0:T(8,128)(2,1)S(1)}, u32[]{:S(2)}, u32[]{:S(2)}) collective-permute-start(bf16[40,32,128]{2,1,0:T(8,128)(2,1)S(1)} %add_convert_fusion.1), channel_id=1, source_target_pairs={{0,6},{2,0},{4,2},{6,4},{1,7},{3,1},{5,3},{7,5},{8,14},{10,8},{12,... | collective-permute-start | bytes 983048 | tf_op jit(solution)/shard_map/ppermute | solution.py:152
  79.0 13.9 %collective-permute-start.8 = (bf16[2560,128]{1,0:T(8,128)(2,1)S(1)}, bf16[2560,128]{1,0:T(8,128)(2,1)S(1)}, u32[]{:S(2)}, u32[]{:S(2)}) collective-permute-start(bf16[2560,128]{1,0:T(8,128)(2,1)S(1)} %bitcast.109), channel_id=1, source_target_pairs={{0,96},{1,25},{2,98},{3,27},{4,100},{5,29},{6,102},{7,31},{8,104},... | collective-permute-start | bytes 1966088 | tf_op jit(solution)/shard_map/ppermute | solution.py:181
  79.8 13.1 %collective-permute-start.7 = (bf16[2560,128]{1,0:T(8,128)(2,1)S(1)}, bf16[2560,128]{1,0:T(8,128)(2,1)S(1)}, u32[]{:S(2)}, u32[]{:S(2)}) collective-permute-start(bf16[2560,128]{1,0:T(8,128)(2,1)S(1)} %bitcast.110), channel_id=1, source_target_pairs={{0,32},{1,9},{2,34},{3,11},{4,36},{5,13},{6,38},{7,15},{8,40},{9,1... | collective-permute-start | bytes 1966088 | tf_op jit(solution)/shard_map/ppermute | solution.py:181
  81.2 4.0 %collective-permute-start.9 = (bf16[1280,128]{1,0:T(8,128)(2,1)S(1)}, bf16[1280,128]{1,0:T(8,128)(2,1)S(1)}, u32[]{:S(2)}, u32[]{:S(2)}) collective-permute-start(bf16[1280,128]{1,0:T(8,128)(2,1)S(1)} %bitcast.122), channel_id=1, source_target_pairs={{0,0},{1,5},{2,2},{3,7},{4,4},{5,1},{6,6},{7,3},{8,8},{9,13},{10,1... | collective-permute-start | bytes 983048 | tf_op jit(solution)/shard_map/ppermute | solution.py:205
  81.9 11.0 %collective-permute-start.10 = (bf16[1280,128]{1,0:T(8,128)(2,1)S(1)}, bf16[1280,128]{1,0:T(8,128)(2,1)S(1)}, u32[]{:S(2)}, u32[]{:S(2)}) collective-permute-start(bf16[1280,128]{1,0:T(8,128)(2,1)S(1)} %bitcast.121), channel_id=1, source_target_pairs={{0,2},{1,7},{2,4},{3,1},{4,6},{5,3},{6,0},{7,5},{8,10},{9,15},{10,... | collective-permute-start | bytes 983048 | tf_op jit(solution)/shard_map/ppermute | solution.py:205
  93.0 8.4 %collective-permute-start.12 = (bf16[1280,128]{1,0:T(8,128)(2,1)S(1)}, bf16[1280,128]{1,0:T(8,128)(2,1)S(1)}, u32[]{:S(2)}, u32[]{:S(2)}) collective-permute-start(bf16[1280,128]{1,0:T(8,128)(2,1)S(1)} %slice.31), channel_id=1, source_target_pairs={{0,32},{1,9},{2,34},{3,11},{4,36},{5,13},{6,38},{7,15},{8,40},{9,1... | collective-permute-start | bytes 983048 | tf_op jit(solution)/shard_map/ppermute | solution.py:181
  96.1 17.6 %collective-permute-start.11 = (bf16[1280,128]{1,0:T(8,128)(2,1)S(1)}, bf16[1280,128]{1,0:T(8,128)(2,1)S(1)}, u32[]{:S(2)}, u32[]{:S(2)}) collective-permute-start(bf16[1280,128]{1,0:T(8,128)(2,1)S(1)} %slice.30), channel_id=1, source_target_pairs={{0,96},{1,25},{2,98},{3,27},{4,100},{5,29},{6,102},{7,31},{8,104},... | collective-permute-start | bytes 983048 | tf_op jit(solution)/shard_map/ppermute | solution.py:181
  96.3 17.7 %collective-permute-start.13 = (bf16[1280,128]{1,0:T(8,128)(2,1)S(1)}, bf16[1280,128]{1,0:T(8,128)(2,1)S(1)}, u32[]{:S(2)}, u32[]{:S(2)}) collective-permute-start(bf16[1280,128]{1,0:T(8,128)(2,1)S(1)} %collective-permute-done.9), channel_id=1, source_target_pairs={{0,0},{5,20},{2,34},{7,54},{4,68},{1,80},{6,102},{3,114},{8,1},{13... | collective-permute-start | bytes 983048 | tf_op jit(solution)/shard_map/ppermute | solution.py:209
  96.9 17.0 %collective-permute-start.14 = (bf16[1280,128]{1,0:T(8,128)(2,1)S(1)}, bf16[1280,128]{1,0:T(8,128)(2,1)S(1)}, u32[]{:S(2)}, u32[]{:S(2)}) collective-permute-start(bf16[1280,128]{1,0:T(8,128)(2,1)S(1)} %collective-permute-done.10), channel_id=1, source_target_pairs={{2,10},{7,30},{4,44},{1,56},{6,78},{3,90},{0,104},{5,124},{10,11},... | collective-permute-start | bytes 983048 | tf_op jit(solution)/shard_map/ppermute | solution.py:209
  113.9 25.1 %copy-start.2 = (bf16[2,2560,128]{2,1,0:T(8,128)(2,1)}, bf16[2,2560,128]{2,1,0:T(8,128)(2,1)S(1)}, u32[]{:S(2)}) copy-start(bf16[2,2560,128]{2,1,0:T(8,128)(2,1)S(1)} %pad_maximum_fusion.refs_6_) | copy-start | bytes 3932164
  114.0 16.6 %collective-permute-start.16 = (bf16[2,1280,128]{2,1,0:T(8,128)(2,1)S(1)}, bf16[2,1280,128]{2,1,0:T(8,128)(2,1)S(1)}, u32[]{:S(2)}, u32[]{:S(2)}) collective-permute-start(bf16[2,1280,128]{2,1,0:T(8,128)(2,1)S(1)} %pad_maximum_fusion.4), channel_id=1, source_target_pairs={{0,6},{2,0},{4,2},{6,4},{1,7},{3,1},{5,3},{7,5},{8,14},{10,8},{12,... | collective-permute-start | bytes 1966088 | tf_op jit(solution)/shard_map/ppermute | solution.py:152
  119.5 14.9 %collective-permute-start.15 = (bf16[2,1280,128]{2,1,0:T(8,128)(2,1)S(1)}, bf16[2,1280,128]{2,1,0:T(8,128)(2,1)S(1)}, u32[]{:S(2)}, u32[]{:S(2)}) collective-permute-start(bf16[2,1280,128]{2,1,0:T(8,128)(2,1)S(1)} %pad_maximum_fusion.4), channel_id=1, source_target_pairs={{0,2},{2,4},{4,6},{6,0},{1,3},{3,5},{5,7},{7,1},{8,10},{10,12},{12... | collective-permute-start | bytes 1966088 | tf_op jit(solution)/shard_map/ppermute | solution.py:152
  119.7 15.0 %copy-start.3 = (bf16[2,2560,128]{2,1,0:T(8,128)(2,1)}, bf16[2,2560,128]{2,1,0:T(8,128)(2,1)S(1)}, u32[]{:S(2)}) copy-start(bf16[2,2560,128]{2,1,0:T(8,128)(2,1)S(1)} %pad_maximum_fusion.3.refs_5_) | copy-start | bytes 3932164
  119.7 23.6 %collective-permute-start.23 = (bf16[2,2560,128]{2,1,0:T(8,128)(2,1)S(1)}, bf16[2,2560,128]{2,1,0:T(8,128)(2,1)S(1)}, u32[]{:S(2)}, u32[]{:S(2)}) collective-permute-start(bf16[2,2560,128]{2,1,0:T(8,128)(2,1)S(1)} %pad_maximum_fusion.3.refs_5_), channel_id=1, source_target_pairs={{0,24},{1,97},{2,26},{3,99},{4,28},{5,101},{6,30},{7,103},{8,0},{9... | collective-permute-start | bytes 3932168 | tf_op jit(solution)/shard_map/ppermute | solution.py:181
  119.8 24.1 %collective-permute-start.21 = (bf16[2,2560,128]{2,1,0:T(8,128)(2,1)S(1)}, bf16[2,2560,128]{2,1,0:T(8,128)(2,1)S(1)}, u32[]{:S(2)}, u32[]{:S(2)}) collective-permute-start(bf16[2,2560,128]{2,1,0:T(8,128)(2,1)S(1)} %pad_maximum_fusion.3.refs_5_), channel_id=1, source_target_pairs={{0,8},{1,33},{2,10},{3,35},{4,12},{5,37},{6,14},{7,39},{8,16},{9,4... | collective-permute-start | bytes 3932168 | tf_op jit(solution)/shard_map/ppermute | solution.py:181
  121.8 30.9 %collective-permute-start.22 = (bf16[2,2560,128]{2,1,0:T(8,128)(2,1)S(1)}, bf16[2,2560,128]{2,1,0:T(8,128)(2,1)S(1)}, u32[]{:S(2)}, u32[]{:S(2)}) collective-permute-start(bf16[2,2560,128]{2,1,0:T(8,128)(2,1)S(1)} %pad_maximum_fusion.refs_6_), channel_id=1, source_target_pairs={{0,8},{1,33},{2,10},{3,35},{4,12},{5,37},{6,14},{7,39},{8,16},{9,4... | collective-permute-start | bytes 3932168 | tf_op jit(solution)/shard_map/ppermute | solution.py:181
  130.7 8.4 %collective-permute-start.17 = (bf16[1280,128]{1,0:T(8,128)(2,1)S(1)}, bf16[1280,128]{1,0:T(8,128)(2,1)S(1)}, u32[]{:S(2)}, u32[]{:S(2)}) collective-permute-start(bf16[1280,128]{1,0:T(8,128)(2,1)S(1)} %slice_bitcast_fusion.1), channel_id=1, source_target_pairs={{0,6},{2,0},{4,2},{6,4},{1,7},{3,1},{5,3},{7,5},{8,14},{10,8},{12,... | collective-permute-start | bytes 983048 | tf_op jit(solution)/shard_map/ppermute | solution.py:152
  134.5 8.6 %collective-permute-start.18 = (bf16[1280,128]{1,0:T(8,128)(2,1)S(1)}, bf16[1280,128]{1,0:T(8,128)(2,1)S(1)}, u32[]{:S(2)}, u32[]{:S(2)}) collective-permute-start(bf16[1280,128]{1,0:T(8,128)(2,1)S(1)} %slice_bitcast_fusion), channel_id=1, source_target_pairs={{0,2},{2,4},{4,6},{6,0},{1,3},{3,5},{5,7},{7,1},{8,10},{10,12},{12... | collective-permute-start | bytes 983048 | tf_op jit(solution)/shard_map/ppermute | solution.py:152
  134.7 8.6 %copy-start.4 = (bf16[2,2,1280,128]{3,2,1,0:T(8,128)(2,1)}, bf16[2,2,1280,128]{3,2,1,0:T(8,128)(2,1)S(1)}, u32[]{:S(2)}) copy-start(bf16[2,2,1280,128]{3,2,1,0:T(8,128)(2,1)S(1)} %pad_maximum_fusion.1.refs_1_) | copy-start | bytes 3932164
  139.0 19.8 %collective-permute-start.24 = (bf16[2,2560,128]{2,1,0:T(8,128)(2,1)S(1)}, bf16[2,2560,128]{2,1,0:T(8,128)(2,1)S(1)}, u32[]{:S(2)}, u32[]{:S(2)}) collective-permute-start(bf16[2,2560,128]{2,1,0:T(8,128)(2,1)S(1)} %pad_maximum_fusion.refs_6_), channel_id=1, source_target_pairs={{0,24},{1,97},{2,26},{3,99},{4,28},{5,101},{6,30},{7,103},{8,0},{9... | collective-permute-start | bytes 3932168 | tf_op jit(solution)/shard_map/ppermute | solution.py:181
  143.0 15.8 %collective-permute-start.19 = (bf16[2,2,1280,128]{3,2,1,0:T(8,128)(2,1)S(1)}, bf16[2,2,1280,128]{3,2,1,0:T(8,128)(2,1)S(1)}, u32[]{:S(2)}, u32[]{:S(2)}) collective-permute-start(bf16[2,2,1280,128]{3,2,1,0:T(8,128)(2,1)S(1)} %pad_maximum_fusion.1.refs_1_), channel_id=1, source_target_pairs={{0,1},{1,0},{2,3},{3,2},{4,5},{5,4},{6,7},{7,6},{8,9},{9,8},{10,11... | collective-permute-start | bytes 3932168 | tf_op jit(solution)/shard_map/ppermute | solution.py:221
  143.3 29.7 %copy-start.5 = (bf16[2,2,1280,128]{3,2,1,0:T(8,128)(2,1)}, bf16[2,2,1280,128]{3,2,1,0:T(8,128)(2,1)S(1)}, u32[]{:S(2)}) copy-start(bf16[2,2,1280,128]{3,2,1,0:T(8,128)(2,1)S(1)} %pad_maximum_fusion.2.refs_2_) | copy-start | bytes 3932164
  143.3 29.6 %copy-start.6 = (bf16[2,2560,128]{2,1,0:T(8,128)(2,1)}, bf16[2,2560,128]{2,1,0:T(8,128)(2,1)S(1)}, u32[]{:S(2)}) copy-start(bf16[2,2560,128]{2,1,0:T(8,128)(2,1)S(1)} %collective-permute-done.23.refs_9_) | copy-start | bytes 3932164
  143.3 15.5 %collective-permute-start.20 = (bf16[2,2,1280,128]{3,2,1,0:T(8,128)(2,1)S(1)}, bf16[2,2,1280,128]{3,2,1,0:T(8,128)(2,1)S(1)}, u32[]{:S(2)}, u32[]{:S(2)}) collective-permute-start(bf16[2,2,1280,128]{3,2,1,0:T(8,128)(2,1)S(1)} %pad_maximum_fusion.2.refs_2_), channel_id=1, source_target_pairs={{0,1},{1,0},{2,3},{3,2},{4,5},{5,4},{6,7},{7,6},{8,9},{9,8},{10,11... | collective-permute-start | bytes 3932168 | tf_op jit(solution)/shard_map/ppermute | solution.py:221
  143.9 29.1 %copy-start.7 = (bf16[2,2560,128]{2,1,0:T(8,128)(2,1)}, bf16[2,2560,128]{2,1,0:T(8,128)(2,1)S(1)}, u32[]{:S(2)}) copy-start(bf16[2,2560,128]{2,1,0:T(8,128)(2,1)S(1)} %collective-permute-done.21.refs_7_) | copy-start | bytes 3932164
  143.9 29.0 %collective-permute-start.25 = (bf16[2,2560,128]{2,1,0:T(8,128)(2,1)S(1)}, bf16[2,2560,128]{2,1,0:T(8,128)(2,1)S(1)}, u32[]{:S(2)}, u32[]{:S(2)}) collective-permute-start(bf16[2,2560,128]{2,1,0:T(8,128)(2,1)S(1)} %collective-permute-done.23.refs_9_), channel_id=1, source_target_pairs={{0,24},{1,97},{2,26},{3,99},{4,28},{5,101},{6,30},{7,103},{8,0},{9... | collective-permute-start | bytes 3932168 | tf_op jit(solution)/shard_map/ppermute | solution.py:181
  152.7 20.2 %copy-start.8 = (bf16[2,2560,128]{2,1,0:T(8,128)(2,1)}, bf16[2,2560,128]{2,1,0:T(8,128)(2,1)S(1)}, u32[]{:S(2)}) copy-start(bf16[2,2560,128]{2,1,0:T(8,128)(2,1)S(1)} %collective-permute-done.22.refs_8_) | copy-start | bytes 3932164
  152.7 20.2 %collective-permute-start.26 = (bf16[2,2560,128]{2,1,0:T(8,128)(2,1)S(1)}, bf16[2,2560,128]{2,1,0:T(8,128)(2,1)}, u32[]{:S(2)}, u32[]{:S(2)}) collective-permute-start(bf16[2,2560,128]{2,1,0:T(8,128)(2,1)S(1)} %collective-permute-done.22.refs_8_), channel_id=1, source_target_pairs={{0,8},{1,33},{2,10},{3,35},{4,12},{5,37},{6,14},{7,39},{8,16},{9,4... | collective-permute-start | bytes 3932168 | tf_op jit(solution)/shard_map/ppermute | solution.py:181
  158.8 14.0 %copy-start.9 = (bf16[2,2560,128]{2,1,0:T(8,128)(2,1)}, bf16[2,2560,128]{2,1,0:T(8,128)(2,1)S(1)}, u32[]{:S(2)}) copy-start(bf16[2,2560,128]{2,1,0:T(8,128)(2,1)S(1)} %collective-permute-done.24.refs_10_) | copy-start | bytes 3932164
  158.8 14.0 %copy-start.10 = (bf16[2,2,1280,128]{3,2,1,0:T(8,128)(2,1)}, bf16[2,2,1280,128]{3,2,1,0:T(8,128)(2,1)S(1)}, u32[]{:S(2)}) copy-start(bf16[2,2,1280,128]{3,2,1,0:T(8,128)(2,1)S(1)} %collective-permute-done.19.refs_3_) | copy-start | bytes 3932164
  158.8 14.0 %copy-start.11 = (bf16[2,2,1280,128]{3,2,1,0:T(8,128)(2,1)}, bf16[2,2,1280,128]{3,2,1,0:T(8,128)(2,1)S(1)}, u32[]{:S(2)}) copy-start(bf16[2,2,1280,128]{3,2,1,0:T(8,128)(2,1)S(1)} %collective-permute-done.20.refs_4_) | copy-start | bytes 3932164
  172.9 1.1 copy-start.12

commit v3 on v2

--- a/solution.py
+++ b/solution.py
@@ -11,8 +11,11 @@
 ALL_AXES = AUX_AXES + BAS_AXES
 TILE_STEP = 32
 COL_STEP = 256
+COL_LOAD = 512
+OUT_PARTS = 4
 SWAP = [(0, 1), (1, 0)]
 VMEM_LIMIT = 56 * 1024 * 1024
+EXCHANGE_LIMIT = 36 * 1024 * 1024
 
 
 def half_kernel(self_ref, owner_ref, col_ref, tiles_ref, orbital_ref, support_ref, out_ref, count_ref, kept_ref):
@@ -223,52 +226,96 @@
 
 
 def exchange_kernel(at_ref, *refs, factor):
-    row_refs, col_refs, (out_ref, row_data) = refs[:4], refs[4:-2], refs[-2:]
-    width = row_refs[0].shape[-1]
-
-    @pl.when(pl.program_id(0) == 0)
-    def _():
-        z_place, y_place, x_place, core = (at_ref[i] for i in range(4))
-
-        def order(offset):
-            odd = lax.bitwise_and(offset, 1)
-            half = lax.shift_right_logical(offset, 1)
-            return jnp.where(odd == 1, 2 - half, offset + half)
-
-        for core_from, pair in ((core, row_refs[:2]), (1 - core, row_refs[2:])):
-            for index, offset in enumerate((0, -1, 1, 2)):
-                for turn in range(2):
-                    zg = lax.bitwise_and(x_place + offset - y_place - z_place, 3)
-                    yg = 2 * lax.bitwise_xor(lax.bitwise_and(y_place, 1), turn) + core_from
-                    z_at = order(lax.bitwise_and(zg - z_place, 3))
-                    y_at = order(lax.bitwise_and(yg - y_place, 3))
-                    place = jnp.where(core == 0, 4 * y_at + z_at, 4 * z_at + y_at)
-                    columns = pl.ds(pl.multiple_of(place * width, width), width)
-                    row_data[:, columns] = pair[index // 2][index % 2, turn]
-
-    columns = jnp.concatenate([col_ref[i] for col_ref in col_refs for i in range(2)], axis=1)
-    out_ref[...] = (
-        lax.dot_general(
-            row_data[...], columns, (((1,), (1,)), ((), ())), preferred_element_type=jnp.float32
+    row_refs, col_refs = refs[:4], refs[4:12]
+    out_ref, row_data, col_data, out_data, row_sem, col_sem, out_sem = refs[12:]
+    width = col_data.shape[-1]
+    rows, col_count = out_data.shape
+    z_place, y_place, x_place, core = (at_ref[i] for i in range(4))
+
+    def order(offset):
+        odd = lax.bitwise_and(offset, 1)
+        half = lax.shift_right_logical(offset, 1)
+        return jnp.where(odd == 1, 2 - half, offset + half)
+
+    row_copies = []
+    for core_from, pair in ((core, row_refs[:2]), (1 - core, row_refs[2:])):
+        for index, offset in enumerate((0, -1, 1, 2)):
+            for turn in range(2):
+                zg = lax.bitwise_and(x_place + offset - y_place - z_place, 3)
+                yg = 2 * lax.bitwise_xor(lax.bitwise_and(y_place, 1), turn) + core_from
+                z_at = order(lax.bitwise_and(zg - z_place, 3))
+                y_at = order(lax.bitwise_and(yg - y_place, 3))
+                place = jnp.where(core == 0, 4 * y_at + z_at, 4 * z_at + y_at)
+                row_copies.append(
+                    pltpu.make_async_copy(
+                        pair[index // 2].at[index % 2, turn],
+                        row_data.at[:, pl.ds(pl.multiple_of(place * width, width), width)],
+                        row_sem.at[len(row_copies)],
+                    )
+                )
+    col_copies = []
+    for first in range(0, col_count, COL_LOAD):
+        part = pl.ds(first, COL_LOAD)
+        col_copies.append(
+            [
+                pltpu.make_async_copy(
+                    col_ref.at[:, part],
+                    col_data.at[pl.ds(2 * index, 2), part],
+                    col_sem.at[len(col_copies), index],
+                )
+                for index, col_ref in enumerate(col_refs)
+            ]
         )
-        * factor
-    )
+    for copy in row_copies + sum(col_copies, []):
+        copy.start()
+    for copy in row_copies:
+        copy.wait()
+
+    out_copies = []
+    out_rows = rows // OUT_PARTS
+    for first in range(0, col_count, COL_STEP):
+        if first % COL_LOAD == 0:
+            for copy in col_copies[first // COL_LOAD]:
+                copy.wait()
+        part = pl.ds(first, COL_STEP)
+        columns = jnp.concatenate([col_data[group, part] for group in range(col_data.shape[0])], axis=1)
+        out_data[:, part] = (
+            lax.dot_general(
+                row_data[...], columns, (((1,), (1,)), ((), ())), preferred_element_type=jnp.float32
+            )
+            * factor
+        )
+        for index in range(OUT_PARTS):
+            block = pl.ds(index * out_rows, out_rows)
+            copy = pltpu.make_async_copy(
+                out_data.at[block, part], out_ref.at[block, part], out_sem.at[len(out_copies)]
+            )
+            copy.start()
+            out_copies.append(copy)
+    for copy in out_copies:
+        copy.wait()
 
 
 def exchange_block(at, row_parts, pieces):
     offsets, turns, rows, width = row_parts[0].shape
     col_count = pieces[0].shape[1]
-    depth = 2 * len(pieces) * width
+    groups = 2 * len(pieces)
+    depth = groups * width
     return pl.pallas_call(
         lambda *refs: exchange_kernel(*refs, factor=1.0 / depth),
-        grid=(col_count // COL_STEP,),
         in_specs=[pl.BlockSpec(memory_space=pltpu.SMEM)]
-        + [pl.BlockSpec(row_parts[0].shape, lambda j: (0, 0, 0, 0))] * len(row_parts)
-        + [pl.BlockSpec((2, COL_STEP, width), lambda j: (0, j, 0))] * len(pieces),
-        out_specs=pl.BlockSpec((rows, COL_STEP), lambda j: (0, j)),
+        + [pl.BlockSpec(memory_space=pl.ANY)] * (len(row_parts) + len(pieces)),
+        out_specs=pl.BlockSpec(memory_space=pl.ANY),
         out_shape=jax.ShapeDtypeStruct((rows, col_count), jnp.float32),
-        scratch_shapes=[pltpu.VMEM((rows, depth), jnp.bfloat16)],
-        compiler_params=pltpu.CompilerParams(vmem_limit_bytes=VMEM_LIMIT),
+        scratch_shapes=[
+            pltpu.VMEM((rows, depth), jnp.bfloat16),
+            pltpu.VMEM((groups, col_count, width), jnp.bfloat16),
+            pltpu.VMEM((rows, col_count), jnp.float32),
+            pltpu.SemaphoreType.DMA((groups,)),
+            pltpu.SemaphoreType.DMA((col_count // COL_LOAD, len(pieces))),
+            pltpu.SemaphoreType.DMA((col_count // COL_STEP * OUT_PARTS,)),
+        ],
+        compiler_params=pltpu.CompilerParams(vmem_limit_bytes=EXCHANGE_LIMIT),
         name="exchange",
     )(at, *row_parts, *pieces)
 

time: 198 us -> 195 us (0.985)
  starting transfers between devices: 42.1 us -> 47.2 us
  waiting for transfers between devices: 74.5 us -> 70.3 us
    ppermute x10, waiting for transfers between devices: 39.1 us -> 30.5 us  [shift_turned(): return lax.ppermute(value, ALL_AXES, pairs)]
    ppermute x2, waiting for transfers between devices: 0.01 us -> 4.64 us  [gather_both(): rows = [lax.ppermute(rows[t], ALL_AXES, pairs[t][1]) for t in range(2)]]
    ppermute x10, starting transfers between devices: 19.2 us -> 23.3 us  [shift(): return lax.ppermute(value, axis, [(i, (i + by) % 4) for i in range(4)])]
where the time goes in v3:
time: 195 us; the launch traced here: 194 us
  waiting for transfers between devices  70.3 us (36%)
  starting transfers between devices  47.2 us (24%)
  blocking collectives  36.5 us (19%)
  Pallas kernels  33.3 us (17%)
  other arithmetic  5.31 us (3%)
    all_to_all x1, blocking collectives, shards(): lax.all_to_all(outgoing, AUX_AXES, split_axis=0, concat_axis=0, tiled=True)  36.5 us
    ppermute x10, waiting for transfers between devices, shift_turned(): return lax.ppermute(value, ALL_AXES, pairs)  30.5 us
    ppermute x10, waiting for transfers between devices, shift(): return lax.ppermute(value, axis, [(i, (i + by) % 4) for i in range(4)])  26.5 us
    ppermute x10, starting transfers between devices, shift(): return lax.ppermute(value, axis, [(i, (i + by) % 4) for i in range(4)])  23.3 us
    pallas_call x1, Pallas kernels, exchange_block(): pl.pallas_call(lambda *refs: exchange_kernel(*refs, factor=1.0 / depth),...  20.5 us
    ppermute x10, starting transfers between devices, shift_turned(): return lax.ppermute(value, ALL_AXES, pairs)  15.8 us
    ppermute x2, waiting for transfers between devices, gather_both(): lax.ppermute(jnp.where(turned, halves[1 - t], halves[t]), ALL_AXES, pairs...  7.5 us
    pallas_call x1, Pallas kernels, half_slots(): pl.pallas_call(half_kernel, grid_spec=pltpu.PrefetchScalarGridSpec(num_sc...  7.2 us
  transfers between devices with their start and end apart: 27, of which 14 were waited for; matrix products, arithmetic and copies ran while one was open for 3% of the time, Pallas kernels for 0%

profile of v3, /device:TPU:0, one launch (start us, length us, event | category | flops | bytes accessed | tf_op | source)
XLA Modules:
  0.0 194.1 jit_solution(7664436163955649821)
XLA Ops:
  0.0 7.2 %half_transform.1 = bf16[256,32,128]{2,1,0:T(8,128)(2,1)} custom-call(s32[1]{0:T(128)} %bitcast.20.self_ref, s32[128,128]{1,0:T(8,128)} %bitcast.123, s32[128,128]{1,0:T(8,128)} %bitcast.125, bf16[128,4,32,128]{3,2,1,0:T(8,128)(2,1)} %tiles_ref.1, bf16[32,20480]{1,0:T(8,128)(2,1)} %orbital_ref.1, s32[32,160]{1,0:T(8,128)} %support_ref.1), custom_call_target="tpu_custom_call" | custom-call | tf_op jit(solution)/shard_map/half_transform/pallas_call | solution.py:70
  7.2 36.5 %all_to_all.5.own_ref = bf16[256,32,128]{2,1,0:T(8,128)(2,1)S(1)} all-to-all(bf16[256,32,128]{2,1,0:T(8,128)(2,1)} %half_transform.1), channel_id=1, replica_groups=mesh['z'=4,'y'=4,'x'=4,'core'=2] {'z','y'}, dimensions={0} | all-to-all | bytes 4194304 | tf_op jit(solution)/shard_map/all_to_all | solution.py:347
  43.8 0.8 constant_dynamic-slice_fusion.1
  44.5 0.8 convert_reduce_fusion
  45.3 0.2 reduce_window_sum.11
  45.5 0.1 convolution_convert_fusion
  45.6 0.1 fusion.20
  45.7 1.1 select_reduce_fusion.list_ref
  46.8 1.2 collective-permute-done.other_ref
  48.0 5.6 %sum_slots.1 = (bf16[80,32,128]{2,1,0:T(8,128)(2,1)}, bf16[40,32,128]{2,1,0:T(8,128)(2,1)}, bf16[40,32,128]{2,1,0:T(8,128)(2,1)}, bf16[40,32,128]{2,1,0:T(8,128)...) custom-call(s32[2]{0:T(128)} %get-tuple-element.32.count_ref, ...), custom_call_target="tpu_custom_call" | custom-call | tf_op jit(solution)/shard_map/sum_slots/pallas_call | solution.py:118
  53.7 1.6 collective-permute-start.1
  55.3 1.6 collective-permute-start.5
  56.9 0.4 collective-permute-start.3
  57.3 2.9 %collective-permute-start.4 = (bf16[40,32,128]{2,1,0:T(8,128)(2,1)}, bf16[40,32,128]{2,1,0:T(8,128)(2,1)S(1)}, u32[]{:S(2)}, u32[]{:S(2)}) collective-permute-start(bf16[40,32,128]{2,1,0:T(8,128)(2,1)} %get-tuple-element.22), channel_id=1, source_target_pairs={{0,6},{2,0},{4,2},{6,4},{1,7},{3,1},{5,3},{7,5},{8,14},{10,8},{12,... | collective-permute-start | bytes 983048 | tf_op jit(solution)/shard_map/ppermute | solution.py:155
  60.1 5.5 %collective-permute-done.1 = bf16[40,32,128]{2,1,0:T(8,128)(2,1)S(1)} collective-permute-done((bf16[40,32,128]{2,1,0:T(8,128)(2,1)}, bf16[40,32,128]{2,1,0:T(8,128)(2,1)S(1)}, u32[]{:S(2)}, u32[]{:S(2)}) %collective-permute-start.1) | collective-permute-done | bytes 327712 | tf_op jit(solution)/shard_map/ppermute | solution.py:155
  65.7 1.1 add_convert_fusion.2
  66.7 0.5 collective-permute-start.2
  67.2 0.0 collective-permute-done.5
  67.2 1.1 add_convert_fusion.1
  68.3 2.9 %collective-permute-start.6 = (bf16[40,32,128]{2,1,0:T(8,128)(2,1)S(1)}, bf16[40,32,128]{2,1,0:T(8,128)(2,1)S(1)}, u32[]{:S(2)}, u32[]{:S(2)}) collective-permute-start(bf16[40,32,128]{2,1,0:T(8,128)(2,1)S(1)} %add_convert_fusion.1), channel_id=1, source_target_pairs={{0,6},{2,0},{4,2},{6,4},{1,7},{3,1},{5,3},{7,5},{8,14},{10,8},{12,... | collective-permute-start | bytes 983048 | tf_op jit(solution)/shard_map/ppermute | solution.py:155
  71.2 1.5 collective-permute-done.3
  72.7 0.4 collective-permute-done.4
  73.1 5.8 %collective-permute-done.2 = bf16[40,32,128]{2,1,0:T(8,128)(2,1)S(1)} collective-permute-done((bf16[40,32,128]{2,1,0:T(8,128)(2,1)S(1)}, bf16[40,32,128]{2,1,0:T(8,128)(2,1)S(1)}, u32[]{:S(2)}, u32[]{:S(2)}) %collective-permute-start.2) | collective-permute-done | bytes 327712 | tf_op jit(solution)/shard_map/ppermute | solution.py:155
  78.9 0.0 collective-permute-done.6
  78.9 0.3 add_convert_fusion
  79.2 0.8 collective-permute-start.8
  80.0 1.3 collective-permute-start.7
  81.3 0.7 collective-permute-start.9
  82.0 3.6 %collective-permute-start.10 = (bf16[1280,128]{1,0:T(8,128)(2,1)S(1)}, bf16[1280,128]{1,0:T(8,128)(2,1)S(1)}, u32[]{:S(2)}, u32[]{:S(2)}) collective-permute-start(bf16[1280,128]{1,0:T(8,128)(2,1)S(1)} %bitcast.121), channel_id=1, source_target_pairs={{0,2},{1,7},{2,4},{3,1},{4,6},{5,3},{6,0},{7,5},{8,10},{9,15},{10,... | collective-permute-start | bytes 983048 | tf_op jit(solution)/shard_map/ppermute | solution.py:208
  85.6 0.0 collective-permute-done.9
  85.6 7.5 %collective-permute-done.10 = bf16[1280,128]{1,0:T(8,128)(2,1)S(1)} collective-permute-done((bf16[1280,128]{1,0:T(8,128)(2,1)S(1)}, bf16[1280,128]{1,0:T(8,128)(2,1)S(1)}, u32[]{:S(2)}, u32[]{:S(2)}) %collective-permute-start.10) | collective-permute-done | bytes 327712 | tf_op jit(solution)/shard_map/ppermute | solution.py:208
  93.1 3.2 %collective-permute-start.12 = (bf16[1280,128]{1,0:T(8,128)(2,1)S(1)}, bf16[1280,128]{1,0:T(8,128)(2,1)S(1)}, u32[]{:S(2)}, u32[]{:S(2)}) collective-permute-start(bf16[1280,128]{1,0:T(8,128)(2,1)S(1)} %slice.31), channel_id=1, source_target_pairs={{0,32},{1,9},{2,34},{3,11},{4,36},{5,13},{6,38},{7,15},{8,40},{9,1... | collective-permute-start | bytes 983048 | tf_op jit(solution)/shard_map/ppermute | solution.py:184
  96.3 0.1 collective-permute-start.11
  96.5 0.7 collective-permute-start.13
  97.1 2.6 %collective-permute-start.14 = (bf16[1280,128]{1,0:T(8,128)(2,1)S(1)}, bf16[1280,128]{1,0:T(8,128)(2,1)S(1)}, u32[]{:S(2)}, u32[]{:S(2)}) collective-permute-start(bf16[1280,128]{1,0:T(8,128)(2,1)S(1)} %collective-permute-done.10), channel_id=1, source_target_pairs={{2,10},{7,30},{4,44},{1,56},{6,78},{3,90},{0,104},{5,124},{10,11},... | collective-permute-start | bytes 983048 | tf_op jit(solution)/shard_map/ppermute | solution.py:212
  99.8 1.7 collective-permute-done.12
  101.5 3.7 %collective-permute-done.11 = bf16[1280,128]{1,0:T(8,128)(2,1)S(1)} collective-permute-done((bf16[1280,128]{1,0:T(8,128)(2,1)S(1)}, bf16[1280,128]{1,0:T(8,128)(2,1)S(1)}, u32[]{:S(2)}, u32[]{:S(2)}) %collective-permute-start.11) | collective-permute-done | bytes 327712 | tf_op jit(solution)/shard_map/ppermute | solution.py:184
  105.2 0.1 pad_maximum_fusion.refs_6_
  105.4 4.6 %collective-permute-done.14 = bf16[1280,128]{1,0:T(8,128)(2,1)S(1)} collective-permute-done((bf16[1280,128]{1,0:T(8,128)(2,1)S(1)}, bf16[1280,128]{1,0:T(8,128)(2,1)S(1)}, u32[]{:S(2)}, u32[]{:S(2)}) %collective-permute-start.14) | collective-permute-done | bytes 327712 | tf_op jit(solution)/shard_map/ppermute | solution.py:212
  110.0 0.1 pad_maximum_fusion.4
  110.1 9.6 %collective-permute-start.16 = (bf16[2,1280,128]{2,1,0:T(8,128)(2,1)S(1)}, bf16[2,1280,128]{2,1,0:T(8,128)(2,1)S(1)}, u32[]{:S(2)}, u32[]{:S(2)}) collective-permute-start(bf16[2,1280,128]{2,1,0:T(8,128)(2,1)S(1)} %pad_maximum_fusion.4), channel_id=1, source_target_pairs={{0,6},{2,0},{4,2},{6,4},{1,7},{3,1},{5,3},{7,5},{8,14},{10,8},{12,... | collective-permute-start | bytes 1966088 | tf_op jit(solution)/shard_map/ppermute | solution.py:155
  119.7 0.1 pad_maximum_fusion.3.refs_5_
  119.8 0.1 collective-permute-start.23
  119.9 2.0 %collective-permute-start.21 = (bf16[2,2560,128]{2,1,0:T(8,128)(2,1)S(1)}, bf16[2,2560,128]{2,1,0:T(8,128)(2,1)S(1)}, u32[]{:S(2)}, u32[]{:S(2)}) collective-permute-start(bf16[2,2560,128]{2,1,0:T(8,128)(2,1)S(1)} %pad_maximum_fusion.3.refs_5_), channel_id=1, source_target_pairs={{0,8},{1,33},{2,10},{3,35},{4,12},{5,37},{6,14},{7,39},{8,16},{9,4... | collective-permute-start | bytes 3932168 | tf_op jit(solution)/shard_map/ppermute | solution.py:184
  121.9 0.0 collective-permute-start.22
  122.0 8.9 %collective-permute-done.16 = bf16[2,1280,128]{2,1,0:T(8,128)(2,1)S(1)} collective-permute-done((bf16[2,1280,128]{2,1,0:T(8,128)(2,1)S(1)}, bf16[2,1280,128]{2,1,0:T(8,128)(2,1)S(1)}, u32[]{:S(2)}, u32[]{:S(2)}) %collective-permute-start.16) | collective-permute-done | bytes 655392 | tf_op jit(solution)/shard_map/ppermute | solution.py:155
  130.8 3.8 %collective-permute-start.17 = (bf16[1280,128]{1,0:T(8,128)(2,1)S(1)}, bf16[1280,128]{1,0:T(8,128)(2,1)S(1)}, u32[]{:S(2)}, u32[]{:S(2)}) collective-permute-start(bf16[1280,128]{1,0:T(8,128)(2,1)S(1)} %slice_bitcast_fusion.1), channel_id=1, source_target_pairs={{0,6},{2,0},{4,2},{6,4},{1,7},{3,1},{5,3},{7,5},{8,14},{10,8},{12,... | collective-permute-start | bytes 983048 | tf_op jit(solution)/shard_map/ppermute | solution.py:155
  134.6 0.0 collective-permute-done.15
  134.6 0.1 collective-permute-start.18
  134.7 0.1 pad_maximum_fusion.1.refs_1_
  134.8 4.4 %collective-permute-done.17 = bf16[1280,128]{1,0:T(8,128)(2,1)S(1)} collective-permute-done((bf16[1280,128]{1,0:T(8,128)(2,1)S(1)}, bf16[1280,128]{1,0:T(8,128)(2,1)S(1)}, u32[]{:S(2)}, u32[]{:S(2)}) %collective-permute-start.17) | collective-permute-done | bytes 327712 | tf_op jit(solution)/shard_map/ppermute | solution.py:155
  139.2 5.1 %collective-permute-start.24 = (bf16[2,2560,128]{2,1,0:T(8,128)(2,1)S(1)}, bf16[2,2560,128]{2,1,0:T(8,128)(2,1)S(1)}, u32[]{:S(2)}, u32[]{:S(2)}) collective-permute-start(bf16[2,2560,128]{2,1,0:T(8,128)(2,1)S(1)} %pad_maximum_fusion.refs_6_), channel_id=1, source_target_pairs={{0,24},{1,97},{2,26},{3,99},{4,28},{5,101},{6,30},{7,103},{8,0},{9... | collective-permute-start | bytes 3932168 | tf_op jit(solution)/shard_map/ppermute | solution.py:184
  144.3 0.0 collective-permute-done.18
  144.3 0.0 collective-permute-start.19
  144.3 0.1 maximum_bitcast_fusion.1
  144.3 0.1 pad_maximum_fusion.2.refs_2_
  144.5 0.6 collective-permute-start.20
  145.1 2.5 %collective-permute-start.25 = (bf16[2,2560,128]{2,1,0:T(8,128)(2,1)S(1)}, bf16[2,2560,128]{2,1,0:T(8,128)(2,1)S(1)}, u32[]{:S(2)}, u32[]{:S(2)}) collective-permute-start(bf16[2,2560,128]{2,1,0:T(8,128)(2,1)S(1)} %collective-permute-done.23.refs_9_), channel_id=1, source_target_pairs={{0,24},{1,97},{2,26},{3,99},{4,28},{5,101},{6,30},{7,103},{8,0},{9... | collective-permute-start | bytes 3932168 | tf_op jit(solution)/shard_map/ppermute | solution.py:184
  147.6 5.3 %collective-permute-done.22.refs_8_ = bf16[2,2560,128]{2,1,0:T(8,128)(2,1)S(1)} collective-permute-done((bf16[2,2560,128]{2,1,0:T(8,128)(2,1)S(1)}, bf16[2,2560,128]{2,1,0:T(8,128)(2,1)S(1)}, u32[]{:S(2)}, u32[]{:S(2)}) %collective-permute-start.22) | collective-permute-done | bytes 1310752 | tf_op jit(solution)/shard_map/ppermute | solution.py:184
  152.8 0.7 collective-permute-start.26
  153.6 0.1 pad_add_fusion.refs_0_
  153.6 5.7 %collective-permute-done.24.refs_10_ = bf16[2,2560,128]{2,1,0:T(8,128)(2,1)S(1)} collective-permute-done((bf16[2,2560,128]{2,1,0:T(8,128)(2,1)S(1)}, bf16[2,2560,128]{2,1,0:T(8,128)(2,1)S(1)}, u32[]{:S(2)}, u32[]{:S(2)}) %collective-permute-start.24) | collective-permute-done | bytes 1310752 | tf_op jit(solution)/shard_map/ppermute | solution.py:184
  159.4 14.0 %collective-permute-done.25.refs_11_ = bf16[2,2560,128]{2,1,0:T(8,128)(2,1)S(1)} collective-permute-done((bf16[2,2560,128]{2,1,0:T(8,128)(2,1)S(1)}, bf16[2,2560,128]{2,1,0:T(8,128)(2,1)S(1)}, u32[]{:S(2)}, u32[]{:S(2)}) %collective-permute-start.25) | collective-permute-done | bytes 1310752 | tf_op jit(solution)/shard_map/ppermute | solution.py:184
  173.4 20.5 %exchange.1 = f32[1280,2560]{1,0:T(8,128)} custom-call(s32[4]{0:T(128)S(1)} %pad_add_fusion.refs_0_, bf16[2,2,1280,128]{3,2,1,0:T(8,128)(2,1)S(1)} %pad_maximum_fusion.1.refs_1_, bf16[2,2,1280,128]{3,2,1,0:T(8,128)(2,1)S(1)} %pad_maximum_fusion.2.refs_2_, bf16[2,2,1280,128]{3,2,1,0:T(8,128)(2,1)S(1)} %collective-permute-done.19.refs_3_, ...), custom_call_target="tpu_custom_call" | custom-call | tf_op jit(solution)/shard_map/exchange/pallas_call | solution.py:304
  (28 shorter events, 0.3 us)
Async XLA Ops:
  0.0 43.7 %copy-start = (s32[16384]{0:T(1024)S(1)}, s32[16384]{0:T(1024)}, u32[]{:S(2)}) copy-start(s32[16384]{0:T(1024)} %param.8) | copy-start | bytes 196612
  43.7 4.3 %copy-start.1 = (bf16[256,32,128]{2,1,0:T(8,128)(2,1)}, bf16[256,32,128]{2,1,0:T(8,128)(2,1)S(1)}, u32[]{:S(2)}) copy-start(bf16[256,32,128]{2,1,0:T(8,128)(2,1)S(1)} %all_to_all.5.own_ref) | copy-start | bytes 6291460
  43.7 4.3 %collective-permute-start = (bf16[256,32,128]{2,1,0:T(8,128)(2,1)S(1)}, bf16[256,32,128]{2,1,0:T(8,128)(2,1)}, u32[]{:S(2)}, u32[]{:S(2)}) collective-permute-start(bf16[256,32,128]{2,1,0:T(8,128)(2,1)S(1)} %all_to_all.5.own_ref), channel_id=1, source_target_pairs={{0,1},{1,0},{2,3},{3,2},{4,5},{5,4},{6,7},{7,6},{8,9},{9,8},{10,11... | collective-permute-start | bytes 6291464 | tf_op jit(solution)/shard_map/ppermute | solution.py:356
  53.7 25.2 %copy-start.2 = (bf16[80,32,128]{2,1,0:T(8,128)(2,1)S(1)}, bf16[80,32,128]{2,1,0:T(8,128)(2,1)}, u32[]{:S(2)}) copy-start(bf16[80,32,128]{2,1,0:T(8,128)(2,1)} %get-tuple-element.18) | copy-start | bytes 1966084
  53.7 12.0 %collective-permute-start.1 = (bf16[40,32,128]{2,1,0:T(8,128)(2,1)}, bf16[40,32,128]{2,1,0:T(8,128)(2,1)S(1)}, u32[]{:S(2)}, u32[]{:S(2)}) collective-permute-start(bf16[40,32,128]{2,1,0:T(8,128)(2,1)} %get-tuple-element.20), channel_id=1, source_target_pairs={{0,2},{2,4},{4,6},{6,0},{1,3},{3,5},{5,7},{7,1},{8,10},{10,12},{12... | collective-permute-start | bytes 983048 | tf_op jit(solution)/shard_map/ppermute | solution.py:155
  55.3 11.9 %collective-permute-start.5 = (bf16[40,32,128]{2,1,0:T(8,128)(2,1)}, bf16[40,32,128]{2,1,0:T(8,128)(2,1)S(1)}, u32[]{:S(2)}, u32[]{:S(2)}) collective-permute-start(bf16[40,32,128]{2,1,0:T(8,128)(2,1)} %get-tuple-element.24), channel_id=1, source_target_pairs={{0,6},{2,0},{4,2},{6,4},{1,7},{3,1},{5,3},{7,5},{8,14},{10,8},{12,... | collective-permute-start | bytes 983048 | tf_op jit(solution)/shard_map/ppermute | solution.py:155
  56.9 15.8 %collective-permute-start.3 = (bf16[40,32,128]{2,1,0:T(8,128)(2,1)}, bf16[40,32,128]{2,1,0:T(8,128)(2,1)S(1)}, u32[]{:S(2)}, u32[]{:S(2)}) collective-permute-start(bf16[40,32,128]{2,1,0:T(8,128)(2,1)} %get-tuple-element.21), channel_id=1, source_target_pairs={{0,2},{2,4},{4,6},{6,0},{1,3},{3,5},{5,7},{7,1},{8,10},{10,12},{12... | collective-permute-start | bytes 983048 | tf_op jit(solution)/shard_map/ppermute | solution.py:155
  57.3 15.8 %collective-permute-start.4 = (bf16[40,32,128]{2,1,0:T(8,128)(2,1)}, bf16[40,32,128]{2,1,0:T(8,128)(2,1)S(1)}, u32[]{:S(2)}, u32[]{:S(2)}) collective-permute-start(bf16[40,32,128]{2,1,0:T(8,128)(2,1)} %get-tuple-element.22), channel_id=1, source_target_pairs={{0,6},{2,0},{4,2},{6,4},{1,7},{3,1},{5,3},{7,5},{8,14},{10,8},{12,... | collective-permute-start | bytes 983048 | tf_op jit(solution)/shard_map/ppermute | solution.py:155
  66.7 12.2 %collective-permute-start.2 = (bf16[40,32,128]{2,1,0:T(8,128)(2,1)S(1)}, bf16[40,32,128]{2,1,0:T(8,128)(2,1)S(1)}, u32[]{:S(2)}, u32[]{:S(2)}) collective-permute-start(bf16[40,32,128]{2,1,0:T(8,128)(2,1)S(1)} %add_convert_fusion.2), channel_id=1, source_target_pairs={{0,2},{2,4},{4,6},{6,0},{1,3},{3,5},{5,7},{7,1},{8,10},{10,12},{12... | collective-permute-start | bytes 983048 | tf_op jit(solution)/shard_map/ppermute | solution.py:155
  68.3 10.6 %collective-permute-start.6 = (bf16[40,32,128]{2,1,0:T(8,128)(2,1)S(1)}, bf16[40,32,128]{2,1,0:T(8,128)(2,1)S(1)}, u32[]{:S(2)}, u32[]{:S(2)}) collective-permute-start(bf16[40,32,128]{2,1,0:T(8,128)(2,1)S(1)} %add_convert_fusion.1), channel_id=1, source_target_pairs={{0,6},{2,0},{4,2},{6,4},{1,7},{3,1},{5,3},{7,5},{8,14},{10,8},{12,... | collective-permute-start | bytes 983048 | tf_op jit(solution)/shard_map/ppermute | solution.py:155
  79.2 13.9 %collective-permute-start.8 = (bf16[2560,128]{1,0:T(8,128)(2,1)S(1)}, bf16[2560,128]{1,0:T(8,128)(2,1)S(1)}, u32[]{:S(2)}, u32[]{:S(2)}) collective-permute-start(bf16[2560,128]{1,0:T(8,128)(2,1)S(1)} %bitcast.109), channel_id=1, source_target_pairs={{0,96},{1,25},{2,98},{3,27},{4,100},{5,29},{6,102},{7,31},{8,104},... | collective-permute-start | bytes 1966088 | tf_op jit(solution)/shard_map/ppermute | solution.py:184
  80.0 13.1 %collective-permute-start.7 = (bf16[2560,128]{1,0:T(8,128)(2,1)S(1)}, bf16[2560,128]{1,0:T(8,128)(2,1)S(1)}, u32[]{:S(2)}, u32[]{:S(2)}) collective-permute-start(bf16[2560,128]{1,0:T(8,128)(2,1)S(1)} %bitcast.110), channel_id=1, source_target_pairs={{0,32},{1,9},{2,34},{3,11},{4,36},{5,13},{6,38},{7,15},{8,40},{9,1... | collective-permute-start | bytes 1966088 | tf_op jit(solution)/shard_map/ppermute | solution.py:184
  81.3 4.3 %collective-permute-start.9 = (bf16[1280,128]{1,0:T(8,128)(2,1)S(1)}, bf16[1280,128]{1,0:T(8,128)(2,1)S(1)}, u32[]{:S(2)}, u32[]{:S(2)}) collective-permute-start(bf16[1280,128]{1,0:T(8,128)(2,1)S(1)} %bitcast.122), channel_id=1, source_target_pairs={{0,0},{1,5},{2,2},{3,7},{4,4},{5,1},{6,6},{7,3},{8,8},{9,13},{10,1... | collective-permute-start | bytes 983048 | tf_op jit(solution)/shard_map/ppermute | solution.py:208
  82.0 11.1 %collective-permute-start.10 = (bf16[1280,128]{1,0:T(8,128)(2,1)S(1)}, bf16[1280,128]{1,0:T(8,128)(2,1)S(1)}, u32[]{:S(2)}, u32[]{:S(2)}) collective-permute-start(bf16[1280,128]{1,0:T(8,128)(2,1)S(1)} %bitcast.121), channel_id=1, source_target_pairs={{0,2},{1,7},{2,4},{3,1},{4,6},{5,3},{6,0},{7,5},{8,10},{9,15},{10,... | collective-permute-start | bytes 983048 | tf_op jit(solution)/shard_map/ppermute | solution.py:208
  93.1 8.4 %collective-permute-start.12 = (bf16[1280,128]{1,0:T(8,128)(2,1)S(1)}, bf16[1280,128]{1,0:T(8,128)(2,1)S(1)}, u32[]{:S(2)}, u32[]{:S(2)}) collective-permute-start(bf16[1280,128]{1,0:T(8,128)(2,1)S(1)} %slice.31), channel_id=1, source_target_pairs={{0,32},{1,9},{2,34},{3,11},{4,36},{5,13},{6,38},{7,15},{8,40},{9,1... | collective-permute-start | bytes 983048 | tf_op jit(solution)/shard_map/ppermute | solution.py:184
  96.3 8.9 %collective-permute-start.11 = (bf16[1280,128]{1,0:T(8,128)(2,1)S(1)}, bf16[1280,128]{1,0:T(8,128)(2,1)S(1)}, u32[]{:S(2)}, u32[]{:S(2)}) collective-permute-start(bf16[1280,128]{1,0:T(8,128)(2,1)S(1)} %slice.30), channel_id=1, source_target_pairs={{0,96},{1,25},{2,98},{3,27},{4,100},{5,29},{6,102},{7,31},{8,104},... | collective-permute-start | bytes 983048 | tf_op jit(solution)/shard_map/ppermute | solution.py:184
  96.5 8.9 %collective-permute-start.13 = (bf16[1280,128]{1,0:T(8,128)(2,1)S(1)}, bf16[1280,128]{1,0:T(8,128)(2,1)S(1)}, u32[]{:S(2)}, u32[]{:S(2)}) collective-permute-start(bf16[1280,128]{1,0:T(8,128)(2,1)S(1)} %collective-permute-done.9), channel_id=1, source_target_pairs={{0,0},{5,20},{2,34},{7,54},{4,68},{1,80},{6,102},{3,114},{8,1},{13... | collective-permute-start | bytes 983048 | tf_op jit(solution)/shard_map/ppermute | solution.py:212
  97.1 12.9 %collective-permute-start.14 = (bf16[1280,128]{1,0:T(8,128)(2,1)S(1)}, bf16[1280,128]{1,0:T(8,128)(2,1)S(1)}, u32[]{:S(2)}, u32[]{:S(2)}) collective-permute-start(bf16[1280,128]{1,0:T(8,128)(2,1)S(1)} %collective-permute-done.10), channel_id=1, source_target_pairs={{2,10},{7,30},{4,44},{1,56},{6,78},{3,90},{0,104},{5,124},{10,11},... | collective-permute-start | bytes 983048 | tf_op jit(solution)/shard_map/ppermute | solution.py:212
  110.1 20.7 %collective-permute-start.16 = (bf16[2,1280,128]{2,1,0:T(8,128)(2,1)S(1)}, bf16[2,1280,128]{2,1,0:T(8,128)(2,1)S(1)}, u32[]{:S(2)}, u32[]{:S(2)}) collective-permute-start(bf16[2,1280,128]{2,1,0:T(8,128)(2,1)S(1)} %pad_maximum_fusion.4), channel_id=1, source_target_pairs={{0,6},{2,0},{4,2},{6,4},{1,7},{3,1},{5,3},{7,5},{8,14},{10,8},{12,... | collective-permute-start | bytes 1966088 | tf_op jit(solution)/shard_map/ppermute | solution.py:155
  119.7 14.9 %collective-permute-start.15 = (bf16[2,1280,128]{2,1,0:T(8,128)(2,1)S(1)}, bf16[2,1280,128]{2,1,0:T(8,128)(2,1)S(1)}, u32[]{:S(2)}, u32[]{:S(2)}) collective-permute-start(bf16[2,1280,128]{2,1,0:T(8,128)(2,1)S(1)} %pad_maximum_fusion.4), channel_id=1, source_target_pairs={{0,2},{2,4},{4,6},{6,0},{1,3},{3,5},{5,7},{7,1},{8,10},{10,12},{12... | collective-permute-start | bytes 1966088 | tf_op jit(solution)/shard_map/ppermute | solution.py:155
  119.8 24.6 %collective-permute-start.23 = (bf16[2,2560,128]{2,1,0:T(8,128)(2,1)S(1)}, bf16[2,2560,128]{2,1,0:T(8,128)(2,1)S(1)}, u32[]{:S(2)}, u32[]{:S(2)}) collective-permute-start(bf16[2,2560,128]{2,1,0:T(8,128)(2,1)S(1)} %pad_maximum_fusion.3.refs_5_), channel_id=1, source_target_pairs={{0,24},{1,97},{2,26},{3,99},{4,28},{5,101},{6,30},{7,103},{8,0},{9... | collective-permute-start | bytes 3932168 | tf_op jit(solution)/shard_map/ppermute | solution.py:184
  119.9 25.2 %collective-permute-start.21 = (bf16[2,2560,128]{2,1,0:T(8,128)(2,1)S(1)}, bf16[2,2560,128]{2,1,0:T(8,128)(2,1)S(1)}, u32[]{:S(2)}, u32[]{:S(2)}) collective-permute-start(bf16[2,2560,128]{2,1,0:T(8,128)(2,1)S(1)} %pad_maximum_fusion.3.refs_5_), channel_id=1, source_target_pairs={{0,8},{1,33},{2,10},{3,35},{4,12},{5,37},{6,14},{7,39},{8,16},{9,4... | collective-permute-start | bytes 3932168 | tf_op jit(solution)/shard_map/ppermute | solution.py:184
  121.9 30.9 %collective-permute-start.22 = (bf16[2,2560,128]{2,1,0:T(8,128)(2,1)S(1)}, bf16[2,2560,128]{2,1,0:T(8,128)(2,1)S(1)}, u32[]{:S(2)}, u32[]{:S(2)}) collective-permute-start(bf16[2,2560,128]{2,1,0:T(8,128)(2,1)S(1)} %pad_maximum_fusion.refs_6_), channel_id=1, source_target_pairs={{0,8},{1,33},{2,10},{3,35},{4,12},{5,37},{6,14},{7,39},{8,16},{9,4... | collective-permute-start | bytes 3932168 | tf_op jit(solution)/shard_map/ppermute | solution.py:184
  130.8 8.4 %collective-permute-start.17 = (bf16[1280,128]{1,0:T(8,128)(2,1)S(1)}, bf16[1280,128]{1,0:T(8,128)(2,1)S(1)}, u32[]{:S(2)}, u32[]{:S(2)}) collective-permute-start(bf16[1280,128]{1,0:T(8,128)(2,1)S(1)} %slice_bitcast_fusion.1), channel_id=1, source_target_pairs={{0,6},{2,0},{4,2},{6,4},{1,7},{3,1},{5,3},{7,5},{8,14},{10,8},{12,... | collective-permute-start | bytes 983048 | tf_op jit(solution)/shard_map/ppermute | solution.py:155
  134.6 9.6 %collective-permute-start.18 = (bf16[1280,128]{1,0:T(8,128)(2,1)S(1)}, bf16[1280,128]{1,0:T(8,128)(2,1)S(1)}, u32[]{:S(2)}, u32[]{:S(2)}) collective-permute-start(bf16[1280,128]{1,0:T(8,128)(2,1)S(1)} %slice_bitcast_fusion), channel_id=1, source_target_pairs={{0,2},{2,4},{4,6},{6,0},{1,3},{3,5},{5,7},{7,1},{8,10},{10,12},{12... | collective-permute-start | bytes 983048 | tf_op jit(solution)/shard_map/ppermute | solution.py:155
  139.2 20.2 %collective-permute-start.24 = (bf16[2,2560,128]{2,1,0:T(8,128)(2,1)S(1)}, bf16[2,2560,128]{2,1,0:T(8,128)(2,1)S(1)}, u32[]{:S(2)}, u32[]{:S(2)}) collective-permute-start(bf16[2,2560,128]{2,1,0:T(8,128)(2,1)S(1)} %pad_maximum_fusion.refs_6_), channel_id=1, source_target_pairs={{0,24},{1,97},{2,26},{3,99},{4,28},{5,101},{6,30},{7,103},{8,0},{9... | collective-permute-start | bytes 3932168 | tf_op jit(solution)/shard_map/ppermute | solution.py:184
  144.3 15.1 %collective-permute-start.19 = (bf16[2,2,1280,128]{3,2,1,0:T(8,128)(2,1)S(1)}, bf16[2,2,1280,128]{3,2,1,0:T(8,128)(2,1)S(1)}, u32[]{:S(2)}, u32[]{:S(2)}) collective-permute-start(bf16[2,2,1280,128]{3,2,1,0:T(8,128)(2,1)S(1)} %pad_maximum_fusion.1.refs_1_), channel_id=1, source_target_pairs={{0,1},{1,0},{2,3},{3,2},{4,5},{5,4},{6,7},{7,6},{8,9},{9,8},{10,11... | collective-permute-start | bytes 3932168 | tf_op jit(solution)/shard_map/ppermute | solution.py:224
  144.5 14.9 %collective-permute-start.20 = (bf16[2,2,1280,128]{3,2,1,0:T(8,128)(2,1)S(1)}, bf16[2,2,1280,128]{3,2,1,0:T(8,128)(2,1)S(1)}, u32[]{:S(2)}, u32[]{:S(2)}) collective-permute-start(bf16[2,2,1280,128]{3,2,1,0:T(8,128)(2,1)S(1)} %pad_maximum_fusion.2.refs_2_), channel_id=1, source_target_pairs={{0,1},{1,0},{2,3},{3,2},{4,5},{5,4},{6,7},{7,6},{8,9},{9,8},{10,11... | collective-permute-start | bytes 3932168 | tf_op jit(solution)/shard_map/ppermute | solution.py:224
  145.1 28.4 %collective-permute-start.25 = (bf16[2,2560,128]{2,1,0:T(8,128)(2,1)S(1)}, bf16[2,2560,128]{2,1,0:T(8,128)(2,1)S(1)}, u32[]{:S(2)}, u32[]{:S(2)}) collective-permute-start(bf16[2,2560,128]{2,1,0:T(8,128)(2,1)S(1)} %collective-permute-done.23.refs_9_), channel_id=1, source_target_pairs={{0,24},{1,97},{2,26},{3,99},{4,28},{5,101},{6,30},{7,103},{8,0},{9... | collective-permute-start | bytes 3932168 | tf_op jit(solution)/shard_map/ppermute | solution.py:184
  152.8 20.6 %collective-permute-start.26 = (bf16[2,2560,128]{2,1,0:T(8,128)(2,1)S(1)}, bf16[2,2560,128]{2,1,0:T(8,128)(2,1)S(1)}, u32[]{:S(2)}, u32[]{:S(2)}) collective-permute-start(bf16[2,2560,128]{2,1,0:T(8,128)(2,1)S(1)} %collective-permute-done.22.refs_8_), channel_id=1, source_target_pairs={{0,8},{1,33},{2,10},{3,35},{4,12},{5,37},{6,14},{7,39},{8,16},{9,4... | collective-permute-start | bytes 3932168 | tf_op jit(solution)/shard_map/ppermute | solution.py:184

commit v4 on v3

--- a/solution.py
+++ b/solution.py
@@ -12,9 +12,10 @@
 TILE_STEP = 32
 COL_STEP = 256
 COL_LOAD = 512
-OUT_PARTS = 4
+ROW_STEP = 256
 SWAP = [(0, 1), (1, 0)]
 VMEM_LIMIT = 56 * 1024 * 1024
+SUM_LIMIT = 24 * 1024 * 1024
 EXCHANGE_LIMIT = 36 * 1024 * 1024
 
 
@@ -92,15 +93,22 @@
 
 
 def sum_kernel(count_ref, list_ref, own_ref, other_ref, *refs):
-    out_refs, total_ref = refs[:-1], refs[-1]
+    out_refs, (total_ref, slots, sem) = refs[:-3], refs[-3:]
+    copies = [
+        pltpu.make_async_copy(slots_ref, slots.at[side], sem.at[side])
+        for side, slots_ref in enumerate((own_ref, other_ref))
+    ]
+    for copy in copies:
+        copy.start()
     total_ref[...] = jnp.zeros_like(total_ref)
-    for side, slots_ref in enumerate((own_ref, other_ref)):
-
-        def add(index, carry, side=side, slots_ref=slots_ref):
+    for side, copy in enumerate(copies):
+        copy.wait()
+
+        def add(index, carry, side=side):
             entry = list_ref[side, index]
             slot = lax.shift_right_logical(entry, 9)
             place = lax.bitwise_and(entry, 511)
-            total_ref[place] += slots_ref[slot].astype(jnp.float32)
+            total_ref[place] += slots[side, slot].astype(jnp.float32)
             return carry
 
         lax.fori_loop(0, count_ref[side], add, 0)
@@ -120,13 +128,17 @@
         in_specs=[
             pl.BlockSpec(memory_space=pltpu.SMEM),
             pl.BlockSpec(memory_space=pltpu.SMEM),
-            pl.BlockSpec(memory_space=pltpu.VMEM),
-            pl.BlockSpec(memory_space=pltpu.VMEM),
+            pl.BlockSpec(memory_space=pl.ANY),
+            pl.BlockSpec(memory_space=pl.ANY),
         ],
         out_specs=[pl.BlockSpec(memory_space=pltpu.VMEM)] * len(sizes),
         out_shape=[jax.ShapeDtypeStruct((size,) + tile_shape, jnp.bfloat16) for size in sizes],
-        scratch_shapes=[pltpu.VMEM((places,) + tile_shape, jnp.float32)],
-        compiler_params=pltpu.CompilerParams(vmem_limit_bytes=VMEM_LIMIT),
+        scratch_shapes=[
+            pltpu.VMEM((places,) + tile_shape, jnp.float32),
+            pltpu.VMEM((2,) + own.shape, jnp.bfloat16),
+            pltpu.SemaphoreType.DMA((2,)),
+        ],
+        compiler_params=pltpu.CompilerParams(vmem_limit_bytes=SUM_LIMIT),
         name="sum_slots",
     )(counts, entries, own, other)
     return outs
@@ -227,7 +239,7 @@
 
 def exchange_kernel(at_ref, *refs, factor):
     row_refs, col_refs = refs[:4], refs[4:12]
-    out_ref, row_data, col_data, out_data, row_sem, col_sem, out_sem = refs[12:]
+    out_ref, row_data, col_data, columns, out_data, row_sem, col_sem, out_sem = refs[12:]
     width = col_data.shape[-1]
     rows, col_count = out_data.shape
     z_place, y_place, x_place, core = (at_ref[i] for i in range(4))
@@ -271,29 +283,36 @@
     for copy in row_copies:
         copy.wait()
 
-    out_copies = []
-    out_rows = rows // OUT_PARTS
-    for first in range(0, col_count, COL_STEP):
+    row_blocks = rows // ROW_STEP
+
+    def out_copy(first, block, index):
+        place = pl.ds(pl.multiple_of(block * ROW_STEP, ROW_STEP), ROW_STEP), pl.ds(first, COL_STEP)
+        return pltpu.make_async_copy(out_data.at[place], out_ref.at[place], out_sem.at[index, block])
+
+    for index, first in enumerate(range(0, col_count, COL_STEP)):
         if first % COL_LOAD == 0:
             for copy in col_copies[first // COL_LOAD]:
                 copy.wait()
         part = pl.ds(first, COL_STEP)
-        columns = jnp.concatenate([col_data[group, part] for group in range(col_data.shape[0])], axis=1)
-        out_data[:, part] = (
-            lax.dot_general(
-                row_data[...], columns, (((1,), (1,)), ((), ())), preferred_element_type=jnp.float32
+        for group in range(col_data.shape[0]):
+            columns[:, pl.ds(group * width, width)] = col_data[group, part]
+
+        def multiply(block, carry, index=index, first=first, part=part):
+            place = pl.ds(pl.multiple_of(block * ROW_STEP, ROW_STEP), ROW_STEP)
+            out_data[place, part] = (
+                lax.dot_general(
+                    row_data[place], columns[...], (((1,), (1,)), ((), ())), preferred_element_type=jnp.float32
+                )
+                * factor
             )
-            * factor
-        )
-        for index in range(OUT_PARTS):
-            block = pl.ds(index * out_rows, out_rows)
-            copy = pltpu.make_async_copy(
-                out_data.at[block, part], out_ref.at[block, part], out_sem.at[len(out_copies)]
-            )
-            copy.start()
-            out_copies.append(copy)
-    for copy in out_copies:
-        copy.wait()
+            out_copy(first, block, index).start()
+            return carry
+
+        lax.fori_loop(0, row_blocks, multiply, 0)
+
+    for index, first in enumerate(range(0, col_count, COL_STEP)):
+        for block in range(row_blocks):
+            out_copy(first, block, index).wait()
 
 
 def exchange_block(at, row_parts, pieces):
@@ -310,10 +329,11 @@
         scratch_shapes=[
             pltpu.VMEM((rows, depth), jnp.bfloat16),
             pltpu.VMEM((groups, col_count, width), jnp.bfloat16),
+            pltpu.VMEM((COL_STEP, depth), jnp.bfloat16),
             pltpu.VMEM((rows, col_count), jnp.float32),
             pltpu.SemaphoreType.DMA((groups,)),
             pltpu.SemaphoreType.DMA((col_count // COL_LOAD, len(pieces))),
-            pltpu.SemaphoreType.DMA((col_count // COL_STEP * OUT_PARTS,)),
+            pltpu.SemaphoreType.DMA((col_count // COL_STEP, rows // ROW_STEP)),
         ],
         compiler_params=pltpu.CompilerParams(vmem_limit_bytes=EXCHANGE_LIMIT),
         name="exchange",

time: 195 us -> 203 us (1.041)
  Pallas kernels: 33.3 us -> 41.6 us
  waiting for transfers between devices: 70.3 us -> 73.5 us
  other arithmetic: 5.31 us -> 2.21 us
    pallas_call x1, Pallas kernels: 20.5 us -> 31.1 us  [exchange_block(): pl.pallas_call(lambda *refs: exchange_kernel(*refs, factor=1.0 / depth),...]
    pallas_call x1, Pallas kernels: 5.65 us -> 3.33 us  [sum_slots(): pl.pallas_call(sum_kernel, in_specs=[pl.BlockSpec(memory_space=pltpu.SMEM...]
  transfers between devices with their start and end apart: 27 -> 27, of which waited for: 14 -> 15; matrix products, arithmetic and copies ran while one was open for 3% -> 1% of each run, Pallas kernels for 0% -> 0%
where the time goes in v4:
time: 203 us; the launch traced here: 202 us
  waiting for transfers between devices  73.5 us (36%)
  starting transfers between devices  47 us (23%)
  Pallas kernels  41.6 us (20%)
  blocking collectives  36.5 us (18%)
  other arithmetic  2.21 us (1%)
    all_to_all x1, blocking collectives, shards(): lax.all_to_all(outgoing, AUX_AXES, split_axis=0, concat_axis=0, tiled=True)  36.5 us
    pallas_call x1, Pallas kernels, exchange_block(): pl.pallas_call(lambda *refs: exchange_kernel(*refs, factor=1.0 / depth),...  31.1 us
    ppermute x10, waiting for transfers between devices, shift_turned(): return lax.ppermute(value, ALL_AXES, pairs)  30.4 us
    ppermute x10, waiting for transfers between devices, shift(): return lax.ppermute(value, axis, [(i, (i + by) % 4) for i in range(4)])  28.3 us
    ppermute x10, starting transfers between devices, shift(): return lax.ppermute(value, axis, [(i, (i + by) % 4) for i in range(4)])  23 us
    ppermute x10, starting transfers between devices, shift_turned(): return lax.ppermute(value, ALL_AXES, pairs)  16 us
    ppermute x2, waiting for transfers between devices, gather_both(): lax.ppermute(jnp.where(turned, halves[1 - t], halves[t]), ALL_AXES, pairs...  7.56 us
    pallas_call x1, Pallas kernels, half_slots(): pl.pallas_call(half_kernel, grid_spec=pltpu.PrefetchScalarGridSpec(num_sc...  7.18 us
  transfers between devices with their start and end apart: 27, of which 15 were waited for; matrix products, arithmetic and copies ran while one was open for 1% of the time, Pallas kernels for 0%

profile of v4, /device:TPU:0, one launch (start us, length us, event | category | flops | bytes accessed | tf_op | source)
XLA Modules:
  0.0 202.2 jit_solution(2530043225945537779)
XLA Ops:
  0.0 7.2 %half_transform.1 = bf16[256,32,128]{2,1,0:T(8,128)(2,1)} custom-call(s32[1]{0:T(128)} %bitcast.20.self_ref, s32[128,128]{1,0:T(8,128)} %bitcast.123, s32[128,128]{1,0:T(8,128)} %bitcast.125, bf16[128,4,32,128]{3,2,1,0:T(8,128)(2,1)} %tiles_ref.1, bf16[32,20480]{1,0:T(8,128)(2,1)} %orbital_ref.1, s32[32,160]{1,0:T(8,128)} %support_ref.1), custom_call_target="tpu_custom_call" | custom-call | tf_op jit(solution)/shard_map/half_transform/pallas_call | solution.py:71
  7.2 36.5 %all_to_all.5.own_ref = bf16[256,32,128]{2,1,0:T(8,128)(2,1)S(1)} all-to-all(bf16[256,32,128]{2,1,0:T(8,128)(2,1)} %half_transform.1), channel_id=1, replica_groups=mesh['z'=4,'y'=4,'x'=4,'core'=2] {'z','y'}, dimensions={0} | all-to-all | bytes 4194304 | tf_op jit(solution)/shard_map/all_to_all | solution.py:367
  43.7 0.0 collective-permute-start
  43.7 0.7 constant_dynamic-slice_fusion.1
  44.5 0.2 convert_reduce_fusion
  44.7 0.2 reduce_window_sum.11
  44.9 0.1 convolution_convert_fusion
  45.0 0.1 fusion.20
  45.1 0.5 select_reduce_fusion.list_ref
  45.6 2.4 %collective-permute-done.other_ref = bf16[256,32,128]{2,1,0:T(8,128)(2,1)} collective-permute-done((bf16[256,32,128]{2,1,0:T(8,128)(2,1)S(1)}, bf16[256,32,128]{2,1,0:T(8,128)(2,1)}, u32[]{:S(2)}, u32[]{:S(2)}) %collective-permute-start) | collective-permute-done | bytes 2097184 | tf_op jit(solution)/shard_map/ppermute | solution.py:376
  48.0 3.3 %sum_slots.1 = (bf16[80,32,128]{2,1,0:T(8,128)(2,1)S(1)}, bf16[40,32,128]{2,1,0:T(8,128)(2,1)S(1)}, bf16[40,32,128]{2,1,0:T(8,128)(2,1)S(1)}, bf16[40,32,128]{2,...) custom-call(s32[2]{0:T(128)S(1)} %get-tuple-element.32.count_ref, ...), custom_call_target="tpu_custom_call" | custom-call | tf_op jit(solution)/shard_map/sum_slots/pallas_call | solution.py:126
  51.4 1.6 collective-permute-start.1
  53.0 1.7 collective-permute-start.5
  54.7 0.3 collective-permute-start.3
  55.0 2.9 %collective-permute-start.4 = (bf16[40,32,128]{2,1,0:T(8,128)(2,1)S(1)}, bf16[40,32,128]{2,1,0:T(8,128)(2,1)S(1)}, u32[]{:S(2)}, u32[]{:S(2)}) collective-permute-start(bf16[40,32,128]{2,1,0:T(8,128)(2,1)S(1)} %get-tuple-element.22), channel_id=1, source_target_pairs={{0,6},{2,0},{4,2},{6,4},{1,7},{3,1},{5,3},{7,5},{8,14},{10,8},{12,... | collective-permute-start | bytes 983048 | tf_op jit(solution)/shard_map/ppermute | solution.py:167
  57.9 5.3 %collective-permute-done.1 = bf16[40,32,128]{2,1,0:T(8,128)(2,1)S(1)} collective-permute-done((bf16[40,32,128]{2,1,0:T(8,128)(2,1)S(1)}, bf16[40,32,128]{2,1,0:T(8,128)(2,1)S(1)}, u32[]{:S(2)}, u32[]{:S(2)}) %collective-permute-start.1) | collective-permute-done | bytes 327712 | tf_op jit(solution)/shard_map/ppermute | solution.py:167
  63.2 0.1 add_convert_fusion.2
  63.3 0.3 collective-permute-start.2
  63.7 0.0 collective-permute-done.5
  63.7 0.1 add_convert_fusion.1
  63.8 3.0 %collective-permute-start.6 = (bf16[40,32,128]{2,1,0:T(8,128)(2,1)S(1)}, bf16[40,32,128]{2,1,0:T(8,128)(2,1)S(1)}, u32[]{:S(2)}, u32[]{:S(2)}) collective-permute-start(bf16[40,32,128]{2,1,0:T(8,128)(2,1)S(1)} %add_convert_fusion.1), channel_id=1, source_target_pairs={{0,6},{2,0},{4,2},{6,4},{1,7},{3,1},{5,3},{7,5},{8,14},{10,8},{12,... | collective-permute-start | bytes 983048 | tf_op jit(solution)/shard_map/ppermute | solution.py:167
  66.8 3.5 %collective-permute-done.3 = bf16[40,32,128]{2,1,0:T(8,128)(2,1)S(1)} collective-permute-done((bf16[40,32,128]{2,1,0:T(8,128)(2,1)S(1)}, bf16[40,32,128]{2,1,0:T(8,128)(2,1)S(1)}, u32[]{:S(2)}, u32[]{:S(2)}) %collective-permute-start.3) | collective-permute-done | bytes 327712 | tf_op jit(solution)/shard_map/ppermute | solution.py:167
  70.2 0.3 collective-permute-done.4
  70.6 5.8 %collective-permute-done.2 = bf16[40,32,128]{2,1,0:T(8,128)(2,1)S(1)} collective-permute-done((bf16[40,32,128]{2,1,0:T(8,128)(2,1)S(1)}, bf16[40,32,128]{2,1,0:T(8,128)(2,1)S(1)}, u32[]{:S(2)}, u32[]{:S(2)}) %collective-permute-start.2) | collective-permute-done | bytes 327712 | tf_op jit(solution)/shard_map/ppermute | solution.py:167
  76.3 0.2 collective-permute-done.6
  76.5 0.3 add_convert_fusion
  76.8 0.7 collective-permute-start.8
  77.5 1.4 collective-permute-start.7
  79.0 0.7 collective-permute-start.9
  79.6 3.3 %collective-permute-start.10 = (bf16[1280,128]{1,0:T(8,128)(2,1)S(1)}, bf16[1280,128]{1,0:T(8,128)(2,1)S(1)}, u32[]{:S(2)}, u32[]{:S(2)}) collective-permute-start(bf16[1280,128]{1,0:T(8,128)(2,1)S(1)} %bitcast.121), channel_id=1, source_target_pairs={{0,2},{1,7},{2,4},{3,1},{4,6},{5,3},{6,0},{7,5},{8,10},{9,15},{10,... | collective-permute-start | bytes 983048 | tf_op jit(solution)/shard_map/ppermute | solution.py:220
  82.9 0.0 collective-permute-done.9
  82.9 7.6 %collective-permute-done.10 = bf16[1280,128]{1,0:T(8,128)(2,1)S(1)} collective-permute-done((bf16[1280,128]{1,0:T(8,128)(2,1)S(1)}, bf16[1280,128]{1,0:T(8,128)(2,1)S(1)}, u32[]{:S(2)}, u32[]{:S(2)}) %collective-permute-start.10) | collective-permute-done | bytes 327712 | tf_op jit(solution)/shard_map/ppermute | solution.py:220
  90.5 0.0 collective-permute-done.8
  90.5 3.2 %collective-permute-start.12 = (bf16[1280,128]{1,0:T(8,128)(2,1)S(1)}, bf16[1280,128]{1,0:T(8,128)(2,1)S(1)}, u32[]{:S(2)}, u32[]{:S(2)}) collective-permute-start(bf16[1280,128]{1,0:T(8,128)(2,1)S(1)} %slice.31), channel_id=1, source_target_pairs={{0,32},{1,9},{2,34},{3,11},{4,36},{5,13},{6,38},{7,15},{8,40},{9,1... | collective-permute-start | bytes 983048 | tf_op jit(solution)/shard_map/ppermute | solution.py:196
  93.7 0.1 collective-permute-start.11
  93.8 0.7 collective-permute-start.13
  94.5 2.8 %collective-permute-start.14 = (bf16[1280,128]{1,0:T(8,128)(2,1)S(1)}, bf16[1280,128]{1,0:T(8,128)(2,1)S(1)}, u32[]{:S(2)}, u32[]{:S(2)}) collective-permute-start(bf16[1280,128]{1,0:T(8,128)(2,1)S(1)} %collective-permute-done.10), channel_id=1, source_target_pairs={{2,10},{7,30},{4,44},{1,56},{6,78},{3,90},{0,104},{5,124},{10,11},... | collective-permute-start | bytes 983048 | tf_op jit(solution)/shard_map/ppermute | solution.py:224
  97.3 1.6 collective-permute-done.12
  98.9 3.8 %collective-permute-done.11 = bf16[1280,128]{1,0:T(8,128)(2,1)S(1)} collective-permute-done((bf16[1280,128]{1,0:T(8,128)(2,1)S(1)}, bf16[1280,128]{1,0:T(8,128)(2,1)S(1)}, u32[]{:S(2)}, u32[]{:S(2)}) %collective-permute-start.11) | collective-permute-done | bytes 327712 | tf_op jit(solution)/shard_map/ppermute | solution.py:196
  102.7 0.1 pad_maximum_fusion.refs_6_
  102.9 4.8 %collective-permute-done.14 = bf16[1280,128]{1,0:T(8,128)(2,1)S(1)} collective-permute-done((bf16[1280,128]{1,0:T(8,128)(2,1)S(1)}, bf16[1280,128]{1,0:T(8,128)(2,1)S(1)}, u32[]{:S(2)}, u32[]{:S(2)}) %collective-permute-start.14) | collective-permute-done | bytes 327712 | tf_op jit(solution)/shard_map/ppermute | solution.py:224
  107.6 0.1 pad_maximum_fusion.4
  107.7 9.3 %collective-permute-start.16 = (bf16[2,1280,128]{2,1,0:T(8,128)(2,1)S(1)}, bf16[2,1280,128]{2,1,0:T(8,128)(2,1)S(1)}, u32[]{:S(2)}, u32[]{:S(2)}) collective-permute-start(bf16[2,1280,128]{2,1,0:T(8,128)(2,1)S(1)} %pad_maximum_fusion.4), channel_id=1, source_target_pairs={{0,6},{2,0},{4,2},{6,4},{1,7},{3,1},{5,3},{7,5},{8,14},{10,8},{12,... | collective-permute-start | bytes 1966088 | tf_op jit(solution)/shard_map/ppermute | solution.py:167
  117.0 0.1 pad_maximum_fusion.3.refs_5_
  117.1 0.1 collective-permute-start.23
  117.2 2.0 collective-permute-start.21
  119.2 0.0 collective-permute-start.22
  119.2 8.9 %collective-permute-done.16 = bf16[2,1280,128]{2,1,0:T(8,128)(2,1)S(1)} collective-permute-done((bf16[2,1280,128]{2,1,0:T(8,128)(2,1)S(1)}, bf16[2,1280,128]{2,1,0:T(8,128)(2,1)S(1)}, u32[]{:S(2)}, u32[]{:S(2)}) %collective-permute-start.16) | collective-permute-done | bytes 655392 | tf_op jit(solution)/shard_map/ppermute | solution.py:167
  128.2 3.8 %collective-permute-start.17 = (bf16[1280,128]{1,0:T(8,128)(2,1)S(1)}, bf16[1280,128]{1,0:T(8,128)(2,1)S(1)}, u32[]{:S(2)}, u32[]{:S(2)}) collective-permute-start(bf16[1280,128]{1,0:T(8,128)(2,1)S(1)} %slice_bitcast_fusion.1), channel_id=1, source_target_pairs={{0,6},{2,0},{4,2},{6,4},{1,7},{3,1},{5,3},{7,5},{8,14},{10,8},{12,... | collective-permute-start | bytes 983048 | tf_op jit(solution)/shard_map/ppermute | solution.py:167
  132.0 0.1 collective-permute-start.18
  132.0 0.1 pad_maximum_fusion.1.refs_1_
  132.2 4.4 %collective-permute-done.17 = bf16[1280,128]{1,0:T(8,128)(2,1)S(1)} collective-permute-done((bf16[1280,128]{1,0:T(8,128)(2,1)S(1)}, bf16[1280,128]{1,0:T(8,128)(2,1)S(1)}, u32[]{:S(2)}, u32[]{:S(2)}) %collective-permute-start.17) | collective-permute-done | bytes 327712 | tf_op jit(solution)/shard_map/ppermute | solution.py:167
  136.5 5.2 %collective-permute-start.24 = (bf16[2,2560,128]{2,1,0:T(8,128)(2,1)S(1)}, bf16[2,2560,128]{2,1,0:T(8,128)(2,1)S(1)}, u32[]{:S(2)}, u32[]{:S(2)}) collective-permute-start(bf16[2,2560,128]{2,1,0:T(8,128)(2,1)S(1)} %pad_maximum_fusion.refs_6_), channel_id=1, source_target_pairs={{0,24},{1,97},{2,26},{3,99},{4,28},{5,101},{6,30},{7,103},{8,0},{9... | collective-permute-start | bytes 3932168 | tf_op jit(solution)/shard_map/ppermute | solution.py:196
  141.7 0.0 collective-permute-start.19
  141.8 0.1 maximum_bitcast_fusion.1
  141.8 0.1 pad_maximum_fusion.2.refs_2_
  142.0 0.6 collective-permute-start.20
  142.5 2.5 %collective-permute-start.25 = (bf16[2,2560,128]{2,1,0:T(8,128)(2,1)S(1)}, bf16[2,2560,128]{2,1,0:T(8,128)(2,1)S(1)}, u32[]{:S(2)}, u32[]{:S(2)}) collective-permute-start(bf16[2,2560,128]{2,1,0:T(8,128)(2,1)S(1)} %collective-permute-done.23.refs_9_), channel_id=1, source_target_pairs={{0,24},{1,97},{2,26},{3,99},{4,28},{5,101},{6,30},{7,103},{8,0},{9... | collective-permute-start | bytes 3932168 | tf_op jit(solution)/shard_map/ppermute | solution.py:196
  145.0 5.1 %collective-permute-done.22.refs_8_ = bf16[2,2560,128]{2,1,0:T(8,128)(2,1)S(1)} collective-permute-done((bf16[2,2560,128]{2,1,0:T(8,128)(2,1)S(1)}, bf16[2,2560,128]{2,1,0:T(8,128)(2,1)S(1)}, u32[]{:S(2)}, u32[]{:S(2)}) %collective-permute-start.22) | collective-permute-done | bytes 1310752 | tf_op jit(solution)/shard_map/ppermute | solution.py:196
  150.1 0.7 collective-permute-start.26
  150.8 0.1 pad_add_fusion.refs_0_
  150.9 5.9 %collective-permute-done.24.refs_10_ = bf16[2,2560,128]{2,1,0:T(8,128)(2,1)S(1)} collective-permute-done((bf16[2,2560,128]{2,1,0:T(8,128)(2,1)S(1)}, bf16[2,2560,128]{2,1,0:T(8,128)(2,1)S(1)}, u32[]{:S(2)}, u32[]{:S(2)}) %collective-permute-start.24) | collective-permute-done | bytes 1310752 | tf_op jit(solution)/shard_map/ppermute | solution.py:196
  156.9 14.0 %collective-permute-done.25.refs_11_ = bf16[2,2560,128]{2,1,0:T(8,128)(2,1)S(1)} collective-permute-done((bf16[2,2560,128]{2,1,0:T(8,128)(2,1)S(1)}, bf16[2,2560,128]{2,1,0:T(8,128)(2,1)S(1)}, u32[]{:S(2)}, u32[]{:S(2)}) %collective-permute-start.25) | collective-permute-done | bytes 1310752 | tf_op jit(solution)/shard_map/ppermute | solution.py:196
  170.9 31.1 %exchange.1 = f32[1280,2560]{1,0:T(8,128)} custom-call(s32[4]{0:T(128)S(1)} %pad_add_fusion.refs_0_, bf16[2,2,1280,128]{3,2,1,0:T(8,128)(2,1)S(1)} %pad_maximum_fusion.1.refs_1_, bf16[2,2,1280,128]{3,2,1,0:T(8,128)(2,1)S(1)} %pad_maximum_fusion.2.refs_2_, bf16[2,2,1280,128]{3,2,1,0:T(8,128)(2,1)S(1)} %collective-permute-done.19.refs_3_, ...), custom_call_target="tpu_custom_call" | custom-call | tf_op jit(solution)/shard_map/exchange/pallas_call | solution.py:323
  (24 shorter events, 0.3 us)
Async XLA Ops:
  0.0 43.7 %copy-start = (s32[16384]{0:T(1024)S(1)}, s32[16384]{0:T(1024)}, u32[]{:S(2)}) copy-start(s32[16384]{0:T(1024)} %param.8) | copy-start | bytes 196612
  43.7 4.3 %collective-permute-start = (bf16[256,32,128]{2,1,0:T(8,128)(2,1)S(1)}, bf16[256,32,128]{2,1,0:T(8,128)(2,1)}, u32[]{:S(2)}, u32[]{:S(2)}) collective-permute-start(bf16[256,32,128]{2,1,0:T(8,128)(2,1)S(1)} %all_to_all.5.own_ref), channel_id=1, source_target_pairs={{0,1},{1,0},{2,3},{3,2},{4,5},{5,4},{6,7},{7,6},{8,9},{9,8},{10,11... | collective-permute-start | bytes 6291464 | tf_op jit(solution)/shard_map/ppermute | solution.py:376
  51.4 11.9 %collective-permute-start.1 = (bf16[40,32,128]{2,1,0:T(8,128)(2,1)S(1)}, bf16[40,32,128]{2,1,0:T(8,128)(2,1)S(1)}, u32[]{:S(2)}, u32[]{:S(2)}) collective-permute-start(bf16[40,32,128]{2,1,0:T(8,128)(2,1)S(1)} %get-tuple-element.20), channel_id=1, source_target_pairs={{0,2},{2,4},{4,6},{6,0},{1,3},{3,5},{5,7},{7,1},{8,10},{10,12},{12... | collective-permute-start | bytes 983048 | tf_op jit(solution)/shard_map/ppermute | solution.py:167
  53.0 10.7 %collective-permute-start.5 = (bf16[40,32,128]{2,1,0:T(8,128)(2,1)S(1)}, bf16[40,32,128]{2,1,0:T(8,128)(2,1)S(1)}, u32[]{:S(2)}, u32[]{:S(2)}) collective-permute-start(bf16[40,32,128]{2,1,0:T(8,128)(2,1)S(1)} %get-tuple-element.24), channel_id=1, source_target_pairs={{0,6},{2,0},{4,2},{6,4},{1,7},{3,1},{5,3},{7,5},{8,14},{10,8},{12,... | collective-permute-start | bytes 983048 | tf_op jit(solution)/shard_map/ppermute | solution.py:167
  54.7 15.6 %collective-permute-start.3 = (bf16[40,32,128]{2,1,0:T(8,128)(2,1)S(1)}, bf16[40,32,128]{2,1,0:T(8,128)(2,1)S(1)}, u32[]{:S(2)}, u32[]{:S(2)}) collective-permute-start(bf16[40,32,128]{2,1,0:T(8,128)(2,1)S(1)} %get-tuple-element.21), channel_id=1, source_target_pairs={{0,2},{2,4},{4,6},{6,0},{1,3},{3,5},{5,7},{7,1},{8,10},{10,12},{12... | collective-permute-start | bytes 983048 | tf_op jit(solution)/shard_map/ppermute | solution.py:167
  55.0 15.6 %collective-permute-start.4 = (bf16[40,32,128]{2,1,0:T(8,128)(2,1)S(1)}, bf16[40,32,128]{2,1,0:T(8,128)(2,1)S(1)}, u32[]{:S(2)}, u32[]{:S(2)}) collective-permute-start(bf16[40,32,128]{2,1,0:T(8,128)(2,1)S(1)} %get-tuple-element.22), channel_id=1, source_target_pairs={{0,6},{2,0},{4,2},{6,4},{1,7},{3,1},{5,3},{7,5},{8,14},{10,8},{12,... | collective-permute-start | bytes 983048 | tf_op jit(solution)/shard_map/ppermute | solution.py:167
  63.3 13.0 %collective-permute-start.2 = (bf16[40,32,128]{2,1,0:T(8,128)(2,1)S(1)}, bf16[40,32,128]{2,1,0:T(8,128)(2,1)S(1)}, u32[]{:S(2)}, u32[]{:S(2)}) collective-permute-start(bf16[40,32,128]{2,1,0:T(8,128)(2,1)S(1)} %add_convert_fusion.2), channel_id=1, source_target_pairs={{0,2},{2,4},{4,6},{6,0},{1,3},{3,5},{5,7},{7,1},{8,10},{10,12},{12... | collective-permute-start | bytes 983048 | tf_op jit(solution)/shard_map/ppermute | solution.py:167
  63.8 12.8 %collective-permute-start.6 = (bf16[40,32,128]{2,1,0:T(8,128)(2,1)S(1)}, bf16[40,32,128]{2,1,0:T(8,128)(2,1)S(1)}, u32[]{:S(2)}, u32[]{:S(2)}) collective-permute-start(bf16[40,32,128]{2,1,0:T(8,128)(2,1)S(1)} %add_convert_fusion.1), channel_id=1, source_target_pairs={{0,6},{2,0},{4,2},{6,4},{1,7},{3,1},{5,3},{7,5},{8,14},{10,8},{12,... | collective-permute-start | bytes 983048 | tf_op jit(solution)/shard_map/ppermute | solution.py:167
  76.8 13.7 %collective-permute-start.8 = (bf16[2560,128]{1,0:T(8,128)(2,1)S(1)}, bf16[2560,128]{1,0:T(8,128)(2,1)S(1)}, u32[]{:S(2)}, u32[]{:S(2)}) collective-permute-start(bf16[2560,128]{1,0:T(8,128)(2,1)S(1)} %bitcast.109), channel_id=1, source_target_pairs={{0,96},{1,25},{2,98},{3,27},{4,100},{5,29},{6,102},{7,31},{8,104},... | collective-permute-start | bytes 1966088 | tf_op jit(solution)/shard_map/ppermute | solution.py:196
  77.5 13.0 %collective-permute-start.7 = (bf16[2560,128]{1,0:T(8,128)(2,1)S(1)}, bf16[2560,128]{1,0:T(8,128)(2,1)S(1)}, u32[]{:S(2)}, u32[]{:S(2)}) collective-permute-start(bf16[2560,128]{1,0:T(8,128)(2,1)S(1)} %bitcast.110), channel_id=1, source_target_pairs={{0,32},{1,9},{2,34},{3,11},{4,36},{5,13},{6,38},{7,15},{8,40},{9,1... | collective-permute-start | bytes 1966088 | tf_op jit(solution)/shard_map/ppermute | solution.py:196
  79.0 4.0 %collective-permute-start.9 = (bf16[1280,128]{1,0:T(8,128)(2,1)S(1)}, bf16[1280,128]{1,0:T(8,128)(2,1)S(1)}, u32[]{:S(2)}, u32[]{:S(2)}) collective-permute-start(bf16[1280,128]{1,0:T(8,128)(2,1)S(1)} %bitcast.122), channel_id=1, source_target_pairs={{0,0},{1,5},{2,2},{3,7},{4,4},{5,1},{6,6},{7,3},{8,8},{9,13},{10,1... | collective-permute-start | bytes 983048 | tf_op jit(solution)/shard_map/ppermute | solution.py:220
  79.6 10.8 %collective-permute-start.10 = (bf16[1280,128]{1,0:T(8,128)(2,1)S(1)}, bf16[1280,128]{1,0:T(8,128)(2,1)S(1)}, u32[]{:S(2)}, u32[]{:S(2)}) collective-permute-start(bf16[1280,128]{1,0:T(8,128)(2,1)S(1)} %bitcast.121), channel_id=1, source_target_pairs={{0,2},{1,7},{2,4},{3,1},{4,6},{5,3},{6,0},{7,5},{8,10},{9,15},{10,... | collective-permute-start | bytes 983048 | tf_op jit(solution)/shard_map/ppermute | solution.py:220
  90.5 8.4 %collective-permute-start.12 = (bf16[1280,128]{1,0:T(8,128)(2,1)S(1)}, bf16[1280,128]{1,0:T(8,128)(2,1)S(1)}, u32[]{:S(2)}, u32[]{:S(2)}) collective-permute-start(bf16[1280,128]{1,0:T(8,128)(2,1)S(1)} %slice.31), channel_id=1, source_target_pairs={{0,32},{1,9},{2,34},{3,11},{4,36},{5,13},{6,38},{7,15},{8,40},{9,1... | collective-permute-start | bytes 983048 | tf_op jit(solution)/shard_map/ppermute | solution.py:196
  93.7 8.9 %collective-permute-start.11 = (bf16[1280,128]{1,0:T(8,128)(2,1)S(1)}, bf16[1280,128]{1,0:T(8,128)(2,1)S(1)}, u32[]{:S(2)}, u32[]{:S(2)}) collective-permute-start(bf16[1280,128]{1,0:T(8,128)(2,1)S(1)} %slice.30), channel_id=1, source_target_pairs={{0,96},{1,25},{2,98},{3,27},{4,100},{5,29},{6,102},{7,31},{8,104},... | collective-permute-start | bytes 983048 | tf_op jit(solution)/shard_map/ppermute | solution.py:196
  93.8 9.0 %collective-permute-start.13 = (bf16[1280,128]{1,0:T(8,128)(2,1)S(1)}, bf16[1280,128]{1,0:T(8,128)(2,1)S(1)}, u32[]{:S(2)}, u32[]{:S(2)}) collective-permute-start(bf16[1280,128]{1,0:T(8,128)(2,1)S(1)} %collective-permute-done.9), channel_id=1, source_target_pairs={{0,0},{5,20},{2,34},{7,54},{4,68},{1,80},{6,102},{3,114},{8,1},{13... | collective-permute-start | bytes 983048 | tf_op jit(solution)/shard_map/ppermute | solution.py:224
  94.5 13.1 %collective-permute-start.14 = (bf16[1280,128]{1,0:T(8,128)(2,1)S(1)}, bf16[1280,128]{1,0:T(8,128)(2,1)S(1)}, u32[]{:S(2)}, u32[]{:S(2)}) collective-permute-start(bf16[1280,128]{1,0:T(8,128)(2,1)S(1)} %collective-permute-done.10), channel_id=1, source_target_pairs={{2,10},{7,30},{4,44},{1,56},{6,78},{3,90},{0,104},{5,124},{10,11},... | collective-permute-start | bytes 983048 | tf_op jit(solution)/shard_map/ppermute | solution.py:224
  107.7 20.5 %collective-permute-start.16 = (bf16[2,1280,128]{2,1,0:T(8,128)(2,1)S(1)}, bf16[2,1280,128]{2,1,0:T(8,128)(2,1)S(1)}, u32[]{:S(2)}, u32[]{:S(2)}) collective-permute-start(bf16[2,1280,128]{2,1,0:T(8,128)(2,1)S(1)} %pad_maximum_fusion.4), channel_id=1, source_target_pairs={{0,6},{2,0},{4,2},{6,4},{1,7},{3,1},{5,3},{7,5},{8,14},{10,8},{12,... | collective-permute-start | bytes 1966088 | tf_op jit(solution)/shard_map/ppermute | solution.py:167
  117.0 15.0 %collective-permute-start.15 = (bf16[2,1280,128]{2,1,0:T(8,128)(2,1)S(1)}, bf16[2,1280,128]{2,1,0:T(8,128)(2,1)S(1)}, u32[]{:S(2)}, u32[]{:S(2)}) collective-permute-start(bf16[2,1280,128]{2,1,0:T(8,128)(2,1)S(1)} %pad_maximum_fusion.4), channel_id=1, source_target_pairs={{0,2},{2,4},{4,6},{6,0},{1,3},{3,5},{5,7},{7,1},{8,10},{10,12},{12... | collective-permute-start | bytes 1966088 | tf_op jit(solution)/shard_map/ppermute | solution.py:167
  117.1 24.8 %collective-permute-start.23 = (bf16[2,2560,128]{2,1,0:T(8,128)(2,1)S(1)}, bf16[2,2560,128]{2,1,0:T(8,128)(2,1)S(1)}, u32[]{:S(2)}, u32[]{:S(2)}) collective-permute-start(bf16[2,2560,128]{2,1,0:T(8,128)(2,1)S(1)} %pad_maximum_fusion.3.refs_5_), channel_id=1, source_target_pairs={{0,24},{1,97},{2,26},{3,99},{4,28},{5,101},{6,30},{7,103},{8,0},{9... | collective-permute-start | bytes 3932168 | tf_op jit(solution)/shard_map/ppermute | solution.py:196
  117.2 25.4 %collective-permute-start.21 = (bf16[2,2560,128]{2,1,0:T(8,128)(2,1)S(1)}, bf16[2,2560,128]{2,1,0:T(8,128)(2,1)S(1)}, u32[]{:S(2)}, u32[]{:S(2)}) collective-permute-start(bf16[2,2560,128]{2,1,0:T(8,128)(2,1)S(1)} %pad_maximum_fusion.3.refs_5_), channel_id=1, source_target_pairs={{0,8},{1,33},{2,10},{3,35},{4,12},{5,37},{6,14},{7,39},{8,16},{9,4... | collective-permute-start | bytes 3932168 | tf_op jit(solution)/shard_map/ppermute | solution.py:196
  119.2 30.9 %collective-permute-start.22 = (bf16[2,2560,128]{2,1,0:T(8,128)(2,1)S(1)}, bf16[2,2560,128]{2,1,0:T(8,128)(2,1)S(1)}, u32[]{:S(2)}, u32[]{:S(2)}) collective-permute-start(bf16[2,2560,128]{2,1,0:T(8,128)(2,1)S(1)} %pad_maximum_fusion.refs_6_), channel_id=1, source_target_pairs={{0,8},{1,33},{2,10},{3,35},{4,12},{5,37},{6,14},{7,39},{8,16},{9,4... | collective-permute-start | bytes 3932168 | tf_op jit(solution)/shard_map/ppermute | solution.py:196
  128.2 8.4 %collective-permute-start.17 = (bf16[1280,128]{1,0:T(8,128)(2,1)S(1)}, bf16[1280,128]{1,0:T(8,128)(2,1)S(1)}, u32[]{:S(2)}, u32[]{:S(2)}) collective-permute-start(bf16[1280,128]{1,0:T(8,128)(2,1)S(1)} %slice_bitcast_fusion.1), channel_id=1, source_target_pairs={{0,6},{2,0},{4,2},{6,4},{1,7},{3,1},{5,3},{7,5},{8,14},{10,8},{12,... | collective-permute-start | bytes 983048 | tf_op jit(solution)/shard_map/ppermute | solution.py:167
  132.0 9.8 %collective-permute-start.18 = (bf16[1280,128]{1,0:T(8,128)(2,1)S(1)}, bf16[1280,128]{1,0:T(8,128)(2,1)S(1)}, u32[]{:S(2)}, u32[]{:S(2)}) collective-permute-start(bf16[1280,128]{1,0:T(8,128)(2,1)S(1)} %slice_bitcast_fusion), channel_id=1, source_target_pairs={{0,2},{2,4},{4,6},{6,0},{1,3},{3,5},{5,7},{7,1},{8,10},{10,12},{12... | collective-permute-start | bytes 983048 | tf_op jit(solution)/shard_map/ppermute | solution.py:167
  136.5 20.3 %collective-permute-start.24 = (bf16[2,2560,128]{2,1,0:T(8,128)(2,1)S(1)}, bf16[2,2560,128]{2,1,0:T(8,128)(2,1)S(1)}, u32[]{:S(2)}, u32[]{:S(2)}) collective-permute-start(bf16[2,2560,128]{2,1,0:T(8,128)(2,1)S(1)} %pad_maximum_fusion.refs_6_), channel_id=1, source_target_pairs={{0,24},{1,97},{2,26},{3,99},{4,28},{5,101},{6,30},{7,103},{8,0},{9... | collective-permute-start | bytes 3932168 | tf_op jit(solution)/shard_map/ppermute | solution.py:196
  141.7 15.1 %collective-permute-start.19 = (bf16[2,2,1280,128]{3,2,1,0:T(8,128)(2,1)S(1)}, bf16[2,2,1280,128]{3,2,1,0:T(8,128)(2,1)S(1)}, u32[]{:S(2)}, u32[]{:S(2)}) collective-permute-start(bf16[2,2,1280,128]{3,2,1,0:T(8,128)(2,1)S(1)} %pad_maximum_fusion.1.refs_1_), channel_id=1, source_target_pairs={{0,1},{1,0},{2,3},{3,2},{4,5},{5,4},{6,7},{7,6},{8,9},{9,8},{10,11... | collective-permute-start | bytes 3932168 | tf_op jit(solution)/shard_map/ppermute | solution.py:236
  142.0 14.9 %collective-permute-start.20 = (bf16[2,2,1280,128]{3,2,1,0:T(8,128)(2,1)S(1)}, bf16[2,2,1280,128]{3,2,1,0:T(8,128)(2,1)S(1)}, u32[]{:S(2)}, u32[]{:S(2)}) collective-permute-start(bf16[2,2,1280,128]{3,2,1,0:T(8,128)(2,1)S(1)} %pad_maximum_fusion.2.refs_2_), channel_id=1, source_target_pairs={{0,1},{1,0},{2,3},{3,2},{4,5},{5,4},{6,7},{7,6},{8,9},{9,8},{10,11... | collective-permute-start | bytes 3932168 | tf_op jit(solution)/shard_map/ppermute | solution.py:236
  142.5 28.4 %collective-permute-start.25 = (bf16[2,2560,128]{2,1,0:T(8,128)(2,1)S(1)}, bf16[2,2560,128]{2,1,0:T(8,128)(2,1)S(1)}, u32[]{:S(2)}, u32[]{:S(2)}) collective-permute-start(bf16[2,2560,128]{2,1,0:T(8,128)(2,1)S(1)} %collective-permute-done.23.refs_9_), channel_id=1, source_target_pairs={{0,24},{1,97},{2,26},{3,99},{4,28},{5,101},{6,30},{7,103},{8,0},{9... | collective-permute-start | bytes 3932168 | tf_op jit(solution)/shard_map/ppermute | solution.py:196
  150.1 20.8 %collective-permute-start.26 = (bf16[2,2560,128]{2,1,0:T(8,128)(2,1)S(1)}, bf16[2,2560,128]{2,1,0:T(8,128)(2,1)S(1)}, u32[]{:S(2)}, u32[]{:S(2)}) collective-permute-start(bf16[2,2560,128]{2,1,0:T(8,128)(2,1)S(1)} %collective-permute-done.22.refs_8_), channel_id=1, source_target_pairs={{0,8},{1,33},{2,10},{3,35},{4,12},{5,37},{6,14},{7,39},{8,16},{9,4... | collective-permute-start | bytes 3932168 | tf_op jit(solution)/shard_map/ppermute | solution.py:196

commit v5 on v3

--- a/solution.py
+++ b/solution.py
@@ -15,6 +15,7 @@
 OUT_PARTS = 4
 SWAP = [(0, 1), (1, 0)]
 VMEM_LIMIT = 56 * 1024 * 1024
+SUM_LIMIT = 24 * 1024 * 1024
 EXCHANGE_LIMIT = 36 * 1024 * 1024
 
 
@@ -92,15 +93,22 @@
 
 
 def sum_kernel(count_ref, list_ref, own_ref, other_ref, *refs):
-    out_refs, total_ref = refs[:-1], refs[-1]
+    out_refs, (total_ref, slots, sem) = refs[:-3], refs[-3:]
+    copies = [
+        pltpu.make_async_copy(slots_ref, slots.at[side], sem.at[side])
+        for side, slots_ref in enumerate((own_ref, other_ref))
+    ]
+    for copy in copies:
+        copy.start()
     total_ref[...] = jnp.zeros_like(total_ref)
-    for side, slots_ref in enumerate((own_ref, other_ref)):
-
-        def add(index, carry, side=side, slots_ref=slots_ref):
+    for side, copy in enumerate(copies):
+        copy.wait()
+
+        def add(index, carry, side=side):
             entry = list_ref[side, index]
             slot = lax.shift_right_logical(entry, 9)
             place = lax.bitwise_and(entry, 511)
-            total_ref[place] += slots_ref[slot].astype(jnp.float32)
+            total_ref[place] += slots[side, slot].astype(jnp.float32)
             return carry
 
         lax.fori_loop(0, count_ref[side], add, 0)
@@ -120,13 +128,17 @@
         in_specs=[
             pl.BlockSpec(memory_space=pltpu.SMEM),
             pl.BlockSpec(memory_space=pltpu.SMEM),
-            pl.BlockSpec(memory_space=pltpu.VMEM),
-            pl.BlockSpec(memory_space=pltpu.VMEM),
+            pl.BlockSpec(memory_space=pl.ANY),
+            pl.BlockSpec(memory_space=pl.ANY),
         ],
         out_specs=[pl.BlockSpec(memory_space=pltpu.VMEM)] * len(sizes),
         out_shape=[jax.ShapeDtypeStruct((size,) + tile_shape, jnp.bfloat16) for size in sizes],
-        scratch_shapes=[pltpu.VMEM((places,) + tile_shape, jnp.float32)],
-        compiler_params=pltpu.CompilerParams(vmem_limit_bytes=VMEM_LIMIT),
+        scratch_shapes=[
+            pltpu.VMEM((places,) + tile_shape, jnp.float32),
+            pltpu.VMEM((2,) + own.shape, jnp.bfloat16),
+            pltpu.SemaphoreType.DMA((2,)),
+        ],
+        compiler_params=pltpu.CompilerParams(vmem_limit_bytes=SUM_LIMIT),
         name="sum_slots",
     )(counts, entries, own, other)
     return outs
@@ -209,12 +221,11 @@
     low, high, rows = stage((low, high, rows))
 
     far_a, far_b = shift_turned(high[:middle], False, -1), shift_turned(low[middle:], False, 1)
-    rows = [lax.ppermute(rows[t], ALL_AXES, pairs[t][1]) for t in range(2)]
     near = jnp.stack([local, low])
     near_low, near_high = shift_turned(near, True, 1), shift_turned(near, True, -1)
+    far_a, far_b, rows = stage((far_a, far_b, rows))
+    rows = jnp.stack([lax.ppermute(rows[t], ALL_AXES, pairs[t][1]) for t in range(2)])
     far = jnp.stack([high, jnp.concatenate([far_a, far_b])])
-    rows = jnp.stack(rows)
-    far, rows = stage((far, rows))
 
     rows_low, rows_high = shift(rows, "x", 1), shift(rows, "x", -1)
     far_low, far_high = shift_turned(far, True, 1), shift_turned(far, True, -1)

time: 195 us -> 194 us (level)
  waiting for transfers between devices: 70.3 us -> 74.8 us
  other arithmetic: 5.31 us -> 2.23 us
  Pallas kernels: 33.3 us -> 30.7 us
    ppermute x10, waiting for transfers between devices: 26.5 us -> 30.8 us  [shift(): return lax.ppermute(value, axis, [(i, (i + by) % 4) for i in range(4)])]
    pallas_call x1, Pallas kernels: 5.65 us -> 3.23 us  [sum_slots(): pl.pallas_call(sum_kernel, in_specs=[pl.BlockSpec(memory_space=pltpu.SMEM...]
    ppermute x10, waiting for transfers between devices: 30.5 us -> 28.1 us  [shift_turned(): return lax.ppermute(value, ALL_AXES, pairs)]
  transfers between devices with their start and end apart: 27 -> 27, of which waited for: 14 -> 14; matrix products, arithmetic and copies ran while one was open for 3% -> 2% of each run, Pallas kernels for 0% -> 0%
where the time goes in v5:
time: 194 us; the launch traced here: 193 us
  waiting for transfers between devices  74.8 us (39%)
  starting transfers between devices  47.7 us (25%)
  blocking collectives  36.5 us (19%)
  Pallas kernels  30.7 us (16%)
  other arithmetic  2.23 us (1%)
    all_to_all x1, blocking collectives, shards(): lax.all_to_all(outgoing, AUX_AXES, split_axis=0, concat_axis=0, tiled=True)  36.5 us
    ppermute x10, waiting for transfers between devices, shift(): return lax.ppermute(value, axis, [(i, (i + by) % 4) for i in range(4)])  30.8 us
    ppermute x10, waiting for transfers between devices, shift_turned(): return lax.ppermute(value, ALL_AXES, pairs)  28.1 us
    ppermute x10, starting transfers between devices, shift(): return lax.ppermute(value, axis, [(i, (i + by) % 4) for i in range(4)])  24.5 us
    pallas_call x1, Pallas kernels, exchange_block(): pl.pallas_call(lambda *refs: exchange_kernel(*refs, factor=1.0 / depth),...  20.3 us
    ppermute x10, starting transfers between devices, shift_turned(): return lax.ppermute(value, ALL_AXES, pairs)  14.8 us
    ppermute x2, waiting for transfers between devices, gather_both(): lax.ppermute(jnp.where(turned, halves[1 - t], halves[t]), ALL_AXES, pairs...  7.57 us
    pallas_call x1, Pallas kernels, half_slots(): pl.pallas_call(half_kernel, grid_spec=pltpu.PrefetchScalarGridSpec(num_sc...  7.18 us
  transfers between devices with their start and end apart: 27, of which 14 were waited for; matrix products, arithmetic and copies ran while one was open for 2% of the time, Pallas kernels for 0%

profile of v5, /device:TPU:0, one launch (start us, length us, event | category | flops | bytes accessed | tf_op | source)
XLA Modules:
  0.0 193.4 jit_solution(775467307497610915)
XLA Ops:
  0.0 7.2 %half_transform.1 = bf16[256,32,128]{2,1,0:T(8,128)(2,1)} custom-call(s32[1]{0:T(128)} %bitcast.20.self_ref, s32[128,128]{1,0:T(8,128)} %bitcast.123, s32[128,128]{1,0:T(8,128)} %bitcast.125, bf16[128,4,32,128]{3,2,1,0:T(8,128)(2,1)} %tiles_ref.1, bf16[32,20480]{1,0:T(8,128)(2,1)} %orbital_ref.1, s32[32,160]{1,0:T(8,128)} %support_ref.1), custom_call_target="tpu_custom_call" | custom-call | tf_op jit(solution)/shard_map/half_transform/pallas_call | solution.py:71
  7.2 36.5 %all_to_all.5.own_ref = bf16[256,32,128]{2,1,0:T(8,128)(2,1)S(1)} all-to-all(bf16[256,32,128]{2,1,0:T(8,128)(2,1)} %half_transform.1), channel_id=1, replica_groups=mesh['z'=4,'y'=4,'x'=4,'core'=2] {'z','y'}, dimensions={0} | all-to-all | bytes 4194304 | tf_op jit(solution)/shard_map/all_to_all | solution.py:358
  43.7 0.0 collective-permute-start
  43.8 0.7 constant_dynamic-slice_fusion.1
  44.5 0.2 convert_reduce_fusion
  44.7 0.2 reduce_window_sum.11
  44.9 0.1 convolution_convert_fusion
  45.0 0.1 fusion.20
  45.1 0.5 select_reduce_fusion.list_ref
  45.7 2.4 %collective-permute-done.other_ref = bf16[256,32,128]{2,1,0:T(8,128)(2,1)} collective-permute-done((bf16[256,32,128]{2,1,0:T(8,128)(2,1)S(1)}, bf16[256,32,128]{2,1,0:T(8,128)(2,1)}, u32[]{:S(2)}, u32[]{:S(2)}) %collective-permute-start) | collective-permute-done | bytes 2097184 | tf_op jit(solution)/shard_map/ppermute | solution.py:367
  48.0 3.2 %sum_slots.1 = (bf16[80,32,128]{2,1,0:T(8,128)(2,1)S(1)}, bf16[40,32,128]{2,1,0:T(8,128)(2,1)S(1)}, bf16[40,32,128]{2,1,0:T(8,128)(2,1)S(1)}, bf16[40,32,128]{2,...) custom-call(s32[2]{0:T(128)S(1)} %get-tuple-element.36.count_ref, ...), custom_call_target="tpu_custom_call" | custom-call | tf_op jit(solution)/shard_map/sum_slots/pallas_call | solution.py:126
  51.3 1.5 collective-permute-start.1
  52.7 1.9 collective-permute-start.5
  54.6 0.2 collective-permute-start.3
  54.7 3.1 %collective-permute-start.4 = (bf16[40,32,128]{2,1,0:T(8,128)(2,1)S(1)}, bf16[40,32,128]{2,1,0:T(8,128)(2,1)S(1)}, u32[]{:S(2)}, u32[]{:S(2)}) collective-permute-start(bf16[40,32,128]{2,1,0:T(8,128)(2,1)S(1)} %get-tuple-element.24), channel_id=1, source_target_pairs={{0,6},{2,0},{4,2},{6,4},{1,7},{3,1},{5,3},{7,5},{8,14},{10,8},{12,... | collective-permute-start | bytes 983048 | tf_op jit(solution)/shard_map/ppermute | solution.py:167
  57.8 5.3 %collective-permute-done.1 = bf16[40,32,128]{2,1,0:T(8,128)(2,1)S(1)} collective-permute-done((bf16[40,32,128]{2,1,0:T(8,128)(2,1)S(1)}, bf16[40,32,128]{2,1,0:T(8,128)(2,1)S(1)}, u32[]{:S(2)}, u32[]{:S(2)}) %collective-permute-start.1) | collective-permute-done | bytes 327712 | tf_op jit(solution)/shard_map/ppermute | solution.py:167
  63.1 0.1 add_convert_fusion.2
  63.2 0.2 collective-permute-start.2
  63.4 0.0 collective-permute-done.5
  63.4 0.1 add_convert_fusion.1
  63.5 3.1 %collective-permute-start.6 = (bf16[40,32,128]{2,1,0:T(8,128)(2,1)S(1)}, bf16[40,32,128]{2,1,0:T(8,128)(2,1)S(1)}, u32[]{:S(2)}, u32[]{:S(2)}) collective-permute-start(bf16[40,32,128]{2,1,0:T(8,128)(2,1)S(1)} %add_convert_fusion.1), channel_id=1, source_target_pairs={{0,6},{2,0},{4,2},{6,4},{1,7},{3,1},{5,3},{7,5},{8,14},{10,8},{12,... | collective-permute-start | bytes 983048 | tf_op jit(solution)/shard_map/ppermute | solution.py:167
  66.7 3.5 %collective-permute-done.3 = bf16[40,32,128]{2,1,0:T(8,128)(2,1)S(1)} collective-permute-done((bf16[40,32,128]{2,1,0:T(8,128)(2,1)S(1)}, bf16[40,32,128]{2,1,0:T(8,128)(2,1)S(1)}, u32[]{:S(2)}, u32[]{:S(2)}) %collective-permute-start.3) | collective-permute-done | bytes 327712 | tf_op jit(solution)/shard_map/ppermute | solution.py:167
  70.1 0.2 collective-permute-done.4
  70.3 5.9 %collective-permute-done.2 = bf16[40,32,128]{2,1,0:T(8,128)(2,1)S(1)} collective-permute-done((bf16[40,32,128]{2,1,0:T(8,128)(2,1)S(1)}, bf16[40,32,128]{2,1,0:T(8,128)(2,1)S(1)}, u32[]{:S(2)}, u32[]{:S(2)}) %collective-permute-start.2) | collective-permute-done | bytes 327712 | tf_op jit(solution)/shard_map/ppermute | solution.py:167
  76.2 0.0 collective-permute-done.6
  76.2 0.3 add_convert_fusion
  76.5 1.1 collective-permute-start.8
  77.6 1.0 collective-permute-start.7
  78.7 0.7 collective-permute-start.9
  79.3 3.4 %collective-permute-start.10 = (bf16[1280,128]{1,0:T(8,128)(2,1)S(1)}, bf16[1280,128]{1,0:T(8,128)(2,1)S(1)}, u32[]{:S(2)}, u32[]{:S(2)}) collective-permute-start(bf16[1280,128]{1,0:T(8,128)(2,1)S(1)} %bitcast.119), channel_id=1, source_target_pairs={{0,2},{1,7},{2,4},{3,1},{4,6},{5,3},{6,0},{7,5},{8,10},{9,15},{10,... | collective-permute-start | bytes 983048 | tf_op jit(solution)/shard_map/ppermute | solution.py:220
  82.7 7.6 %collective-permute-done.10 = bf16[1280,128]{1,0:T(8,128)(2,1)S(1)} collective-permute-done((bf16[1280,128]{1,0:T(8,128)(2,1)S(1)}, bf16[1280,128]{1,0:T(8,128)(2,1)S(1)}, u32[]{:S(2)}, u32[]{:S(2)}) %collective-permute-start.10) | collective-permute-done | bytes 327712 | tf_op jit(solution)/shard_map/ppermute | solution.py:220
  90.4 3.3 %collective-permute-start.12 = (bf16[1280,128]{1,0:T(8,128)(2,1)S(1)}, bf16[1280,128]{1,0:T(8,128)(2,1)S(1)}, u32[]{:S(2)}, u32[]{:S(2)}) collective-permute-start(bf16[1280,128]{1,0:T(8,128)(2,1)S(1)} %slice.31), channel_id=1, source_target_pairs={{0,32},{1,9},{2,34},{3,11},{4,36},{5,13},{6,38},{7,15},{8,40},{9,1... | collective-permute-start | bytes 983048 | tf_op jit(solution)/shard_map/ppermute | solution.py:196
  93.7 5.0 %collective-permute-done.12 = bf16[1280,128]{1,0:T(8,128)(2,1)S(1)} collective-permute-done((bf16[1280,128]{1,0:T(8,128)(2,1)S(1)}, bf16[1280,128]{1,0:T(8,128)(2,1)S(1)}, u32[]{:S(2)}, u32[]{:S(2)}) %collective-permute-start.12) | collective-permute-done | bytes 327712 | tf_op jit(solution)/shard_map/ppermute | solution.py:196
  98.7 2.0 %collective-permute-done.11 = bf16[1280,128]{1,0:T(8,128)(2,1)S(1)} collective-permute-done((bf16[1280,128]{1,0:T(8,128)(2,1)S(1)}, bf16[1280,128]{1,0:T(8,128)(2,1)S(1)}, u32[]{:S(2)}, u32[]{:S(2)}) %collective-permute-start.11) | collective-permute-done | bytes 327712 | tf_op jit(solution)/shard_map/ppermute | solution.py:196
  100.7 0.7 collective-permute-start.13
  101.4 2.8 %collective-permute-start.14 = (bf16[1280,128]{1,0:T(8,128)(2,1)S(1)}, bf16[1280,128]{1,0:T(8,128)(2,1)S(1)}, u32[]{:S(2)}, u32[]{:S(2)}) collective-permute-start(bf16[1280,128]{1,0:T(8,128)(2,1)S(1)} %collective-permute-done.10), channel_id=1, source_target_pairs={{2,10},{7,30},{4,44},{1,56},{6,78},{3,90},{0,104},{5,124},{10,11},... | collective-permute-start | bytes 983048 | tf_op jit(solution)/shard_map/ppermute | solution.py:227
  104.2 0.1 pad_maximum_fusion.2.refs_5_
  104.3 4.0 %collective-permute-start.23 = (bf16[2,2560,128]{2,1,0:T(8,128)(2,1)S(1)}, bf16[2,2560,128]{2,1,0:T(8,128)(2,1)S(1)}, u32[]{:S(2)}, u32[]{:S(2)}) collective-permute-start(bf16[2,2560,128]{2,1,0:T(8,128)(2,1)S(1)} %pad_maximum_fusion.2.refs_5_), channel_id=1, source_target_pairs={{0,24},{1,97},{2,26},{3,99},{4,28},{5,101},{6,30},{7,103},{8,0},{9... | collective-permute-start | bytes 3932168 | tf_op jit(solution)/shard_map/ppermute | solution.py:196
  108.3 6.0 %collective-permute-done.14 = bf16[1280,128]{1,0:T(8,128)(2,1)S(1)} collective-permute-done((bf16[1280,128]{1,0:T(8,128)(2,1)S(1)}, bf16[1280,128]{1,0:T(8,128)(2,1)S(1)}, u32[]{:S(2)}, u32[]{:S(2)}) %collective-permute-start.14) | collective-permute-done | bytes 327712 | tf_op jit(solution)/shard_map/ppermute | solution.py:227
  114.3 0.1 fusion.32
  114.4 8.9 %collective-permute-start.15 = (bf16[2,1280,128]{2,1,0:T(8,128)(2,1)S(1)}, bf16[2,1280,128]{2,1,0:T(8,128)(2,1)S(1)}, u32[]{:S(2)}, u32[]{:S(2)}) collective-permute-start(bf16[2,1280,128]{2,1,0:T(8,128)(2,1)S(1)} %get-tuple-element.40), channel_id=1, source_target_pairs={{0,2},{2,4},{4,6},{6,0},{1,3},{3,5},{5,7},{7,1},{8,10},{10,12},{12... | collective-permute-start | bytes 1966088 | tf_op jit(solution)/shard_map/ppermute | solution.py:167
  123.4 2.8 %collective-permute-start.16 = (bf16[2,1280,128]{2,1,0:T(8,128)(2,1)S(1)}, bf16[2,1280,128]{2,1,0:T(8,128)(2,1)S(1)}, u32[]{:S(2)}, u32[]{:S(2)}) collective-permute-start(bf16[2,1280,128]{2,1,0:T(8,128)(2,1)S(1)} %get-tuple-element.40), channel_id=1, source_target_pairs={{0,6},{2,0},{4,2},{6,4},{1,7},{3,1},{5,3},{7,5},{8,14},{10,8},{12,... | collective-permute-start | bytes 1966088 | tf_op jit(solution)/shard_map/ppermute | solution.py:167
  126.1 0.1 pad_maximum_fusion.3.refs_6_
  126.3 0.1 collective-permute-start.22
  126.3 11.2 %collective-permute-done.15 = bf16[2,1280,128]{2,1,0:T(8,128)(2,1)S(1)} collective-permute-done((bf16[2,1280,128]{2,1,0:T(8,128)(2,1)S(1)}, bf16[2,1280,128]{2,1,0:T(8,128)(2,1)S(1)}, u32[]{:S(2)}, u32[]{:S(2)}) %collective-permute-start.15) | collective-permute-done | bytes 655392 | tf_op jit(solution)/shard_map/ppermute | solution.py:167
  137.6 0.4 collective-permute-start.18
  138.0 0.5 collective-permute-done.16
  138.6 2.5 %collective-permute-start.17 = (bf16[1280,128]{1,0:T(8,128)(2,1)S(1)}, bf16[1280,128]{1,0:T(8,128)(2,1)S(1)}, u32[]{:S(2)}, u32[]{:S(2)}) collective-permute-start(bf16[1280,128]{1,0:T(8,128)(2,1)S(1)} %slice_bitcast_fusion.1), channel_id=1, source_target_pairs={{0,6},{2,0},{4,2},{6,4},{1,7},{3,1},{5,3},{7,5},{8,14},{10,8},{12,... | collective-permute-start | bytes 983048 | tf_op jit(solution)/shard_map/ppermute | solution.py:167
  141.0 0.1 pad_maximum_fusion.refs_1_
  141.1 0.0 collective-permute-done.23.refs_9_
  141.1 0.6 collective-permute-start.24
  141.8 4.2 %collective-permute-done.18 = bf16[1280,128]{1,0:T(8,128)(2,1)S(1)} collective-permute-done((bf16[1280,128]{1,0:T(8,128)(2,1)S(1)}, bf16[1280,128]{1,0:T(8,128)(2,1)S(1)}, u32[]{:S(2)}, u32[]{:S(2)}) %collective-permute-start.18) | collective-permute-done | bytes 327712 | tf_op jit(solution)/shard_map/ppermute | solution.py:167
  146.0 0.0 collective-permute-done.17
  146.0 2.4 %collective-permute-start.25 = (bf16[2,2560,128]{2,1,0:T(8,128)(2,1)S(1)}, bf16[2,2560,128]{2,1,0:T(8,128)(2,1)S(1)}, u32[]{:S(2)}, u32[]{:S(2)}) collective-permute-start(bf16[2,2560,128]{2,1,0:T(8,128)(2,1)S(1)} %collective-permute-done.23.refs_9_), channel_id=1, source_target_pairs={{0,24},{1,97},{2,26},{3,99},{4,28},{5,101},{6,30},{7,103},{8,0},{9... | collective-permute-start | bytes 3932168 | tf_op jit(solution)/shard_map/ppermute | solution.py:196
  148.4 0.1 maximum_bitcast_fusion
  148.4 0.1 pad_maximum_fusion.1.refs_2_
  148.6 0.9 collective-permute-start.20
  149.5 2.3 %collective-permute-start.26 = (bf16[2,2560,128]{2,1,0:T(8,128)(2,1)S(1)}, bf16[2,2560,128]{2,1,0:T(8,128)(2,1)S(1)}, u32[]{:S(2)}, u32[]{:S(2)}) collective-permute-start(bf16[2,2560,128]{2,1,0:T(8,128)(2,1)S(1)} %collective-permute-done.22.refs_8_), channel_id=1, source_target_pairs={{0,8},{1,33},{2,10},{3,35},{4,12},{5,37},{6,14},{7,39},{8,16},{9,4... | collective-permute-start | bytes 3932168 | tf_op jit(solution)/shard_map/ppermute | solution.py:196
  151.8 0.1 pad_add_fusion.refs_0_
  151.9 7.0 %collective-permute-done.24.refs_10_ = bf16[2,2560,128]{2,1,0:T(8,128)(2,1)S(1)} collective-permute-done((bf16[2,2560,128]{2,1,0:T(8,128)(2,1)S(1)}, bf16[2,2560,128]{2,1,0:T(8,128)(2,1)S(1)}, u32[]{:S(2)}, u32[]{:S(2)}) %collective-permute-start.24) | collective-permute-done | bytes 1310752 | tf_op jit(solution)/shard_map/ppermute | solution.py:196
  158.8 14.0 %collective-permute-done.25.refs_11_ = bf16[2,2560,128]{2,1,0:T(8,128)(2,1)S(1)} collective-permute-done((bf16[2,2560,128]{2,1,0:T(8,128)(2,1)S(1)}, bf16[2,2560,128]{2,1,0:T(8,128)(2,1)S(1)}, u32[]{:S(2)}, u32[]{:S(2)}) %collective-permute-start.25) | collective-permute-done | bytes 1310752 | tf_op jit(solution)/shard_map/ppermute | solution.py:196
  172.9 0.0 collective-permute-done.20.refs_4_
  172.9 0.0 collective-permute-done.26.refs_12_
  172.9 20.3 %exchange.1 = f32[1280,2560]{1,0:T(8,128)} custom-call(s32[4]{0:T(128)S(1)} %pad_add_fusion.refs_0_, bf16[2,2,1280,128]{3,2,1,0:T(8,128)(2,1)S(1)} %pad_maximum_fusion.refs_1_, bf16[2,2,1280,128]{3,2,1,0:T(8,128)(2,1)S(1)} %pad_maximum_fusion.1.refs_2_, bf16[2,2,1280,128]{3,2,1,0:T(8,128)(2,1)S(1)} %collective-permute-done.19.refs_3_, ...), custom_call_target="tpu_custom_call" | custom-call | tf_op jit(solution)/shard_map/exchange/pallas_call | solution.py:315
  (24 shorter events, 0.3 us)
Async XLA Ops:
  0.0 43.7 %copy-start = (s32[16384]{0:T(1024)S(1)}, s32[16384]{0:T(1024)}, u32[]{:S(2)}) copy-start(s32[16384]{0:T(1024)} %param.8) | copy-start | bytes 196612
  43.7 4.3 %collective-permute-start = (bf16[256,32,128]{2,1,0:T(8,128)(2,1)S(1)}, bf16[256,32,128]{2,1,0:T(8,128)(2,1)}, u32[]{:S(2)}, u32[]{:S(2)}) collective-permute-start(bf16[256,32,128]{2,1,0:T(8,128)(2,1)S(1)} %all_to_all.5.own_ref), channel_id=1, source_target_pairs={{0,1},{1,0},{2,3},{3,2},{4,5},{5,4},{6,7},{7,6},{8,9},{9,8},{10,11... | collective-permute-start | bytes 6291464 | tf_op jit(solution)/shard_map/ppermute | solution.py:367
  51.3 11.9 %collective-permute-start.1 = (bf16[40,32,128]{2,1,0:T(8,128)(2,1)S(1)}, bf16[40,32,128]{2,1,0:T(8,128)(2,1)S(1)}, u32[]{:S(2)}, u32[]{:S(2)}) collective-permute-start(bf16[40,32,128]{2,1,0:T(8,128)(2,1)S(1)} %get-tuple-element.22), channel_id=1, source_target_pairs={{0,2},{2,4},{4,6},{6,0},{1,3},{3,5},{5,7},{7,1},{8,10},{10,12},{12... | collective-permute-start | bytes 983048 | tf_op jit(solution)/shard_map/ppermute | solution.py:167
  52.7 10.7 %collective-permute-start.5 = (bf16[40,32,128]{2,1,0:T(8,128)(2,1)S(1)}, bf16[40,32,128]{2,1,0:T(8,128)(2,1)S(1)}, u32[]{:S(2)}, u32[]{:S(2)}) collective-permute-start(bf16[40,32,128]{2,1,0:T(8,128)(2,1)S(1)} %get-tuple-element.26), channel_id=1, source_target_pairs={{0,6},{2,0},{4,2},{6,4},{1,7},{3,1},{5,3},{7,5},{8,14},{10,8},{12,... | collective-permute-start | bytes 983048 | tf_op jit(solution)/shard_map/ppermute | solution.py:167
  54.6 15.6 %collective-permute-start.3 = (bf16[40,32,128]{2,1,0:T(8,128)(2,1)S(1)}, bf16[40,32,128]{2,1,0:T(8,128)(2,1)S(1)}, u32[]{:S(2)}, u32[]{:S(2)}) collective-permute-start(bf16[40,32,128]{2,1,0:T(8,128)(2,1)S(1)} %get-tuple-element.23), channel_id=1, source_target_pairs={{0,2},{2,4},{4,6},{6,0},{1,3},{3,5},{5,7},{7,1},{8,10},{10,12},{12... | collective-permute-start | bytes 983048 | tf_op jit(solution)/shard_map/ppermute | solution.py:167
  54.7 15.6 %collective-permute-start.4 = (bf16[40,32,128]{2,1,0:T(8,128)(2,1)S(1)}, bf16[40,32,128]{2,1,0:T(8,128)(2,1)S(1)}, u32[]{:S(2)}, u32[]{:S(2)}) collective-permute-start(bf16[40,32,128]{2,1,0:T(8,128)(2,1)S(1)} %get-tuple-element.24), channel_id=1, source_target_pairs={{0,6},{2,0},{4,2},{6,4},{1,7},{3,1},{5,3},{7,5},{8,14},{10,8},{12,... | collective-permute-start | bytes 983048 | tf_op jit(solution)/shard_map/ppermute | solution.py:167
  63.2 13.0 %collective-permute-start.2 = (bf16[40,32,128]{2,1,0:T(8,128)(2,1)S(1)}, bf16[40,32,128]{2,1,0:T(8,128)(2,1)S(1)}, u32[]{:S(2)}, u32[]{:S(2)}) collective-permute-start(bf16[40,32,128]{2,1,0:T(8,128)(2,1)S(1)} %add_convert_fusion.2), channel_id=1, source_target_pairs={{0,2},{2,4},{4,6},{6,0},{1,3},{3,5},{5,7},{7,1},{8,10},{10,12},{12... | collective-permute-start | bytes 983048 | tf_op jit(solution)/shard_map/ppermute | solution.py:167
  63.5 12.7 %collective-permute-start.6 = (bf16[40,32,128]{2,1,0:T(8,128)(2,1)S(1)}, bf16[40,32,128]{2,1,0:T(8,128)(2,1)S(1)}, u32[]{:S(2)}, u32[]{:S(2)}) collective-permute-start(bf16[40,32,128]{2,1,0:T(8,128)(2,1)S(1)} %add_convert_fusion.1), channel_id=1, source_target_pairs={{0,6},{2,0},{4,2},{6,4},{1,7},{3,1},{5,3},{7,5},{8,14},{10,8},{12,... | collective-permute-start | bytes 983048 | tf_op jit(solution)/shard_map/ppermute | solution.py:167
  76.5 13.8 %collective-permute-start.8 = (bf16[2560,128]{1,0:T(8,128)(2,1)S(1)}, bf16[2560,128]{1,0:T(8,128)(2,1)S(1)}, u32[]{:S(2)}, u32[]{:S(2)}) collective-permute-start(bf16[2560,128]{1,0:T(8,128)(2,1)S(1)} %bitcast.110), channel_id=1, source_target_pairs={{0,96},{1,25},{2,98},{3,27},{4,100},{5,29},{6,102},{7,31},{8,104},... | collective-permute-start | bytes 1966088 | tf_op jit(solution)/shard_map/ppermute | solution.py:196
  77.6 12.7 %collective-permute-start.7 = (bf16[2560,128]{1,0:T(8,128)(2,1)S(1)}, bf16[2560,128]{1,0:T(8,128)(2,1)S(1)}, u32[]{:S(2)}, u32[]{:S(2)}) collective-permute-start(bf16[2560,128]{1,0:T(8,128)(2,1)S(1)} %bitcast.111), channel_id=1, source_target_pairs={{0,32},{1,9},{2,34},{3,11},{4,36},{5,13},{6,38},{7,15},{8,40},{9,1... | collective-permute-start | bytes 1966088 | tf_op jit(solution)/shard_map/ppermute | solution.py:196
  78.7 4.1 %collective-permute-start.9 = (bf16[1280,128]{1,0:T(8,128)(2,1)S(1)}, bf16[1280,128]{1,0:T(8,128)(2,1)S(1)}, u32[]{:S(2)}, u32[]{:S(2)}) collective-permute-start(bf16[1280,128]{1,0:T(8,128)(2,1)S(1)} %bitcast.120), channel_id=1, source_target_pairs={{0,0},{1,5},{2,2},{3,7},{4,4},{5,1},{6,6},{7,3},{8,8},{9,13},{10,1... | collective-permute-start | bytes 983048 | tf_op jit(solution)/shard_map/ppermute | solution.py:220
  79.3 10.9 %collective-permute-start.10 = (bf16[1280,128]{1,0:T(8,128)(2,1)S(1)}, bf16[1280,128]{1,0:T(8,128)(2,1)S(1)}, u32[]{:S(2)}, u32[]{:S(2)}) collective-permute-start(bf16[1280,128]{1,0:T(8,128)(2,1)S(1)} %bitcast.119), channel_id=1, source_target_pairs={{0,2},{1,7},{2,4},{3,1},{4,6},{5,3},{6,0},{7,5},{8,10},{9,15},{10,... | collective-permute-start | bytes 983048 | tf_op jit(solution)/shard_map/ppermute | solution.py:220
  90.4 8.4 %collective-permute-start.12 = (bf16[1280,128]{1,0:T(8,128)(2,1)S(1)}, bf16[1280,128]{1,0:T(8,128)(2,1)S(1)}, u32[]{:S(2)}, u32[]{:S(2)}) collective-permute-start(bf16[1280,128]{1,0:T(8,128)(2,1)S(1)} %slice.31), channel_id=1, source_target_pairs={{0,32},{1,9},{2,34},{3,11},{4,36},{5,13},{6,38},{7,15},{8,40},{9,1... | collective-permute-start | bytes 983048 | tf_op jit(solution)/shard_map/ppermute | solution.py:196
  93.7 7.1 %collective-permute-start.11 = (bf16[1280,128]{1,0:T(8,128)(2,1)S(1)}, bf16[1280,128]{1,0:T(8,128)(2,1)S(1)}, u32[]{:S(2)}, u32[]{:S(2)}) collective-permute-start(bf16[1280,128]{1,0:T(8,128)(2,1)S(1)} %slice.30), channel_id=1, source_target_pairs={{0,96},{1,25},{2,98},{3,27},{4,100},{5,29},{6,102},{7,31},{8,104},... | collective-permute-start | bytes 983048 | tf_op jit(solution)/shard_map/ppermute | solution.py:196
  100.7 7.6 %collective-permute-start.13 = (bf16[1280,128]{1,0:T(8,128)(2,1)S(1)}, bf16[1280,128]{1,0:T(8,128)(2,1)S(1)}, u32[]{:S(2)}, u32[]{:S(2)}) collective-permute-start(bf16[1280,128]{1,0:T(8,128)(2,1)S(1)} %collective-permute-done.9), channel_id=1, source_target_pairs={{0,0},{5,20},{2,34},{7,54},{4,68},{1,80},{6,102},{3,114},{8,1},{13... | collective-permute-start | bytes 983048 | tf_op jit(solution)/shard_map/ppermute | solution.py:227
  101.4 12.9 %collective-permute-start.14 = (bf16[1280,128]{1,0:T(8,128)(2,1)S(1)}, bf16[1280,128]{1,0:T(8,128)(2,1)S(1)}, u32[]{:S(2)}, u32[]{:S(2)}) collective-permute-start(bf16[1280,128]{1,0:T(8,128)(2,1)S(1)} %collective-permute-done.10), channel_id=1, source_target_pairs={{2,10},{7,30},{4,44},{1,56},{6,78},{3,90},{0,104},{5,124},{10,11},... | collective-permute-start | bytes 983048 | tf_op jit(solution)/shard_map/ppermute | solution.py:227
  104.3 36.8 %collective-permute-start.23 = (bf16[2,2560,128]{2,1,0:T(8,128)(2,1)S(1)}, bf16[2,2560,128]{2,1,0:T(8,128)(2,1)S(1)}, u32[]{:S(2)}, u32[]{:S(2)}) collective-permute-start(bf16[2,2560,128]{2,1,0:T(8,128)(2,1)S(1)} %pad_maximum_fusion.2.refs_5_), channel_id=1, source_target_pairs={{0,24},{1,97},{2,26},{3,99},{4,28},{5,101},{6,30},{7,103},{8,0},{9... | collective-permute-start | bytes 3932168 | tf_op jit(solution)/shard_map/ppermute | solution.py:196
  108.3 40.3 %collective-permute-start.21 = (bf16[2,2560,128]{2,1,0:T(8,128)(2,1)S(1)}, bf16[2,2560,128]{2,1,0:T(8,128)(2,1)S(1)}, u32[]{:S(2)}, u32[]{:S(2)}) collective-permute-start(bf16[2,2560,128]{2,1,0:T(8,128)(2,1)S(1)} %pad_maximum_fusion.2.refs_5_), channel_id=1, source_target_pairs={{0,8},{1,33},{2,10},{3,35},{4,12},{5,37},{6,14},{7,39},{8,16},{9,4... | collective-permute-start | bytes 3932168 | tf_op jit(solution)/shard_map/ppermute | solution.py:196
  114.4 23.2 %collective-permute-start.15 = (bf16[2,1280,128]{2,1,0:T(8,128)(2,1)S(1)}, bf16[2,1280,128]{2,1,0:T(8,128)(2,1)S(1)}, u32[]{:S(2)}, u32[]{:S(2)}) collective-permute-start(bf16[2,1280,128]{2,1,0:T(8,128)(2,1)S(1)} %get-tuple-element.40), channel_id=1, source_target_pairs={{0,2},{2,4},{4,6},{6,0},{1,3},{3,5},{5,7},{7,1},{8,10},{10,12},{12... | collective-permute-start | bytes 1966088 | tf_op jit(solution)/shard_map/ppermute | solution.py:167
  123.4 15.2 %collective-permute-start.16 = (bf16[2,1280,128]{2,1,0:T(8,128)(2,1)S(1)}, bf16[2,1280,128]{2,1,0:T(8,128)(2,1)S(1)}, u32[]{:S(2)}, u32[]{:S(2)}) collective-permute-start(bf16[2,1280,128]{2,1,0:T(8,128)(2,1)S(1)} %get-tuple-element.40), channel_id=1, source_target_pairs={{0,6},{2,0},{4,2},{6,4},{1,7},{3,1},{5,3},{7,5},{8,14},{10,8},{12,... | collective-permute-start | bytes 1966088 | tf_op jit(solution)/shard_map/ppermute | solution.py:167
  126.3 23.2 %collective-permute-start.22 = (bf16[2,2560,128]{2,1,0:T(8,128)(2,1)S(1)}, bf16[2,2560,128]{2,1,0:T(8,128)(2,1)S(1)}, u32[]{:S(2)}, u32[]{:S(2)}) collective-permute-start(bf16[2,2560,128]{2,1,0:T(8,128)(2,1)S(1)} %pad_maximum_fusion.3.refs_6_), channel_id=1, source_target_pairs={{0,8},{1,33},{2,10},{3,35},{4,12},{5,37},{6,14},{7,39},{8,16},{9,4... | collective-permute-start | bytes 3932168 | tf_op jit(solution)/shard_map/ppermute | solution.py:196
  137.6 8.4 %collective-permute-start.18 = (bf16[1280,128]{1,0:T(8,128)(2,1)S(1)}, bf16[1280,128]{1,0:T(8,128)(2,1)S(1)}, u32[]{:S(2)}, u32[]{:S(2)}) collective-permute-start(bf16[1280,128]{1,0:T(8,128)(2,1)S(1)} %slice_bitcast_fusion), channel_id=1, source_target_pairs={{0,2},{2,4},{4,6},{6,0},{1,3},{3,5},{5,7},{7,1},{8,10},{10,12},{12... | collective-permute-start | bytes 983048 | tf_op jit(solution)/shard_map/ppermute | solution.py:167
  138.6 7.4 %collective-permute-start.17 = (bf16[1280,128]{1,0:T(8,128)(2,1)S(1)}, bf16[1280,128]{1,0:T(8,128)(2,1)S(1)}, u32[]{:S(2)}, u32[]{:S(2)}) collective-permute-start(bf16[1280,128]{1,0:T(8,128)(2,1)S(1)} %slice_bitcast_fusion.1), channel_id=1, source_target_pairs={{0,6},{2,0},{4,2},{6,4},{1,7},{3,1},{5,3},{7,5},{8,14},{10,8},{12,... | collective-permute-start | bytes 983048 | tf_op jit(solution)/shard_map/ppermute | solution.py:167
  141.1 17.7 %collective-permute-start.24 = (bf16[2,2560,128]{2,1,0:T(8,128)(2,1)S(1)}, bf16[2,2560,128]{2,1,0:T(8,128)(2,1)S(1)}, u32[]{:S(2)}, u32[]{:S(2)}) collective-permute-start(bf16[2,2560,128]{2,1,0:T(8,128)(2,1)S(1)} %pad_maximum_fusion.3.refs_6_), channel_id=1, source_target_pairs={{0,24},{1,97},{2,26},{3,99},{4,28},{5,101},{6,30},{7,103},{8,0},{9... | collective-permute-start | bytes 3932168 | tf_op jit(solution)/shard_map/ppermute | solution.py:196
  146.0 12.9 %collective-permute-start.19 = (bf16[2,2,1280,128]{3,2,1,0:T(8,128)(2,1)S(1)}, bf16[2,2,1280,128]{3,2,1,0:T(8,128)(2,1)S(1)}, u32[]{:S(2)}, u32[]{:S(2)}) collective-permute-start(bf16[2,2,1280,128]{3,2,1,0:T(8,128)(2,1)S(1)} %pad_maximum_fusion.refs_1_), channel_id=1, source_target_pairs={{0,1},{1,0},{2,3},{3,2},{4,5},{5,4},{6,7},{7,6},{8,9},{9,8},{10,11... | collective-permute-start | bytes 3932168 | tf_op jit(solution)/shard_map/ppermute | solution.py:235
  146.0 26.9 %collective-permute-start.25 = (bf16[2,2560,128]{2,1,0:T(8,128)(2,1)S(1)}, bf16[2,2560,128]{2,1,0:T(8,128)(2,1)S(1)}, u32[]{:S(2)}, u32[]{:S(2)}) collective-permute-start(bf16[2,2560,128]{2,1,0:T(8,128)(2,1)S(1)} %collective-permute-done.23.refs_9_), channel_id=1, source_target_pairs={{0,24},{1,97},{2,26},{3,99},{4,28},{5,101},{6,30},{7,103},{8,0},{9... | collective-permute-start | bytes 3932168 | tf_op jit(solution)/shard_map/ppermute | solution.py:196
  148.6 24.3 %collective-permute-start.20 = (bf16[2,2,1280,128]{3,2,1,0:T(8,128)(2,1)S(1)}, bf16[2,2,1280,128]{3,2,1,0:T(8,128)(2,1)S(1)}, u32[]{:S(2)}, u32[]{:S(2)}) collective-permute-start(bf16[2,2,1280,128]{3,2,1,0:T(8,128)(2,1)S(1)} %pad_maximum_fusion.1.refs_2_), channel_id=1, source_target_pairs={{0,1},{1,0},{2,3},{3,2},{4,5},{5,4},{6,7},{7,6},{8,9},{9,8},{10,11... | collective-permute-start | bytes 3932168 | tf_op jit(solution)/shard_map/ppermute | solution.py:235
  149.5 23.4 %collective-permute-start.26 = (bf16[2,2560,128]{2,1,0:T(8,128)(2,1)S(1)}, bf16[2,2560,128]{2,1,0:T(8,128)(2,1)S(1)}, u32[]{:S(2)}, u32[]{:S(2)}) collective-permute-start(bf16[2,2560,128]{2,1,0:T(8,128)(2,1)S(1)} %collective-permute-done.22.refs_8_), channel_id=1, source_target_pairs={{0,8},{1,33},{2,10},{3,35},{4,12},{5,37},{6,14},{7,39},{8,16},{9,4... | collective-permute-start | bytes 3932168 | tf_op jit(solution)/shard_map/ppermute | solution.py:196

commit v6 on v5

--- a/solution.py
+++ b/solution.py
@@ -223,14 +223,16 @@
     far_a, far_b = shift_turned(high[:middle], False, -1), shift_turned(low[middle:], False, 1)
     near = jnp.stack([local, low])
     near_low, near_high = shift_turned(near, True, 1), shift_turned(near, True, -1)
-    far_a, far_b, rows = stage((far_a, far_b, rows))
     rows = jnp.stack([lax.ppermute(rows[t], ALL_AXES, pairs[t][1]) for t in range(2)])
     far = jnp.stack([high, jnp.concatenate([far_a, far_b])])
+    near_low, near_high, far, rows = stage((near_low, near_high, far, rows))
 
     rows_low, rows_high = shift(rows, "x", 1), shift(rows, "x", -1)
     far_low, far_high = shift_turned(far, True, 1), shift_turned(far, True, -1)
+    far_low, far_high, rows_low, rows_high = stage((far_low, far_high, rows_low, rows_high))
+
+    near_far, far_far = shift_turned(near_high, True, -1), shift_turned(far_low, True, 1)
     rows_far = jnp.stack([shift(rows_high[0], "x", -1), shift(rows_low[1], "x", 1)])
-    near_far, far_far = shift_turned(near_high, True, -1), shift_turned(far_low, True, 1)
     rows_near, rows_far = jnp.stack([rows, rows_low]), jnp.stack([rows_high, rows_far])
     rows = [rows_near, rows_far, lax.ppermute(rows_near, "core", SWAP), lax.ppermute(rows_far, "core", SWAP)]
     return [near, far, near_low, far_low, near_high, far_high, near_far, far_far], rows

time: 194 us -> 193 us (level)
  starting transfers between devices: 47.7 us -> 45.3 us
    ppermute x10, waiting for transfers between devices: 28.1 us -> 16.1 us  [shift_turned(): return lax.ppermute(value, ALL_AXES, pairs)]
    ppermute x10, starting transfers between devices: 24.5 us -> 15 us  [shift(): return lax.ppermute(value, axis, [(i, (i + by) % 4) for i in range(4)])]
    ppermute x2, waiting for transfers between devices: 6.02 us -> 15.1 us  [gather_both(): lax.ppermute(rows[t], ALL_AXES, pairs[t][1])]
    ppermute x10, starting transfers between devices: 14.8 us -> 20 us  [shift_turned(): return lax.ppermute(value, ALL_AXES, pairs)]
    ppermute x10, waiting for transfers between devices: 30.8 us -> 34.5 us  [shift(): return lax.ppermute(value, axis, [(i, (i + by) % 4) for i in range(4)])]
where the time goes in v6:
time: 193 us; the launch traced here: 192 us
  waiting for transfers between devices  75.7 us (39%)
  starting transfers between devices  45.3 us (23%)
  blocking collectives  36.5 us (19%)
  Pallas kernels  30.8 us (16%)
  other arithmetic  2.21 us (1%)
    all_to_all x1, blocking collectives, shards(): lax.all_to_all(outgoing, AUX_AXES, split_axis=0, concat_axis=0, tiled=True)  36.5 us
    ppermute x10, waiting for transfers between devices, shift(): return lax.ppermute(value, axis, [(i, (i + by) % 4) for i in range(4)])  34.5 us
    pallas_call x1, Pallas kernels, exchange_block(): pl.pallas_call(lambda *refs: exchange_kernel(*refs, factor=1.0 / depth),...  20.3 us
    ppermute x10, starting transfers between devices, shift_turned(): return lax.ppermute(value, ALL_AXES, pairs)  20 us
    ppermute x10, waiting for transfers between devices, shift_turned(): return lax.ppermute(value, ALL_AXES, pairs)  16.1 us
    ppermute x2, waiting for transfers between devices, gather_both(): lax.ppermute(rows[t], ALL_AXES, pairs[t][1])  15.1 us
    ppermute x10, starting transfers between devices, shift(): return lax.ppermute(value, axis, [(i, (i + by) % 4) for i in range(4)])  15 us
    ppermute x2, waiting for transfers between devices, gather_both(): lax.ppermute(jnp.where(turned, halves[1 - t], halves[t]), ALL_AXES, pairs...  7.57 us
  transfers between devices with their start and end apart: 27, of which 14 were waited for; matrix products, arithmetic and copies ran while one was open for 2% of the time, Pallas kernels for 0%

profile of v6, /device:TPU:0, one launch (start us, length us, event | category | flops | bytes accessed | tf_op | source)
XLA Modules:
  0.0 191.9 jit_solution(695496242300283397)
XLA Ops:
  0.0 7.2 %half_transform.1 = bf16[256,32,128]{2,1,0:T(8,128)(2,1)} custom-call(s32[1]{0:T(128)} %bitcast.20.self_ref, s32[128,128]{1,0:T(8,128)} %bitcast.123, s32[128,128]{1,0:T(8,128)} %bitcast.125, bf16[128,4,32,128]{3,2,1,0:T(8,128)(2,1)} %tiles_ref.1, bf16[32,20480]{1,0:T(8,128)(2,1)} %orbital_ref.1, s32[32,160]{1,0:T(8,128)} %support_ref.1), custom_call_target="tpu_custom_call" | custom-call | tf_op jit(solution)/shard_map/half_transform/pallas_call | solution.py:71
  7.2 36.5 %all_to_all.5.own_ref = bf16[256,32,128]{2,1,0:T(8,128)(2,1)S(1)} all-to-all(bf16[256,32,128]{2,1,0:T(8,128)(2,1)} %half_transform.1), channel_id=1, replica_groups=mesh['z'=4,'y'=4,'x'=4,'core'=2] {'z','y'}, dimensions={0} | all-to-all | bytes 4194304 | tf_op jit(solution)/shard_map/all_to_all | solution.py:360
  43.7 0.0 collective-permute-start
  43.8 0.7 constant_dynamic-slice_fusion.1
  44.5 0.2 convert_reduce_fusion
  44.7 0.2 reduce_window_sum.11
  44.9 0.1 convolution_convert_fusion
  45.0 0.1 fusion.20
  45.1 0.5 select_reduce_fusion.list_ref
  45.7 2.4 %collective-permute-done.other_ref = bf16[256,32,128]{2,1,0:T(8,128)(2,1)} collective-permute-done((bf16[256,32,128]{2,1,0:T(8,128)(2,1)S(1)}, bf16[256,32,128]{2,1,0:T(8,128)(2,1)}, u32[]{:S(2)}, u32[]{:S(2)}) %collective-permute-start) | collective-permute-done | bytes 2097184 | tf_op jit(solution)/shard_map/ppermute | solution.py:369
  48.0 3.3 %sum_slots.1 = (bf16[80,32,128]{2,1,0:T(8,128)(2,1)S(1)}, bf16[40,32,128]{2,1,0:T(8,128)(2,1)S(1)}, bf16[40,32,128]{2,1,0:T(8,128)(2,1)S(1)}, bf16[40,32,128]{2,...) custom-call(s32[2]{0:T(128)S(1)} %get-tuple-element.44.count_ref, ...), custom_call_target="tpu_custom_call" | custom-call | tf_op jit(solution)/shard_map/sum_slots/pallas_call | solution.py:126
  51.3 1.5 collective-permute-start.1
  52.8 1.8 collective-permute-start.5
  54.6 0.2 collective-permute-start.3
  54.8 3.0 %collective-permute-start.4 = (bf16[40,32,128]{2,1,0:T(8,128)(2,1)S(1)}, bf16[40,32,128]{2,1,0:T(8,128)(2,1)S(1)}, u32[]{:S(2)}, u32[]{:S(2)}) collective-permute-start(bf16[40,32,128]{2,1,0:T(8,128)(2,1)S(1)} %get-tuple-element.28), channel_id=1, source_target_pairs={{0,6},{2,0},{4,2},{6,4},{1,7},{3,1},{5,3},{7,5},{8,14},{10,8},{12,... | collective-permute-start | bytes 983048 | tf_op jit(solution)/shard_map/ppermute | solution.py:167
  57.9 5.3 %collective-permute-done.1 = bf16[40,32,128]{2,1,0:T(8,128)(2,1)S(1)} collective-permute-done((bf16[40,32,128]{2,1,0:T(8,128)(2,1)S(1)}, bf16[40,32,128]{2,1,0:T(8,128)(2,1)S(1)}, u32[]{:S(2)}, u32[]{:S(2)}) %collective-permute-start.1) | collective-permute-done | bytes 327712 | tf_op jit(solution)/shard_map/ppermute | solution.py:167
  63.2 0.1 add_convert_fusion.2
  63.3 0.3 collective-permute-start.2
  63.5 0.1 add_convert_fusion.1
  63.6 3.1 %collective-permute-start.6 = (bf16[40,32,128]{2,1,0:T(8,128)(2,1)S(1)}, bf16[40,32,128]{2,1,0:T(8,128)(2,1)S(1)}, u32[]{:S(2)}, u32[]{:S(2)}) collective-permute-start(bf16[40,32,128]{2,1,0:T(8,128)(2,1)S(1)} %add_convert_fusion.1), channel_id=1, source_target_pairs={{0,6},{2,0},{4,2},{6,4},{1,7},{3,1},{5,3},{7,5},{8,14},{10,8},{12,... | collective-permute-start | bytes 983048 | tf_op jit(solution)/shard_map/ppermute | solution.py:167
  66.7 3.5 %collective-permute-done.3 = bf16[40,32,128]{2,1,0:T(8,128)(2,1)S(1)} collective-permute-done((bf16[40,32,128]{2,1,0:T(8,128)(2,1)S(1)}, bf16[40,32,128]{2,1,0:T(8,128)(2,1)S(1)}, u32[]{:S(2)}, u32[]{:S(2)}) %collective-permute-start.3) | collective-permute-done | bytes 327712 | tf_op jit(solution)/shard_map/ppermute | solution.py:167
  70.2 0.2 collective-permute-done.4
  70.4 5.9 %collective-permute-done.2 = bf16[40,32,128]{2,1,0:T(8,128)(2,1)S(1)} collective-permute-done((bf16[40,32,128]{2,1,0:T(8,128)(2,1)S(1)}, bf16[40,32,128]{2,1,0:T(8,128)(2,1)S(1)}, u32[]{:S(2)}, u32[]{:S(2)}) %collective-permute-start.2) | collective-permute-done | bytes 327712 | tf_op jit(solution)/shard_map/ppermute | solution.py:167
  76.3 0.1 collective-permute-done.6
  76.4 0.3 add_convert_fusion
  76.7 1.0 collective-permute-start.8
  77.7 1.1 collective-permute-start.7
  78.8 0.7 collective-permute-start.9
  79.5 3.2 %collective-permute-start.10 = (bf16[1280,128]{1,0:T(8,128)(2,1)S(1)}, bf16[1280,128]{1,0:T(8,128)(2,1)S(1)}, u32[]{:S(2)}, u32[]{:S(2)}) collective-permute-start(bf16[1280,128]{1,0:T(8,128)(2,1)S(1)} %bitcast.121), channel_id=1, source_target_pairs={{0,2},{1,7},{2,4},{3,1},{4,6},{5,3},{6,0},{7,5},{8,10},{9,15},{10,... | collective-permute-start | bytes 983048 | tf_op jit(solution)/shard_map/ppermute | solution.py:220
  82.8 7.6 %collective-permute-done.10 = bf16[1280,128]{1,0:T(8,128)(2,1)S(1)} collective-permute-done((bf16[1280,128]{1,0:T(8,128)(2,1)S(1)}, bf16[1280,128]{1,0:T(8,128)(2,1)S(1)}, u32[]{:S(2)}, u32[]{:S(2)}) %collective-permute-start.10) | collective-permute-done | bytes 327712 | tf_op jit(solution)/shard_map/ppermute | solution.py:220
  90.3 0.7 collective-permute-start.15
  91.0 0.1 pad_maximum_fusion.refs_5_
  91.2 5.1 %collective-permute-start.12 = (bf16[2,2560,128]{2,1,0:T(8,128)(2,1)S(1)}, bf16[2,2560,128]{2,1,0:T(8,128)(2,1)S(1)}, u32[]{:S(2)}, u32[]{:S(2)}) collective-permute-start(bf16[2,2560,128]{2,1,0:T(8,128)(2,1)S(1)} %pad_maximum_fusion.refs_5_), channel_id=1, source_target_pairs={{0,24},{1,97},{2,26},{3,99},{4,28},{5,101},{6,30},{7,103},{8,0},{9... | collective-permute-start | bytes 3932168 | tf_op jit(solution)/shard_map/ppermute | solution.py:196
  96.2 0.0 collective-permute-start.11
  96.2 3.6 %collective-permute-start.16 = (bf16[1280,128]{1,0:T(8,128)(2,1)S(1)}, bf16[1280,128]{1,0:T(8,128)(2,1)S(1)}, u32[]{:S(2)}, u32[]{:S(2)}) collective-permute-start(bf16[1280,128]{1,0:T(8,128)(2,1)S(1)} %collective-permute-done.10), channel_id=1, source_target_pairs={{2,10},{7,30},{4,44},{1,56},{6,78},{3,90},{0,104},{5,124},{10,11},... | collective-permute-start | bytes 983048 | tf_op jit(solution)/shard_map/ppermute | solution.py:226
  99.9 0.6 collective-permute-start.13
  100.5 0.0 collective-permute-done.15
  100.5 7.5 %collective-permute-start.14 = (bf16[1280,128]{1,0:T(8,128)(2,1)S(1)}, bf16[1280,128]{1,0:T(8,128)(2,1)S(1)}, u32[]{:S(2)}, u32[]{:S(2)}) collective-permute-start(bf16[1280,128]{1,0:T(8,128)(2,1)S(1)} %slice.31), channel_id=1, source_target_pairs={{0,32},{1,9},{2,34},{3,11},{4,36},{5,13},{6,38},{7,15},{8,40},{9,1... | collective-permute-start | bytes 983048 | tf_op jit(solution)/shard_map/ppermute | solution.py:196
  108.1 15.1 %collective-permute-done.16 = bf16[1280,128]{1,0:T(8,128)(2,1)S(1)} collective-permute-done((bf16[1280,128]{1,0:T(8,128)(2,1)S(1)}, bf16[1280,128]{1,0:T(8,128)(2,1)S(1)}, u32[]{:S(2)}, u32[]{:S(2)}) %collective-permute-start.16) | collective-permute-done | bytes 327712 | tf_op jit(solution)/shard_map/ppermute | solution.py:226
  123.1 0.1 pad_maximum_fusion.4
  123.2 0.0 collective-permute-done.14
  123.3 0.1 pad_maximum_fusion.1.refs_6_
  123.4 0.0 collective-permute-done.12.refs_9_
  123.4 2.2 %collective-permute-start.18 = (bf16[2,2560,128]{2,1,0:T(8,128)(2,1)S(1)}, bf16[2,2560,128]{2,1,0:T(8,128)(2,1)S(1)}, u32[]{:S(2)}, u32[]{:S(2)}) collective-permute-start(bf16[2,2560,128]{2,1,0:T(8,128)(2,1)S(1)} %pad_maximum_fusion.1.refs_6_), channel_id=1, source_target_pairs={{0,24},{1,97},{2,26},{3,99},{4,28},{5,101},{6,30},{7,103},{8,0},{9... | collective-permute-start | bytes 3932168 | tf_op jit(solution)/shard_map/ppermute | solution.py:196
  125.6 0.0 collective-permute-start.17
  125.6 3.0 %collective-permute-start.20 = (bf16[2,1280,128]{2,1,0:T(8,128)(2,1)S(1)}, bf16[2,1280,128]{2,1,0:T(8,128)(2,1)S(1)}, u32[]{:S(2)}, u32[]{:S(2)}) collective-permute-start(bf16[2,1280,128]{2,1,0:T(8,128)(2,1)S(1)} %pad_maximum_fusion.4), channel_id=1, source_target_pairs={{0,6},{2,0},{4,2},{6,4},{1,7},{3,1},{5,3},{7,5},{8,14},{10,8},{12,... | collective-permute-start | bytes 1966088 | tf_op jit(solution)/shard_map/ppermute | solution.py:167
  128.6 0.0 collective-permute-start.19
  128.6 10.3 %collective-permute-done.20 = bf16[2,1280,128]{2,1,0:T(8,128)(2,1)S(1)} collective-permute-done((bf16[2,1280,128]{2,1,0:T(8,128)(2,1)S(1)}, bf16[2,1280,128]{2,1,0:T(8,128)(2,1)S(1)}, u32[]{:S(2)}, u32[]{:S(2)}) %collective-permute-start.20) | collective-permute-done | bytes 655392 | tf_op jit(solution)/shard_map/ppermute | solution.py:167
  138.9 3.9 %collective-permute-done.19 = bf16[2,1280,128]{2,1,0:T(8,128)(2,1)S(1)} collective-permute-done((bf16[2,1280,128]{2,1,0:T(8,128)(2,1)S(1)}, bf16[2,1280,128]{2,1,0:T(8,128)(2,1)S(1)}, u32[]{:S(2)}, u32[]{:S(2)}) %collective-permute-start.19) | collective-permute-done | bytes 655392 | tf_op jit(solution)/shard_map/ppermute | solution.py:167
  142.8 5.1 %collective-permute-done.17.refs_8_ = bf16[2,2560,128]{2,1,0:T(8,128)(2,1)S(1)} collective-permute-done((bf16[2,2560,128]{2,1,0:T(8,128)(2,1)S(1)}, bf16[2,2560,128]{2,1,0:T(8,128)(2,1)S(1)}, u32[]{:S(2)}, u32[]{:S(2)}) %collective-permute-start.17) | collective-permute-done | bytes 1310752 | tf_op jit(solution)/shard_map/ppermute | solution.py:196
  148.0 0.1 collective-permute-start.21
  148.1 2.0 %collective-permute-start.22 = (bf16[1280,128]{1,0:T(8,128)(2,1)S(1)}, bf16[1280,128]{1,0:T(8,128)(2,1)S(1)}, u32[]{:S(2)}, u32[]{:S(2)}) collective-permute-start(bf16[1280,128]{1,0:T(8,128)(2,1)S(1)} %slice_bitcast_fusion), channel_id=1, source_target_pairs={{0,2},{2,4},{4,6},{6,0},{1,3},{3,5},{5,7},{7,1},{8,10},{10,12},{12... | collective-permute-start | bytes 983048 | tf_op jit(solution)/shard_map/ppermute | solution.py:167
  150.1 2.0 %collective-permute-start.25 = (bf16[2,2560,128]{2,1,0:T(8,128)(2,1)S(1)}, bf16[2,2560,128]{2,1,0:T(8,128)(2,1)S(1)}, u32[]{:S(2)}, u32[]{:S(2)}) collective-permute-start(bf16[2,2560,128]{2,1,0:T(8,128)(2,1)S(1)} %collective-permute-done.12.refs_9_), channel_id=1, source_target_pairs={{0,24},{1,97},{2,26},{3,99},{4,28},{5,101},{6,30},{7,103},{8,0},{9... | collective-permute-start | bytes 3932168 | tf_op jit(solution)/shard_map/ppermute | solution.py:196
  152.1 0.1 pad_maximum_fusion.2.refs_1_
  152.3 0.3 collective-permute-start.23
  152.5 0.4 collective-permute-start.26
  152.9 5.3 %collective-permute-done.21 = bf16[1280,128]{1,0:T(8,128)(2,1)S(1)} collective-permute-done((bf16[1280,128]{1,0:T(8,128)(2,1)S(1)}, bf16[1280,128]{1,0:T(8,128)(2,1)S(1)}, u32[]{:S(2)}, u32[]{:S(2)}) %collective-permute-start.21) | collective-permute-done | bytes 327712 | tf_op jit(solution)/shard_map/ppermute | solution.py:167
  158.2 0.1 maximum_bitcast_fusion.1
  158.3 0.1 pad_maximum_fusion.3.refs_2_
  158.4 1.9 %collective-permute-start.24 = (bf16[2,2,1280,128]{3,2,1,0:T(8,128)(2,1)S(1)}, bf16[2,2,1280,128]{3,2,1,0:T(8,128)(2,1)S(1)}, u32[]{:S(2)}, u32[]{:S(2)}) collective-permute-start(bf16[2,2,1280,128]{3,2,1,0:T(8,128)(2,1)S(1)} %pad_maximum_fusion.3.refs_2_), channel_id=1, source_target_pairs={{0,1},{1,0},{2,3},{3,2},{4,5},{5,4},{6,7},{7,6},{8,9},{9,8},{10,11... | collective-permute-start | bytes 3932168 | tf_op jit(solution)/shard_map/ppermute | solution.py:237
  160.4 0.1 pad_add_fusion.refs_0_
  160.4 7.6 %collective-permute-done.25.refs_11_ = bf16[2,2560,128]{2,1,0:T(8,128)(2,1)S(1)} collective-permute-done((bf16[2,2560,128]{2,1,0:T(8,128)(2,1)S(1)}, bf16[2,2560,128]{2,1,0:T(8,128)(2,1)S(1)}, u32[]{:S(2)}, u32[]{:S(2)}) %collective-permute-start.25) | collective-permute-done | bytes 1310752 | tf_op jit(solution)/shard_map/ppermute | solution.py:196
  168.0 3.4 %collective-permute-done.26.refs_12_ = bf16[2,2560,128]{2,1,0:T(8,128)(2,1)S(1)} collective-permute-done((bf16[2,2560,128]{2,1,0:T(8,128)(2,1)S(1)}, bf16[2,2560,128]{2,1,0:T(8,128)(2,1)S(1)}, u32[]{:S(2)}, u32[]{:S(2)}) %collective-permute-start.26) | collective-permute-done | bytes 1310752 | tf_op jit(solution)/shard_map/ppermute | solution.py:196
  171.4 20.3 %exchange.1 = f32[1280,2560]{1,0:T(8,128)} custom-call(s32[4]{0:T(128)S(1)} %pad_add_fusion.refs_0_, bf16[2,2,1280,128]{3,2,1,0:T(8,128)(2,1)S(1)} %pad_maximum_fusion.2.refs_1_, bf16[2,2,1280,128]{3,2,1,0:T(8,128)(2,1)S(1)} %pad_maximum_fusion.3.refs_2_, bf16[2,2,1280,128]{3,2,1,0:T(8,128)(2,1)S(1)} %collective-permute-done.23.refs_3_, ...), custom_call_target="tpu_custom_call" | custom-call | tf_op jit(solution)/shard_map/exchange/pallas_call | solution.py:317
  (24 shorter events, 0.3 us)
Async XLA Ops:
  0.0 43.7 %copy-start = (s32[16384]{0:T(1024)S(1)}, s32[16384]{0:T(1024)}, u32[]{:S(2)}) copy-start(s32[16384]{0:T(1024)} %param.8) | copy-start | bytes 196612
  43.7 4.3 %collective-permute-start = (bf16[256,32,128]{2,1,0:T(8,128)(2,1)S(1)}, bf16[256,32,128]{2,1,0:T(8,128)(2,1)}, u32[]{:S(2)}, u32[]{:S(2)}) collective-permute-start(bf16[256,32,128]{2,1,0:T(8,128)(2,1)S(1)} %all_to_all.5.own_ref), channel_id=1, source_target_pairs={{0,1},{1,0},{2,3},{3,2},{4,5},{5,4},{6,7},{7,6},{8,9},{9,8},{10,11... | collective-permute-start | bytes 6291464 | tf_op jit(solution)/shard_map/ppermute | solution.py:369
  51.3 11.9 %collective-permute-start.1 = (bf16[40,32,128]{2,1,0:T(8,128)(2,1)S(1)}, bf16[40,32,128]{2,1,0:T(8,128)(2,1)S(1)}, u32[]{:S(2)}, u32[]{:S(2)}) collective-permute-start(bf16[40,32,128]{2,1,0:T(8,128)(2,1)S(1)} %get-tuple-element.26), channel_id=1, source_target_pairs={{0,2},{2,4},{4,6},{6,0},{1,3},{3,5},{5,7},{7,1},{8,10},{10,12},{12... | collective-permute-start | bytes 983048 | tf_op jit(solution)/shard_map/ppermute | solution.py:167
  52.8 10.7 %collective-permute-start.5 = (bf16[40,32,128]{2,1,0:T(8,128)(2,1)S(1)}, bf16[40,32,128]{2,1,0:T(8,128)(2,1)S(1)}, u32[]{:S(2)}, u32[]{:S(2)}) collective-permute-start(bf16[40,32,128]{2,1,0:T(8,128)(2,1)S(1)} %get-tuple-element.30), channel_id=1, source_target_pairs={{0,6},{2,0},{4,2},{6,4},{1,7},{3,1},{5,3},{7,5},{8,14},{10,8},{12,... | collective-permute-start | bytes 983048 | tf_op jit(solution)/shard_map/ppermute | solution.py:167
  54.6 15.6 %collective-permute-start.3 = (bf16[40,32,128]{2,1,0:T(8,128)(2,1)S(1)}, bf16[40,32,128]{2,1,0:T(8,128)(2,1)S(1)}, u32[]{:S(2)}, u32[]{:S(2)}) collective-permute-start(bf16[40,32,128]{2,1,0:T(8,128)(2,1)S(1)} %get-tuple-element.27), channel_id=1, source_target_pairs={{0,2},{2,4},{4,6},{6,0},{1,3},{3,5},{5,7},{7,1},{8,10},{10,12},{12... | collective-permute-start | bytes 983048 | tf_op jit(solution)/shard_map/ppermute | solution.py:167
  54.8 15.6 %collective-permute-start.4 = (bf16[40,32,128]{2,1,0:T(8,128)(2,1)S(1)}, bf16[40,32,128]{2,1,0:T(8,128)(2,1)S(1)}, u32[]{:S(2)}, u32[]{:S(2)}) collective-permute-start(bf16[40,32,128]{2,1,0:T(8,128)(2,1)S(1)} %get-tuple-element.28), channel_id=1, source_target_pairs={{0,6},{2,0},{4,2},{6,4},{1,7},{3,1},{5,3},{7,5},{8,14},{10,8},{12,... | collective-permute-start | bytes 983048 | tf_op jit(solution)/shard_map/ppermute | solution.py:167
  63.3 13.0 %collective-permute-start.2 = (bf16[40,32,128]{2,1,0:T(8,128)(2,1)S(1)}, bf16[40,32,128]{2,1,0:T(8,128)(2,1)S(1)}, u32[]{:S(2)}, u32[]{:S(2)}) collective-permute-start(bf16[40,32,128]{2,1,0:T(8,128)(2,1)S(1)} %add_convert_fusion.2), channel_id=1, source_target_pairs={{0,2},{2,4},{4,6},{6,0},{1,3},{3,5},{5,7},{7,1},{8,10},{10,12},{12... | collective-permute-start | bytes 983048 | tf_op jit(solution)/shard_map/ppermute | solution.py:167
  63.6 12.8 %collective-permute-start.6 = (bf16[40,32,128]{2,1,0:T(8,128)(2,1)S(1)}, bf16[40,32,128]{2,1,0:T(8,128)(2,1)S(1)}, u32[]{:S(2)}, u32[]{:S(2)}) collective-permute-start(bf16[40,32,128]{2,1,0:T(8,128)(2,1)S(1)} %add_convert_fusion.1), channel_id=1, source_target_pairs={{0,6},{2,0},{4,2},{6,4},{1,7},{3,1},{5,3},{7,5},{8,14},{10,8},{12,... | collective-permute-start | bytes 983048 | tf_op jit(solution)/shard_map/ppermute | solution.py:167
  76.7 13.7 %collective-permute-start.8 = (bf16[2560,128]{1,0:T(8,128)(2,1)S(1)}, bf16[2560,128]{1,0:T(8,128)(2,1)S(1)}, u32[]{:S(2)}, u32[]{:S(2)}) collective-permute-start(bf16[2560,128]{1,0:T(8,128)(2,1)S(1)} %bitcast.109), channel_id=1, source_target_pairs={{0,96},{1,25},{2,98},{3,27},{4,100},{5,29},{6,102},{7,31},{8,104},... | collective-permute-start | bytes 1966088 | tf_op jit(solution)/shard_map/ppermute | solution.py:196
  77.7 12.7 %collective-permute-start.7 = (bf16[2560,128]{1,0:T(8,128)(2,1)S(1)}, bf16[2560,128]{1,0:T(8,128)(2,1)S(1)}, u32[]{:S(2)}, u32[]{:S(2)}) collective-permute-start(bf16[2560,128]{1,0:T(8,128)(2,1)S(1)} %bitcast.110), channel_id=1, source_target_pairs={{0,32},{1,9},{2,34},{3,11},{4,36},{5,13},{6,38},{7,15},{8,40},{9,1... | collective-permute-start | bytes 1966088 | tf_op jit(solution)/shard_map/ppermute | solution.py:196
  78.8 3.9 %collective-permute-start.9 = (bf16[1280,128]{1,0:T(8,128)(2,1)S(1)}, bf16[1280,128]{1,0:T(8,128)(2,1)S(1)}, u32[]{:S(2)}, u32[]{:S(2)}) collective-permute-start(bf16[1280,128]{1,0:T(8,128)(2,1)S(1)} %bitcast.122), channel_id=1, source_target_pairs={{0,0},{1,5},{2,2},{3,7},{4,4},{5,1},{6,6},{7,3},{8,8},{9,13},{10,1... | collective-permute-start | bytes 983048 | tf_op jit(solution)/shard_map/ppermute | solution.py:220
  79.5 10.8 %collective-permute-start.10 = (bf16[1280,128]{1,0:T(8,128)(2,1)S(1)}, bf16[1280,128]{1,0:T(8,128)(2,1)S(1)}, u32[]{:S(2)}, u32[]{:S(2)}) collective-permute-start(bf16[1280,128]{1,0:T(8,128)(2,1)S(1)} %bitcast.121), channel_id=1, source_target_pairs={{0,2},{1,7},{2,4},{3,1},{4,6},{5,3},{6,0},{7,5},{8,10},{9,15},{10,... | collective-permute-start | bytes 983048 | tf_op jit(solution)/shard_map/ppermute | solution.py:220
  90.3 10.2 %collective-permute-start.15 = (bf16[1280,128]{1,0:T(8,128)(2,1)S(1)}, bf16[1280,128]{1,0:T(8,128)(2,1)S(1)}, u32[]{:S(2)}, u32[]{:S(2)}) collective-permute-start(bf16[1280,128]{1,0:T(8,128)(2,1)S(1)} %collective-permute-done.9), channel_id=1, source_target_pairs={{0,0},{5,20},{2,34},{7,54},{4,68},{1,80},{6,102},{3,114},{8,1},{13... | collective-permute-start | bytes 983048 | tf_op jit(solution)/shard_map/ppermute | solution.py:226
  91.2 32.2 %collective-permute-start.12 = (bf16[2,2560,128]{2,1,0:T(8,128)(2,1)S(1)}, bf16[2,2560,128]{2,1,0:T(8,128)(2,1)S(1)}, u32[]{:S(2)}, u32[]{:S(2)}) collective-permute-start(bf16[2,2560,128]{2,1,0:T(8,128)(2,1)S(1)} %pad_maximum_fusion.refs_5_), channel_id=1, source_target_pairs={{0,24},{1,97},{2,26},{3,99},{4,28},{5,101},{6,30},{7,103},{8,0},{9... | collective-permute-start | bytes 3932168 | tf_op jit(solution)/shard_map/ppermute | solution.py:196
  96.2 27.1 %collective-permute-start.11 = (bf16[2,2560,128]{2,1,0:T(8,128)(2,1)S(1)}, bf16[2,2560,128]{2,1,0:T(8,128)(2,1)S(1)}, u32[]{:S(2)}, u32[]{:S(2)}) collective-permute-start(bf16[2,2560,128]{2,1,0:T(8,128)(2,1)S(1)} %pad_maximum_fusion.refs_5_), channel_id=1, source_target_pairs={{0,8},{1,33},{2,10},{3,35},{4,12},{5,37},{6,14},{7,39},{8,16},{9,4... | collective-permute-start | bytes 3932168 | tf_op jit(solution)/shard_map/ppermute | solution.py:196
  96.2 26.9 %collective-permute-start.16 = (bf16[1280,128]{1,0:T(8,128)(2,1)S(1)}, bf16[1280,128]{1,0:T(8,128)(2,1)S(1)}, u32[]{:S(2)}, u32[]{:S(2)}) collective-permute-start(bf16[1280,128]{1,0:T(8,128)(2,1)S(1)} %collective-permute-done.10), channel_id=1, source_target_pairs={{2,10},{7,30},{4,44},{1,56},{6,78},{3,90},{0,104},{5,124},{10,11},... | collective-permute-start | bytes 983048 | tf_op jit(solution)/shard_map/ppermute | solution.py:226
  99.9 23.3 %collective-permute-start.13 = (bf16[1280,128]{1,0:T(8,128)(2,1)S(1)}, bf16[1280,128]{1,0:T(8,128)(2,1)S(1)}, u32[]{:S(2)}, u32[]{:S(2)}) collective-permute-start(bf16[1280,128]{1,0:T(8,128)(2,1)S(1)} %slice.30), channel_id=1, source_target_pairs={{0,96},{1,25},{2,98},{3,27},{4,100},{5,29},{6,102},{7,31},{8,104},... | collective-permute-start | bytes 983048 | tf_op jit(solution)/shard_map/ppermute | solution.py:196
  100.5 22.7 %collective-permute-start.14 = (bf16[1280,128]{1,0:T(8,128)(2,1)S(1)}, bf16[1280,128]{1,0:T(8,128)(2,1)S(1)}, u32[]{:S(2)}, u32[]{:S(2)}) collective-permute-start(bf16[1280,128]{1,0:T(8,128)(2,1)S(1)} %slice.31), channel_id=1, source_target_pairs={{0,32},{1,9},{2,34},{3,11},{4,36},{5,13},{6,38},{7,15},{8,40},{9,1... | collective-permute-start | bytes 983048 | tf_op jit(solution)/shard_map/ppermute | solution.py:196
  123.4 19.4 %collective-permute-start.18 = (bf16[2,2560,128]{2,1,0:T(8,128)(2,1)S(1)}, bf16[2,2560,128]{2,1,0:T(8,128)(2,1)S(1)}, u32[]{:S(2)}, u32[]{:S(2)}) collective-permute-start(bf16[2,2560,128]{2,1,0:T(8,128)(2,1)S(1)} %pad_maximum_fusion.1.refs_6_), channel_id=1, source_target_pairs={{0,24},{1,97},{2,26},{3,99},{4,28},{5,101},{6,30},{7,103},{8,0},{9... | collective-permute-start | bytes 3932168 | tf_op jit(solution)/shard_map/ppermute | solution.py:196
  125.6 22.4 %collective-permute-start.17 = (bf16[2,2560,128]{2,1,0:T(8,128)(2,1)S(1)}, bf16[2,2560,128]{2,1,0:T(8,128)(2,1)S(1)}, u32[]{:S(2)}, u32[]{:S(2)}) collective-permute-start(bf16[2,2560,128]{2,1,0:T(8,128)(2,1)S(1)} %pad_maximum_fusion.1.refs_6_), channel_id=1, source_target_pairs={{0,8},{1,33},{2,10},{3,35},{4,12},{5,37},{6,14},{7,39},{8,16},{9,4... | collective-permute-start | bytes 3932168 | tf_op jit(solution)/shard_map/ppermute | solution.py:196
  125.6 13.3 %collective-permute-start.20 = (bf16[2,1280,128]{2,1,0:T(8,128)(2,1)S(1)}, bf16[2,1280,128]{2,1,0:T(8,128)(2,1)S(1)}, u32[]{:S(2)}, u32[]{:S(2)}) collective-permute-start(bf16[2,1280,128]{2,1,0:T(8,128)(2,1)S(1)} %pad_maximum_fusion.4), channel_id=1, source_target_pairs={{0,6},{2,0},{4,2},{6,4},{1,7},{3,1},{5,3},{7,5},{8,14},{10,8},{12,... | collective-permute-start | bytes 1966088 | tf_op jit(solution)/shard_map/ppermute | solution.py:167
  128.6 14.2 %collective-permute-start.19 = (bf16[2,1280,128]{2,1,0:T(8,128)(2,1)S(1)}, bf16[2,1280,128]{2,1,0:T(8,128)(2,1)S(1)}, u32[]{:S(2)}, u32[]{:S(2)}) collective-permute-start(bf16[2,1280,128]{2,1,0:T(8,128)(2,1)S(1)} %pad_maximum_fusion.4), channel_id=1, source_target_pairs={{0,2},{2,4},{4,6},{6,0},{1,3},{3,5},{5,7},{7,1},{8,10},{10,12},{12... | collective-permute-start | bytes 1966088 | tf_op jit(solution)/shard_map/ppermute | solution.py:167
  148.0 10.2 %collective-permute-start.21 = (bf16[1280,128]{1,0:T(8,128)(2,1)S(1)}, bf16[1280,128]{1,0:T(8,128)(2,1)S(1)}, u32[]{:S(2)}, u32[]{:S(2)}) collective-permute-start(bf16[1280,128]{1,0:T(8,128)(2,1)S(1)} %slice_bitcast_fusion.1), channel_id=1, source_target_pairs={{0,6},{2,0},{4,2},{6,4},{1,7},{3,1},{5,3},{7,5},{8,14},{10,8},{12,... | collective-permute-start | bytes 983048 | tf_op jit(solution)/shard_map/ppermute | solution.py:167
  148.1 10.1 %collective-permute-start.22 = (bf16[1280,128]{1,0:T(8,128)(2,1)S(1)}, bf16[1280,128]{1,0:T(8,128)(2,1)S(1)}, u32[]{:S(2)}, u32[]{:S(2)}) collective-permute-start(bf16[1280,128]{1,0:T(8,128)(2,1)S(1)} %slice_bitcast_fusion), channel_id=1, source_target_pairs={{0,2},{2,4},{4,6},{6,0},{1,3},{3,5},{5,7},{7,1},{8,10},{10,12},{12... | collective-permute-start | bytes 983048 | tf_op jit(solution)/shard_map/ppermute | solution.py:167
  150.1 17.9 %collective-permute-start.25 = (bf16[2,2560,128]{2,1,0:T(8,128)(2,1)S(1)}, bf16[2,2560,128]{2,1,0:T(8,128)(2,1)S(1)}, u32[]{:S(2)}, u32[]{:S(2)}) collective-permute-start(bf16[2,2560,128]{2,1,0:T(8,128)(2,1)S(1)} %collective-permute-done.12.refs_9_), channel_id=1, source_target_pairs={{0,24},{1,97},{2,26},{3,99},{4,28},{5,101},{6,30},{7,103},{8,0},{9... | collective-permute-start | bytes 3932168 | tf_op jit(solution)/shard_map/ppermute | solution.py:196
  152.3 15.8 %collective-permute-start.23 = (bf16[2,2,1280,128]{3,2,1,0:T(8,128)(2,1)S(1)}, bf16[2,2,1280,128]{3,2,1,0:T(8,128)(2,1)S(1)}, u32[]{:S(2)}, u32[]{:S(2)}) collective-permute-start(bf16[2,2,1280,128]{3,2,1,0:T(8,128)(2,1)S(1)} %pad_maximum_fusion.2.refs_1_), channel_id=1, source_target_pairs={{0,1},{1,0},{2,3},{3,2},{4,5},{5,4},{6,7},{7,6},{8,9},{9,8},{10,11... | collective-permute-start | bytes 3932168 | tf_op jit(solution)/shard_map/ppermute | solution.py:237
  152.5 18.9 %collective-permute-start.26 = (bf16[2,2560,128]{2,1,0:T(8,128)(2,1)S(1)}, bf16[2,2560,128]{2,1,0:T(8,128)(2,1)S(1)}, u32[]{:S(2)}, u32[]{:S(2)}) collective-permute-start(bf16[2,2560,128]{2,1,0:T(8,128)(2,1)S(1)} %collective-permute-done.17.refs_8_), channel_id=1, source_target_pairs={{0,8},{1,33},{2,10},{3,35},{4,12},{5,37},{6,14},{7,39},{8,16},{9,4... | collective-permute-start | bytes 3932168 | tf_op jit(solution)/shard_map/ppermute | solution.py:196
  158.4 13.0 %collective-permute-start.24 = (bf16[2,2,1280,128]{3,2,1,0:T(8,128)(2,1)S(1)}, bf16[2,2,1280,128]{3,2,1,0:T(8,128)(2,1)S(1)}, u32[]{:S(2)}, u32[]{:S(2)}) collective-permute-start(bf16[2,2,1280,128]{3,2,1,0:T(8,128)(2,1)S(1)} %pad_maximum_fusion.3.refs_2_), channel_id=1, source_target_pairs={{0,1},{1,0},{2,3},{3,2},{4,5},{5,4},{6,7},{7,6},{8,9},{9,8},{10,11... | collective-permute-start | bytes 3932168 | tf_op jit(solution)/shard_map/ppermute | solution.py:237

commit v7 on v6

--- a/solution.py
+++ b/solution.py
@@ -43,25 +43,27 @@
 
     row = lax.bitwise_and(self_ref[0], 7)
     lane = lax.broadcasted_iota(jnp.int32, (tile_rows, width), 1)
-    for index in range(tiles_ref.shape[0]):
-        tile = step * tiles_ref.shape[0] + index
-        block = lax.shift_right_logical(owner_ref[row, tile], 3)
-        rank = count_ref[block]
-        count_ref[block] = rank + 1
-        col = col_ref[row, tile]
-        chosen = orbital_ref[:, pl.ds(pl.multiple_of(col * tile_cols, tile_cols), tile_cols)]
-        product = lax.dot_general(
-            tiles_ref[index].reshape(aux_here * tile_rows, tile_cols),
-            jnp.concatenate([chosen] * aux_here, axis=0),
+    height = aux_here * tile_rows
+    for first in range(0, tiles_ref.shape[0], 2):
+        cols = [col_ref[row, step * tiles_ref.shape[0] + first + turn] for turn in range(2)]
+        chosen = [orbital_ref[:, pl.ds(pl.multiple_of(col * tile_cols, tile_cols), tile_cols)] for col in cols]
+        products = lax.dot_general(
+            tiles_ref[pl.ds(first, 2)].reshape(2 * height, tile_cols),
+            jnp.concatenate([chosen[0]] * aux_here + [chosen[1]] * aux_here, axis=0),
             (((1,), (1,)), ((), ())),
             preferred_element_type=jnp.float32,
         )
-        half = product[:tile_rows]
-        for aux in range(1, aux_here):
-            part = product[aux * tile_rows : (aux + 1) * tile_rows]
-            half = jnp.where(lane >= aux * orbital_count, part, half)
-        kept = kept_ref[pl.ds(col, 1), :] > 0.5
-        out_ref[block * per_block + rank] = jnp.where(kept, half, 0.0).astype(out_ref.dtype)
+        for turn in range(2):
+            product = products[turn * height : (turn + 1) * height, turn * width : (turn + 1) * width]
+            block = lax.shift_right_logical(owner_ref[row, step * tiles_ref.shape[0] + first + turn], 3)
+            rank = count_ref[block]
+            count_ref[block] = rank + 1
+            half = product[:tile_rows]
+            for aux in range(1, aux_here):
+                part = product[aux * tile_rows : (aux + 1) * tile_rows]
+                half = jnp.where(lane >= aux * orbital_count, part, half)
+            kept = kept_ref[pl.ds(cols[turn], 1), :] > 0.5
+            out_ref[block * per_block + rank] = jnp.where(kept, half, 0.0).astype(out_ref.dtype)
 
 
 def half_slots(myself, tiles, owners, cols, orbitals, support, block_count, per_block):

time: 193 us -> 192 us (level)
  transfers between devices with their start and end apart: 27 -> 27, of which waited for: 14 -> 13; matrix products, arithmetic and copies ran while one was open for 2% -> 2% of each run, Pallas kernels for 0% -> 0%
where the time goes in v7:
time: 192 us; the launch traced here: 191 us
  waiting for transfers between devices  76 us (40%)
  starting transfers between devices  44.7 us (23%)
  blocking collectives  36.5 us (19%)
  Pallas kernels  30.6 us (16%)
  other arithmetic  2.21 us (1%)
    all_to_all x1, blocking collectives, shards(): lax.all_to_all(outgoing, AUX_AXES, split_axis=0, concat_axis=0, tiled=True)  36.5 us
    ppermute x10, waiting for transfers between devices, shift(): return lax.ppermute(value, axis, [(i, (i + by) % 4) for i in range(4)])  34.8 us
    pallas_call x1, Pallas kernels, exchange_block(): pl.pallas_call(lambda *refs: exchange_kernel(*refs, factor=1.0 / depth),...  20.5 us
    ppermute x10, starting transfers between devices, shift_turned(): return lax.ppermute(value, ALL_AXES, pairs)  19.6 us
    ppermute x10, waiting for transfers between devices, shift_turned(): return lax.ppermute(value, ALL_AXES, pairs)  16.3 us
    ppermute x2, waiting for transfers between devices, gather_both(): lax.ppermute(rows[t], ALL_AXES, pairs[t][1])  14.8 us
    ppermute x10, starting transfers between devices, shift(): return lax.ppermute(value, axis, [(i, (i + by) % 4) for i in range(4)])  14.7 us
    ppermute x2, waiting for transfers between devices, gather_both(): lax.ppermute(jnp.where(turned, halves[1 - t], halves[t]), ALL_AXES, pairs...  7.79 us
  transfers between devices with their start and end apart: 27, of which 13 were waited for; matrix products, arithmetic and copies ran while one was open for 2% of the time, Pallas kernels for 0%

profile of v7, /device:TPU:0, one launch (start us, length us, event | category | flops | bytes accessed | tf_op | source)
XLA Modules:
  0.0 191.4 jit_solution(14514546610107384029)
XLA Ops:
  0.0 6.8 %half_transform.1 = bf16[256,32,128]{2,1,0:T(8,128)(2,1)} custom-call(s32[1]{0:T(128)} %bitcast.20.self_ref, s32[128,128]{1,0:T(8,128)} %bitcast.123, s32[128,128]{1,0:T(8,128)} %bitcast.125, bf16[128,4,32,128]{3,2,1,0:T(8,128)(2,1)} %tiles_ref.1, bf16[32,20480]{1,0:T(8,128)(2,1)} %orbital_ref.1, s32[32,160]{1,0:T(8,128)} %support_ref.1), custom_call_target="tpu_custom_call" | custom-call | tf_op jit(solution)/shard_map/half_transform/pallas_call | solution.py:73
  6.8 36.5 %all_to_all.5.own_ref = bf16[256,32,128]{2,1,0:T(8,128)(2,1)S(1)} all-to-all(bf16[256,32,128]{2,1,0:T(8,128)(2,1)} %half_transform.1), channel_id=1, replica_groups=mesh['z'=4,'y'=4,'x'=4,'core'=2] {'z','y'}, dimensions={0} | all-to-all | bytes 4194304 | tf_op jit(solution)/shard_map/all_to_all | solution.py:362
  43.3 0.0 collective-permute-start
  43.4 0.7 constant_dynamic-slice_fusion.1
  44.1 0.2 convert_reduce_fusion
  44.3 0.2 reduce_window_sum.11
  44.5 0.1 convolution_convert_fusion
  44.6 0.1 fusion.20
  44.7 0.5 select_reduce_fusion.list_ref
  45.2 2.4 %collective-permute-done.other_ref = bf16[256,32,128]{2,1,0:T(8,128)(2,1)} collective-permute-done((bf16[256,32,128]{2,1,0:T(8,128)(2,1)S(1)}, bf16[256,32,128]{2,1,0:T(8,128)(2,1)}, u32[]{:S(2)}, u32[]{:S(2)}) %collective-permute-start) | collective-permute-done | bytes 2097184 | tf_op jit(solution)/shard_map/ppermute | solution.py:371
  47.6 3.3 %sum_slots.1 = (bf16[80,32,128]{2,1,0:T(8,128)(2,1)S(1)}, bf16[40,32,128]{2,1,0:T(8,128)(2,1)S(1)}, bf16[40,32,128]{2,1,0:T(8,128)(2,1)S(1)}, bf16[40,32,128]{2,...) custom-call(s32[2]{0:T(128)S(1)} %get-tuple-element.44.count_ref, ...), custom_call_target="tpu_custom_call" | custom-call | tf_op jit(solution)/shard_map/sum_slots/pallas_call | solution.py:128
  50.9 1.6 collective-permute-start.1
  52.5 1.8 collective-permute-start.5
  54.2 0.3 collective-permute-start.3
  54.5 3.0 %collective-permute-start.4 = (bf16[40,32,128]{2,1,0:T(8,128)(2,1)S(1)}, bf16[40,32,128]{2,1,0:T(8,128)(2,1)S(1)}, u32[]{:S(2)}, u32[]{:S(2)}) collective-permute-start(bf16[40,32,128]{2,1,0:T(8,128)(2,1)S(1)} %get-tuple-element.28), channel_id=1, source_target_pairs={{0,6},{2,0},{4,2},{6,4},{1,7},{3,1},{5,3},{7,5},{8,14},{10,8},{12,... | collective-permute-start | bytes 983048 | tf_op jit(solution)/shard_map/ppermute | solution.py:169
  57.4 5.3 %collective-permute-done.1 = bf16[40,32,128]{2,1,0:T(8,128)(2,1)S(1)} collective-permute-done((bf16[40,32,128]{2,1,0:T(8,128)(2,1)S(1)}, bf16[40,32,128]{2,1,0:T(8,128)(2,1)S(1)}, u32[]{:S(2)}, u32[]{:S(2)}) %collective-permute-start.1) | collective-permute-done | bytes 327712 | tf_op jit(solution)/shard_map/ppermute | solution.py:169
  62.7 0.1 add_convert_fusion.2
  62.8 0.3 collective-permute-start.2
  63.2 0.0 collective-permute-done.5
  63.2 0.1 add_convert_fusion.1
  63.3 3.0 %collective-permute-start.6 = (bf16[40,32,128]{2,1,0:T(8,128)(2,1)S(1)}, bf16[40,32,128]{2,1,0:T(8,128)(2,1)S(1)}, u32[]{:S(2)}, u32[]{:S(2)}) collective-permute-start(bf16[40,32,128]{2,1,0:T(8,128)(2,1)S(1)} %add_convert_fusion.1), channel_id=1, source_target_pairs={{0,6},{2,0},{4,2},{6,4},{1,7},{3,1},{5,3},{7,5},{8,14},{10,8},{12,... | collective-permute-start | bytes 983048 | tf_op jit(solution)/shard_map/ppermute | solution.py:169
  66.3 3.5 %collective-permute-done.3 = bf16[40,32,128]{2,1,0:T(8,128)(2,1)S(1)} collective-permute-done((bf16[40,32,128]{2,1,0:T(8,128)(2,1)S(1)}, bf16[40,32,128]{2,1,0:T(8,128)(2,1)S(1)}, u32[]{:S(2)}, u32[]{:S(2)}) %collective-permute-start.3) | collective-permute-done | bytes 327712 | tf_op jit(solution)/shard_map/ppermute | solution.py:169
  69.8 0.3 collective-permute-done.4
  70.1 5.9 %collective-permute-done.2 = bf16[40,32,128]{2,1,0:T(8,128)(2,1)S(1)} collective-permute-done((bf16[40,32,128]{2,1,0:T(8,128)(2,1)S(1)}, bf16[40,32,128]{2,1,0:T(8,128)(2,1)S(1)}, u32[]{:S(2)}, u32[]{:S(2)}) %collective-permute-start.2) | collective-permute-done | bytes 327712 | tf_op jit(solution)/shard_map/ppermute | solution.py:169
  76.0 0.3 add_convert_fusion
  76.3 0.9 collective-permute-start.8
  77.2 1.2 collective-permute-start.7
  78.4 0.7 collective-permute-start.9
  79.1 3.3 %collective-permute-start.10 = (bf16[1280,128]{1,0:T(8,128)(2,1)S(1)}, bf16[1280,128]{1,0:T(8,128)(2,1)S(1)}, u32[]{:S(2)}, u32[]{:S(2)}) collective-permute-start(bf16[1280,128]{1,0:T(8,128)(2,1)S(1)} %bitcast.121), channel_id=1, source_target_pairs={{0,2},{1,7},{2,4},{3,1},{4,6},{5,3},{6,0},{7,5},{8,10},{9,15},{10,... | collective-permute-start | bytes 983048 | tf_op jit(solution)/shard_map/ppermute | solution.py:222
  82.4 0.0 collective-permute-done.9
  82.4 7.8 %collective-permute-done.10 = bf16[1280,128]{1,0:T(8,128)(2,1)S(1)} collective-permute-done((bf16[1280,128]{1,0:T(8,128)(2,1)S(1)}, bf16[1280,128]{1,0:T(8,128)(2,1)S(1)}, u32[]{:S(2)}, u32[]{:S(2)}) %collective-permute-start.10) | collective-permute-done | bytes 327712 | tf_op jit(solution)/shard_map/ppermute | solution.py:222
  90.2 0.0 collective-permute-done.8
  90.2 0.0 collective-permute-done.7
  90.2 0.7 collective-permute-start.15
  90.9 0.1 pad_maximum_fusion.refs_5_
  91.0 4.8 %collective-permute-start.12 = (bf16[2,2560,128]{2,1,0:T(8,128)(2,1)S(1)}, bf16[2,2560,128]{2,1,0:T(8,128)(2,1)S(1)}, u32[]{:S(2)}, u32[]{:S(2)}) collective-permute-start(bf16[2,2560,128]{2,1,0:T(8,128)(2,1)S(1)} %pad_maximum_fusion.refs_5_), channel_id=1, source_target_pairs={{0,24},{1,97},{2,26},{3,99},{4,28},{5,101},{6,30},{7,103},{8,0},{9... | collective-permute-start | bytes 3932168 | tf_op jit(solution)/shard_map/ppermute | solution.py:198
  95.9 0.0 collective-permute-start.11
  95.9 3.7 %collective-permute-start.16 = (bf16[1280,128]{1,0:T(8,128)(2,1)S(1)}, bf16[1280,128]{1,0:T(8,128)(2,1)S(1)}, u32[]{:S(2)}, u32[]{:S(2)}) collective-permute-start(bf16[1280,128]{1,0:T(8,128)(2,1)S(1)} %collective-permute-done.10), channel_id=1, source_target_pairs={{2,10},{7,30},{4,44},{1,56},{6,78},{3,90},{0,104},{5,124},{10,11},... | collective-permute-start | bytes 983048 | tf_op jit(solution)/shard_map/ppermute | solution.py:228
  99.6 0.6 collective-permute-start.13
  100.2 0.0 collective-permute-done.15
  100.2 7.6 %collective-permute-start.14 = (bf16[1280,128]{1,0:T(8,128)(2,1)S(1)}, bf16[1280,128]{1,0:T(8,128)(2,1)S(1)}, u32[]{:S(2)}, u32[]{:S(2)}) collective-permute-start(bf16[1280,128]{1,0:T(8,128)(2,1)S(1)} %slice.31), channel_id=1, source_target_pairs={{0,32},{1,9},{2,34},{3,11},{4,36},{5,13},{6,38},{7,15},{8,40},{9,1... | collective-permute-start | bytes 983048 | tf_op jit(solution)/shard_map/ppermute | solution.py:198
  107.9 14.8 %collective-permute-done.16 = bf16[1280,128]{1,0:T(8,128)(2,1)S(1)} collective-permute-done((bf16[1280,128]{1,0:T(8,128)(2,1)S(1)}, bf16[1280,128]{1,0:T(8,128)(2,1)S(1)}, u32[]{:S(2)}, u32[]{:S(2)}) %collective-permute-start.16) | collective-permute-done | bytes 327712 | tf_op jit(solution)/shard_map/ppermute | solution.py:228
  122.6 0.1 pad_maximum_fusion.4
  122.7 0.0 collective-permute-done.13
  122.8 0.1 pad_maximum_fusion.1.refs_6_
  122.9 2.3 %collective-permute-start.18 = (bf16[2,2560,128]{2,1,0:T(8,128)(2,1)S(1)}, bf16[2,2560,128]{2,1,0:T(8,128)(2,1)S(1)}, u32[]{:S(2)}, u32[]{:S(2)}) collective-permute-start(bf16[2,2560,128]{2,1,0:T(8,128)(2,1)S(1)} %pad_maximum_fusion.1.refs_6_), channel_id=1, source_target_pairs={{0,24},{1,97},{2,26},{3,99},{4,28},{5,101},{6,30},{7,103},{8,0},{9... | collective-permute-start | bytes 3932168 | tf_op jit(solution)/shard_map/ppermute | solution.py:198
  125.2 2.7 %collective-permute-start.20 = (bf16[2,1280,128]{2,1,0:T(8,128)(2,1)S(1)}, bf16[2,1280,128]{2,1,0:T(8,128)(2,1)S(1)}, u32[]{:S(2)}, u32[]{:S(2)}) collective-permute-start(bf16[2,1280,128]{2,1,0:T(8,128)(2,1)S(1)} %pad_maximum_fusion.4), channel_id=1, source_target_pairs={{0,6},{2,0},{4,2},{6,4},{1,7},{3,1},{5,3},{7,5},{8,14},{10,8},{12,... | collective-permute-start | bytes 1966088 | tf_op jit(solution)/shard_map/ppermute | solution.py:169
  127.9 10.7 %collective-permute-done.20 = bf16[2,1280,128]{2,1,0:T(8,128)(2,1)S(1)} collective-permute-done((bf16[2,1280,128]{2,1,0:T(8,128)(2,1)S(1)}, bf16[2,1280,128]{2,1,0:T(8,128)(2,1)S(1)}, u32[]{:S(2)}, u32[]{:S(2)}) %collective-permute-start.20) | collective-permute-done | bytes 655392 | tf_op jit(solution)/shard_map/ppermute | solution.py:169
  138.7 3.3 %collective-permute-done.19 = bf16[2,1280,128]{2,1,0:T(8,128)(2,1)S(1)} collective-permute-done((bf16[2,1280,128]{2,1,0:T(8,128)(2,1)S(1)}, bf16[2,1280,128]{2,1,0:T(8,128)(2,1)S(1)}, u32[]{:S(2)}, u32[]{:S(2)}) %collective-permute-start.19) | collective-permute-done | bytes 655392 | tf_op jit(solution)/shard_map/ppermute | solution.py:169
  142.0 5.5 %collective-permute-done.17.refs_8_ = bf16[2,2560,128]{2,1,0:T(8,128)(2,1)S(1)} collective-permute-done((bf16[2,2560,128]{2,1,0:T(8,128)(2,1)S(1)}, bf16[2,2560,128]{2,1,0:T(8,128)(2,1)S(1)}, u32[]{:S(2)}, u32[]{:S(2)}) %collective-permute-start.17) | collective-permute-done | bytes 1310752 | tf_op jit(solution)/shard_map/ppermute | solution.py:198
  147.5 0.1 collective-permute-start.21
  147.6 2.0 %collective-permute-start.22 = (bf16[1280,128]{1,0:T(8,128)(2,1)S(1)}, bf16[1280,128]{1,0:T(8,128)(2,1)S(1)}, u32[]{:S(2)}, u32[]{:S(2)}) collective-permute-start(bf16[1280,128]{1,0:T(8,128)(2,1)S(1)} %slice_bitcast_fusion), channel_id=1, source_target_pairs={{0,2},{2,4},{4,6},{6,0},{1,3},{3,5},{5,7},{7,1},{8,10},{10,12},{12... | collective-permute-start | bytes 983048 | tf_op jit(solution)/shard_map/ppermute | solution.py:169
  149.6 2.0 %collective-permute-start.25 = (bf16[2,2560,128]{2,1,0:T(8,128)(2,1)S(1)}, bf16[2,2560,128]{2,1,0:T(8,128)(2,1)S(1)}, u32[]{:S(2)}, u32[]{:S(2)}) collective-permute-start(bf16[2,2560,128]{2,1,0:T(8,128)(2,1)S(1)} %collective-permute-done.12.refs_9_), channel_id=1, source_target_pairs={{0,24},{1,97},{2,26},{3,99},{4,28},{5,101},{6,30},{7,103},{8,0},{9... | collective-permute-start | bytes 3932168 | tf_op jit(solution)/shard_map/ppermute | solution.py:198
  151.6 0.1 pad_maximum_fusion.2.refs_1_
  151.8 0.1 collective-permute-start.23
  151.9 0.1 collective-permute-start.26
  151.9 5.8 %collective-permute-done.21 = bf16[1280,128]{1,0:T(8,128)(2,1)S(1)} collective-permute-done((bf16[1280,128]{1,0:T(8,128)(2,1)S(1)}, bf16[1280,128]{1,0:T(8,128)(2,1)S(1)}, u32[]{:S(2)}, u32[]{:S(2)}) %collective-permute-start.21) | collective-permute-done | bytes 327712 | tf_op jit(solution)/shard_map/ppermute | solution.py:169
  157.7 0.1 maximum_bitcast_fusion.1
  157.8 0.1 pad_maximum_fusion.3.refs_2_
  157.9 2.0 %collective-permute-start.24 = (bf16[2,2,1280,128]{3,2,1,0:T(8,128)(2,1)S(1)}, bf16[2,2,1280,128]{3,2,1,0:T(8,128)(2,1)S(1)}, u32[]{:S(2)}, u32[]{:S(2)}) collective-permute-start(bf16[2,2,1280,128]{3,2,1,0:T(8,128)(2,1)S(1)} %pad_maximum_fusion.3.refs_2_), channel_id=1, source_target_pairs={{0,1},{1,0},{2,3},{3,2},{4,5},{5,4},{6,7},{7,6},{8,9},{9,8},{10,11... | collective-permute-start | bytes 3932168 | tf_op jit(solution)/shard_map/ppermute | solution.py:239
  159.9 0.1 pad_add_fusion.refs_0_
  159.9 7.3 %collective-permute-done.25.refs_11_ = bf16[2,2560,128]{2,1,0:T(8,128)(2,1)S(1)} collective-permute-done((bf16[2,2560,128]{2,1,0:T(8,128)(2,1)S(1)}, bf16[2,2560,128]{2,1,0:T(8,128)(2,1)S(1)}, u32[]{:S(2)}, u32[]{:S(2)}) %collective-permute-start.25) | collective-permute-done | bytes 1310752 | tf_op jit(solution)/shard_map/ppermute | solution.py:198
  167.2 3.5 %collective-permute-done.26.refs_12_ = bf16[2,2560,128]{2,1,0:T(8,128)(2,1)S(1)} collective-permute-done((bf16[2,2560,128]{2,1,0:T(8,128)(2,1)S(1)}, bf16[2,2560,128]{2,1,0:T(8,128)(2,1)S(1)}, u32[]{:S(2)}, u32[]{:S(2)}) %collective-permute-start.26) | collective-permute-done | bytes 1310752 | tf_op jit(solution)/shard_map/ppermute | solution.py:198
  170.7 20.5 %exchange.1 = f32[1280,2560]{1,0:T(8,128)} custom-call(s32[4]{0:T(128)S(1)} %pad_add_fusion.refs_0_, bf16[2,2,1280,128]{3,2,1,0:T(8,128)(2,1)S(1)} %pad_maximum_fusion.2.refs_1_, bf16[2,2,1280,128]{3,2,1,0:T(8,128)(2,1)S(1)} %pad_maximum_fusion.3.refs_2_, bf16[2,2,1280,128]{3,2,1,0:T(8,128)(2,1)S(1)} %collective-permute-done.23.refs_3_, ...), custom_call_target="tpu_custom_call" | custom-call | tf_op jit(solution)/shard_map/exchange/pallas_call | solution.py:319
  (24 shorter events, 0.3 us)
Async XLA Ops:
  0.0 43.3 %copy-start = (s32[16384]{0:T(1024)S(1)}, s32[16384]{0:T(1024)}, u32[]{:S(2)}) copy-start(s32[16384]{0:T(1024)} %param.8) | copy-start | bytes 196612
  43.3 4.3 %collective-permute-start = (bf16[256,32,128]{2,1,0:T(8,128)(2,1)S(1)}, bf16[256,32,128]{2,1,0:T(8,128)(2,1)}, u32[]{:S(2)}, u32[]{:S(2)}) collective-permute-start(bf16[256,32,128]{2,1,0:T(8,128)(2,1)S(1)} %all_to_all.5.own_ref), channel_id=1, source_target_pairs={{0,1},{1,0},{2,3},{3,2},{4,5},{5,4},{6,7},{7,6},{8,9},{9,8},{10,11... | collective-permute-start | bytes 6291464 | tf_op jit(solution)/shard_map/ppermute | solution.py:371
  50.9 11.8 %collective-permute-start.1 = (bf16[40,32,128]{2,1,0:T(8,128)(2,1)S(1)}, bf16[40,32,128]{2,1,0:T(8,128)(2,1)S(1)}, u32[]{:S(2)}, u32[]{:S(2)}) collective-permute-start(bf16[40,32,128]{2,1,0:T(8,128)(2,1)S(1)} %get-tuple-element.26), channel_id=1, source_target_pairs={{0,2},{2,4},{4,6},{6,0},{1,3},{3,5},{5,7},{7,1},{8,10},{10,12},{12... | collective-permute-start | bytes 983048 | tf_op jit(solution)/shard_map/ppermute | solution.py:169
  52.5 10.7 %collective-permute-start.5 = (bf16[40,32,128]{2,1,0:T(8,128)(2,1)S(1)}, bf16[40,32,128]{2,1,0:T(8,128)(2,1)S(1)}, u32[]{:S(2)}, u32[]{:S(2)}) collective-permute-start(bf16[40,32,128]{2,1,0:T(8,128)(2,1)S(1)} %get-tuple-element.30), channel_id=1, source_target_pairs={{0,6},{2,0},{4,2},{6,4},{1,7},{3,1},{5,3},{7,5},{8,14},{10,8},{12,... | collective-permute-start | bytes 983048 | tf_op jit(solution)/shard_map/ppermute | solution.py:169
  54.2 15.6 %collective-permute-start.3 = (bf16[40,32,128]{2,1,0:T(8,128)(2,1)S(1)}, bf16[40,32,128]{2,1,0:T(8,128)(2,1)S(1)}, u32[]{:S(2)}, u32[]{:S(2)}) collective-permute-start(bf16[40,32,128]{2,1,0:T(8,128)(2,1)S(1)} %get-tuple-element.27), channel_id=1, source_target_pairs={{0,2},{2,4},{4,6},{6,0},{1,3},{3,5},{5,7},{7,1},{8,10},{10,12},{12... | collective-permute-start | bytes 983048 | tf_op jit(solution)/shard_map/ppermute | solution.py:169
  54.5 15.6 %collective-permute-start.4 = (bf16[40,32,128]{2,1,0:T(8,128)(2,1)S(1)}, bf16[40,32,128]{2,1,0:T(8,128)(2,1)S(1)}, u32[]{:S(2)}, u32[]{:S(2)}) collective-permute-start(bf16[40,32,128]{2,1,0:T(8,128)(2,1)S(1)} %get-tuple-element.28), channel_id=1, source_target_pairs={{0,6},{2,0},{4,2},{6,4},{1,7},{3,1},{5,3},{7,5},{8,14},{10,8},{12,... | collective-permute-start | bytes 983048 | tf_op jit(solution)/shard_map/ppermute | solution.py:169
  62.8 13.2 %collective-permute-start.2 = (bf16[40,32,128]{2,1,0:T(8,128)(2,1)S(1)}, bf16[40,32,128]{2,1,0:T(8,128)(2,1)S(1)}, u32[]{:S(2)}, u32[]{:S(2)}) collective-permute-start(bf16[40,32,128]{2,1,0:T(8,128)(2,1)S(1)} %add_convert_fusion.2), channel_id=1, source_target_pairs={{0,2},{2,4},{4,6},{6,0},{1,3},{3,5},{5,7},{7,1},{8,10},{10,12},{12... | collective-permute-start | bytes 983048 | tf_op jit(solution)/shard_map/ppermute | solution.py:169
  63.3 12.7 %collective-permute-start.6 = (bf16[40,32,128]{2,1,0:T(8,128)(2,1)S(1)}, bf16[40,32,128]{2,1,0:T(8,128)(2,1)S(1)}, u32[]{:S(2)}, u32[]{:S(2)}) collective-permute-start(bf16[40,32,128]{2,1,0:T(8,128)(2,1)S(1)} %add_convert_fusion.1), channel_id=1, source_target_pairs={{0,6},{2,0},{4,2},{6,4},{1,7},{3,1},{5,3},{7,5},{8,14},{10,8},{12,... | collective-permute-start | bytes 983048 | tf_op jit(solution)/shard_map/ppermute | solution.py:169
  76.3 13.9 %collective-permute-start.8 = (bf16[2560,128]{1,0:T(8,128)(2,1)S(1)}, bf16[2560,128]{1,0:T(8,128)(2,1)S(1)}, u32[]{:S(2)}, u32[]{:S(2)}) collective-permute-start(bf16[2560,128]{1,0:T(8,128)(2,1)S(1)} %bitcast.109), channel_id=1, source_target_pairs={{0,96},{1,25},{2,98},{3,27},{4,100},{5,29},{6,102},{7,31},{8,104},... | collective-permute-start | bytes 1966088 | tf_op jit(solution)/shard_map/ppermute | solution.py:198
  77.2 13.0 %collective-permute-start.7 = (bf16[2560,128]{1,0:T(8,128)(2,1)S(1)}, bf16[2560,128]{1,0:T(8,128)(2,1)S(1)}, u32[]{:S(2)}, u32[]{:S(2)}) collective-permute-start(bf16[2560,128]{1,0:T(8,128)(2,1)S(1)} %bitcast.110), channel_id=1, source_target_pairs={{0,32},{1,9},{2,34},{3,11},{4,36},{5,13},{6,38},{7,15},{8,40},{9,1... | collective-permute-start | bytes 1966088 | tf_op jit(solution)/shard_map/ppermute | solution.py:198
  78.4 4.0 %collective-permute-start.9 = (bf16[1280,128]{1,0:T(8,128)(2,1)S(1)}, bf16[1280,128]{1,0:T(8,128)(2,1)S(1)}, u32[]{:S(2)}, u32[]{:S(2)}) collective-permute-start(bf16[1280,128]{1,0:T(8,128)(2,1)S(1)} %bitcast.122), channel_id=1, source_target_pairs={{0,0},{1,5},{2,2},{3,7},{4,4},{5,1},{6,6},{7,3},{8,8},{9,13},{10,1... | collective-permute-start | bytes 983048 | tf_op jit(solution)/shard_map/ppermute | solution.py:222
  79.1 11.1 %collective-permute-start.10 = (bf16[1280,128]{1,0:T(8,128)(2,1)S(1)}, bf16[1280,128]{1,0:T(8,128)(2,1)S(1)}, u32[]{:S(2)}, u32[]{:S(2)}) collective-permute-start(bf16[1280,128]{1,0:T(8,128)(2,1)S(1)} %bitcast.121), channel_id=1, source_target_pairs={{0,2},{1,7},{2,4},{3,1},{4,6},{5,3},{6,0},{7,5},{8,10},{9,15},{10,... | collective-permute-start | bytes 983048 | tf_op jit(solution)/shard_map/ppermute | solution.py:222
  90.2 10.0 %collective-permute-start.15 = (bf16[1280,128]{1,0:T(8,128)(2,1)S(1)}, bf16[1280,128]{1,0:T(8,128)(2,1)S(1)}, u32[]{:S(2)}, u32[]{:S(2)}) collective-permute-start(bf16[1280,128]{1,0:T(8,128)(2,1)S(1)} %collective-permute-done.9), channel_id=1, source_target_pairs={{0,0},{5,20},{2,34},{7,54},{4,68},{1,80},{6,102},{3,114},{8,1},{13... | collective-permute-start | bytes 983048 | tf_op jit(solution)/shard_map/ppermute | solution.py:228
  91.0 31.9 %collective-permute-start.12 = (bf16[2,2560,128]{2,1,0:T(8,128)(2,1)S(1)}, bf16[2,2560,128]{2,1,0:T(8,128)(2,1)S(1)}, u32[]{:S(2)}, u32[]{:S(2)}) collective-permute-start(bf16[2,2560,128]{2,1,0:T(8,128)(2,1)S(1)} %pad_maximum_fusion.refs_5_), channel_id=1, source_target_pairs={{0,24},{1,97},{2,26},{3,99},{4,28},{5,101},{6,30},{7,103},{8,0},{9... | collective-permute-start | bytes 3932168 | tf_op jit(solution)/shard_map/ppermute | solution.py:198
  95.9 27.0 %collective-permute-start.11 = (bf16[2,2560,128]{2,1,0:T(8,128)(2,1)S(1)}, bf16[2,2560,128]{2,1,0:T(8,128)(2,1)S(1)}, u32[]{:S(2)}, u32[]{:S(2)}) collective-permute-start(bf16[2,2560,128]{2,1,0:T(8,128)(2,1)S(1)} %pad_maximum_fusion.refs_5_), channel_id=1, source_target_pairs={{0,8},{1,33},{2,10},{3,35},{4,12},{5,37},{6,14},{7,39},{8,16},{9,4... | collective-permute-start | bytes 3932168 | tf_op jit(solution)/shard_map/ppermute | solution.py:198
  95.9 26.8 %collective-permute-start.16 = (bf16[1280,128]{1,0:T(8,128)(2,1)S(1)}, bf16[1280,128]{1,0:T(8,128)(2,1)S(1)}, u32[]{:S(2)}, u32[]{:S(2)}) collective-permute-start(bf16[1280,128]{1,0:T(8,128)(2,1)S(1)} %collective-permute-done.10), channel_id=1, source_target_pairs={{2,10},{7,30},{4,44},{1,56},{6,78},{3,90},{0,104},{5,124},{10,11},... | collective-permute-start | bytes 983048 | tf_op jit(solution)/shard_map/ppermute | solution.py:228
  99.6 23.1 %collective-permute-start.13 = (bf16[1280,128]{1,0:T(8,128)(2,1)S(1)}, bf16[1280,128]{1,0:T(8,128)(2,1)S(1)}, u32[]{:S(2)}, u32[]{:S(2)}) collective-permute-start(bf16[1280,128]{1,0:T(8,128)(2,1)S(1)} %slice.30), channel_id=1, source_target_pairs={{0,96},{1,25},{2,98},{3,27},{4,100},{5,29},{6,102},{7,31},{8,104},... | collective-permute-start | bytes 983048 | tf_op jit(solution)/shard_map/ppermute | solution.py:198
  100.2 22.5 %collective-permute-start.14 = (bf16[1280,128]{1,0:T(8,128)(2,1)S(1)}, bf16[1280,128]{1,0:T(8,128)(2,1)S(1)}, u32[]{:S(2)}, u32[]{:S(2)}) collective-permute-start(bf16[1280,128]{1,0:T(8,128)(2,1)S(1)} %slice.31), channel_id=1, source_target_pairs={{0,32},{1,9},{2,34},{3,11},{4,36},{5,13},{6,38},{7,15},{8,40},{9,1... | collective-permute-start | bytes 983048 | tf_op jit(solution)/shard_map/ppermute | solution.py:198
  122.9 19.1 %collective-permute-start.18 = (bf16[2,2560,128]{2,1,0:T(8,128)(2,1)S(1)}, bf16[2,2560,128]{2,1,0:T(8,128)(2,1)S(1)}, u32[]{:S(2)}, u32[]{:S(2)}) collective-permute-start(bf16[2,2560,128]{2,1,0:T(8,128)(2,1)S(1)} %pad_maximum_fusion.1.refs_6_), channel_id=1, source_target_pairs={{0,24},{1,97},{2,26},{3,99},{4,28},{5,101},{6,30},{7,103},{8,0},{9... | collective-permute-start | bytes 3932168 | tf_op jit(solution)/shard_map/ppermute | solution.py:198
  125.2 22.2 %collective-permute-start.17 = (bf16[2,2560,128]{2,1,0:T(8,128)(2,1)S(1)}, bf16[2,2560,128]{2,1,0:T(8,128)(2,1)S(1)}, u32[]{:S(2)}, u32[]{:S(2)}) collective-permute-start(bf16[2,2560,128]{2,1,0:T(8,128)(2,1)S(1)} %pad_maximum_fusion.1.refs_6_), channel_id=1, source_target_pairs={{0,8},{1,33},{2,10},{3,35},{4,12},{5,37},{6,14},{7,39},{8,16},{9,4... | collective-permute-start | bytes 3932168 | tf_op jit(solution)/shard_map/ppermute | solution.py:198
  125.2 13.4 %collective-permute-start.20 = (bf16[2,1280,128]{2,1,0:T(8,128)(2,1)S(1)}, bf16[2,1280,128]{2,1,0:T(8,128)(2,1)S(1)}, u32[]{:S(2)}, u32[]{:S(2)}) collective-permute-start(bf16[2,1280,128]{2,1,0:T(8,128)(2,1)S(1)} %pad_maximum_fusion.4), channel_id=1, source_target_pairs={{0,6},{2,0},{4,2},{6,4},{1,7},{3,1},{5,3},{7,5},{8,14},{10,8},{12,... | collective-permute-start | bytes 1966088 | tf_op jit(solution)/shard_map/ppermute | solution.py:169
  127.9 14.0 %collective-permute-start.19 = (bf16[2,1280,128]{2,1,0:T(8,128)(2,1)S(1)}, bf16[2,1280,128]{2,1,0:T(8,128)(2,1)S(1)}, u32[]{:S(2)}, u32[]{:S(2)}) collective-permute-start(bf16[2,1280,128]{2,1,0:T(8,128)(2,1)S(1)} %pad_maximum_fusion.4), channel_id=1, source_target_pairs={{0,2},{2,4},{4,6},{6,0},{1,3},{3,5},{5,7},{7,1},{8,10},{10,12},{12... | collective-permute-start | bytes 1966088 | tf_op jit(solution)/shard_map/ppermute | solution.py:169
  147.5 10.2 %collective-permute-start.21 = (bf16[1280,128]{1,0:T(8,128)(2,1)S(1)}, bf16[1280,128]{1,0:T(8,128)(2,1)S(1)}, u32[]{:S(2)}, u32[]{:S(2)}) collective-permute-start(bf16[1280,128]{1,0:T(8,128)(2,1)S(1)} %slice_bitcast_fusion.1), channel_id=1, source_target_pairs={{0,6},{2,0},{4,2},{6,4},{1,7},{3,1},{5,3},{7,5},{8,14},{10,8},{12,... | collective-permute-start | bytes 983048 | tf_op jit(solution)/shard_map/ppermute | solution.py:169
  147.6 10.1 %collective-permute-start.22 = (bf16[1280,128]{1,0:T(8,128)(2,1)S(1)}, bf16[1280,128]{1,0:T(8,128)(2,1)S(1)}, u32[]{:S(2)}, u32[]{:S(2)}) collective-permute-start(bf16[1280,128]{1,0:T(8,128)(2,1)S(1)} %slice_bitcast_fusion), channel_id=1, source_target_pairs={{0,2},{2,4},{4,6},{6,0},{1,3},{3,5},{5,7},{7,1},{8,10},{10,12},{12... | collective-permute-start | bytes 983048 | tf_op jit(solution)/shard_map/ppermute | solution.py:169
  149.6 17.6 %collective-permute-start.25 = (bf16[2,2560,128]{2,1,0:T(8,128)(2,1)S(1)}, bf16[2,2560,128]{2,1,0:T(8,128)(2,1)S(1)}, u32[]{:S(2)}, u32[]{:S(2)}) collective-permute-start(bf16[2,2560,128]{2,1,0:T(8,128)(2,1)S(1)} %collective-permute-done.12.refs_9_), channel_id=1, source_target_pairs={{0,24},{1,97},{2,26},{3,99},{4,28},{5,101},{6,30},{7,103},{8,0},{9... | collective-permute-start | bytes 3932168 | tf_op jit(solution)/shard_map/ppermute | solution.py:198
  151.8 15.5 %collective-permute-start.23 = (bf16[2,2,1280,128]{3,2,1,0:T(8,128)(2,1)S(1)}, bf16[2,2,1280,128]{3,2,1,0:T(8,128)(2,1)S(1)}, u32[]{:S(2)}, u32[]{:S(2)}) collective-permute-start(bf16[2,2,1280,128]{3,2,1,0:T(8,128)(2,1)S(1)} %pad_maximum_fusion.2.refs_1_), channel_id=1, source_target_pairs={{0,1},{1,0},{2,3},{3,2},{4,5},{5,4},{6,7},{7,6},{8,9},{9,8},{10,11... | collective-permute-start | bytes 3932168 | tf_op jit(solution)/shard_map/ppermute | solution.py:239
  151.9 18.9 %collective-permute-start.26 = (bf16[2,2560,128]{2,1,0:T(8,128)(2,1)S(1)}, bf16[2,2560,128]{2,1,0:T(8,128)(2,1)S(1)}, u32[]{:S(2)}, u32[]{:S(2)}) collective-permute-start(bf16[2,2560,128]{2,1,0:T(8,128)(2,1)S(1)} %collective-permute-done.17.refs_8_), channel_id=1, source_target_pairs={{0,8},{1,33},{2,10},{3,35},{4,12},{5,37},{6,14},{7,39},{8,16},{9,4... | collective-permute-start | bytes 3932168 | tf_op jit(solution)/shard_map/ppermute | solution.py:198
  157.9 12.9 %collective-permute-start.24 = (bf16[2,2,1280,128]{3,2,1,0:T(8,128)(2,1)S(1)}, bf16[2,2,1280,128]{3,2,1,0:T(8,128)(2,1)S(1)}, u32[]{:S(2)}, u32[]{:S(2)}) collective-permute-start(bf16[2,2,1280,128]{3,2,1,0:T(8,128)(2,1)S(1)} %pad_maximum_fusion.3.refs_2_), channel_id=1, source_target_pairs={{0,1},{1,0},{2,3},{3,2},{4,5},{5,4},{6,7},{7,6},{8,9},{9,8},{10,11... | collective-permute-start | bytes 3932168 | tf_op jit(solution)/shard_map/ppermute | solution.py:239

commit v8 on v7

--- a/solution.py
+++ b/solution.py
@@ -281,10 +281,12 @@
                 for index, col_ref in enumerate(col_refs)
             ]
         )
-    for copy in row_copies + sum(col_copies, []):
+    for copy in row_copies + col_copies[0]:
         copy.start()
     for copy in row_copies:
         copy.wait()
+    for copy in sum(col_copies[1:], []):
+        copy.start()
 
     out_copies = []
     out_rows = rows // OUT_PARTS

time: 192 us -> 192 us (level)
  transfers between devices with their start and end apart: 27 -> 27, of which waited for: 13 -> 14; matrix products, arithmetic and copies ran while one was open for 2% -> 2% of each run, Pallas kernels for 0% -> 0%
where the time goes in v8:
time: 192 us; the launch traced here: 191 us
  waiting for transfers between devices  76 us (40%)
  starting transfers between devices  44.7 us (23%)
  blocking collectives  36.5 us (19%)
  Pallas kernels  30.5 us (16%)
  other arithmetic  2.21 us (1%)
    all_to_all x1, blocking collectives, shards(): lax.all_to_all(outgoing, AUX_AXES, split_axis=0, concat_axis=0, tiled=True)  36.5 us
    ppermute x10, waiting for transfers between devices, shift(): return lax.ppermute(value, axis, [(i, (i + by) % 4) for i in range(4)])  34.9 us
    pallas_call x1, Pallas kernels, exchange_block(): pl.pallas_call(lambda *refs: exchange_kernel(*refs, factor=1.0 / depth),...  20.5 us
    ppermute x10, starting transfers between devices, shift_turned(): return lax.ppermute(value, ALL_AXES, pairs)  19.4 us
    ppermute x10, waiting for transfers between devices, shift_turned(): return lax.ppermute(value, ALL_AXES, pairs)  16.3 us
    ppermute x2, waiting for transfers between devices, gather_both(): lax.ppermute(rows[t], ALL_AXES, pairs[t][1])  14.9 us
    ppermute x10, starting transfers between devices, shift(): return lax.ppermute(value, axis, [(i, (i + by) % 4) for i in range(4)])  14.9 us
    ppermute x2, waiting for transfers between devices, gather_both(): lax.ppermute(jnp.where(turned, halves[1 - t], halves[t]), ALL_AXES, pairs...  7.5 us
  transfers between devices with their start and end apart: 27, of which 14 were waited for; matrix products, arithmetic and copies ran while one was open for 2% of the time, Pallas kernels for 0%

profile of v8, /device:TPU:0, one launch (start us, length us, event | category | flops | bytes accessed | tf_op | source)
XLA Modules:
  0.0 191.3 jit_solution(6525566268714557984)
XLA Ops:
  0.0 6.8 %half_transform.1 = bf16[256,32,128]{2,1,0:T(8,128)(2,1)} custom-call(s32[1]{0:T(128)} %bitcast.20.self_ref, s32[128,128]{1,0:T(8,128)} %bitcast.123, s32[128,128]{1,0:T(8,128)} %bitcast.125, bf16[128,4,32,128]{3,2,1,0:T(8,128)(2,1)} %tiles_ref.1, bf16[32,20480]{1,0:T(8,128)(2,1)} %orbital_ref.1, s32[32,160]{1,0:T(8,128)} %support_ref.1), custom_call_target="tpu_custom_call" | custom-call | tf_op jit(solution)/shard_map/half_transform/pallas_call | solution.py:73
  6.8 36.5 %all_to_all.5.own_ref = bf16[256,32,128]{2,1,0:T(8,128)(2,1)S(1)} all-to-all(bf16[256,32,128]{2,1,0:T(8,128)(2,1)} %half_transform.1), channel_id=1, replica_groups=mesh['z'=4,'y'=4,'x'=4,'core'=2] {'z','y'}, dimensions={0} | all-to-all | bytes 4194304 | tf_op jit(solution)/shard_map/all_to_all | solution.py:364
  43.3 0.0 collective-permute-start
  43.4 0.7 constant_dynamic-slice_fusion.1
  44.1 0.2 convert_reduce_fusion
  44.3 0.2 reduce_window_sum.11
  44.5 0.1 convolution_convert_fusion
  44.6 0.1 fusion.20
  44.7 0.5 select_reduce_fusion.list_ref
  45.2 2.4 %collective-permute-done.other_ref = bf16[256,32,128]{2,1,0:T(8,128)(2,1)} collective-permute-done((bf16[256,32,128]{2,1,0:T(8,128)(2,1)S(1)}, bf16[256,32,128]{2,1,0:T(8,128)(2,1)}, u32[]{:S(2)}, u32[]{:S(2)}) %collective-permute-start) | collective-permute-done | bytes 2097184 | tf_op jit(solution)/shard_map/ppermute | solution.py:373
  47.6 3.3 %sum_slots.1 = (bf16[80,32,128]{2,1,0:T(8,128)(2,1)S(1)}, bf16[40,32,128]{2,1,0:T(8,128)(2,1)S(1)}, bf16[40,32,128]{2,1,0:T(8,128)(2,1)S(1)}, bf16[40,32,128]{2,...) custom-call(s32[2]{0:T(128)S(1)} %get-tuple-element.44.count_ref, ...), custom_call_target="tpu_custom_call" | custom-call | tf_op jit(solution)/shard_map/sum_slots/pallas_call | solution.py:128
  50.9 1.4 collective-permute-start.1
  52.3 1.9 collective-permute-start.5
  54.2 0.2 collective-permute-start.3
  54.4 3.1 %collective-permute-start.4 = (bf16[40,32,128]{2,1,0:T(8,128)(2,1)S(1)}, bf16[40,32,128]{2,1,0:T(8,128)(2,1)S(1)}, u32[]{:S(2)}, u32[]{:S(2)}) collective-permute-start(bf16[40,32,128]{2,1,0:T(8,128)(2,1)S(1)} %get-tuple-element.28), channel_id=1, source_target_pairs={{0,6},{2,0},{4,2},{6,4},{1,7},{3,1},{5,3},{7,5},{8,14},{10,8},{12,... | collective-permute-start | bytes 983048 | tf_op jit(solution)/shard_map/ppermute | solution.py:169
  57.4 5.3 %collective-permute-done.1 = bf16[40,32,128]{2,1,0:T(8,128)(2,1)S(1)} collective-permute-done((bf16[40,32,128]{2,1,0:T(8,128)(2,1)S(1)}, bf16[40,32,128]{2,1,0:T(8,128)(2,1)S(1)}, u32[]{:S(2)}, u32[]{:S(2)}) %collective-permute-start.1) | collective-permute-done | bytes 327712 | tf_op jit(solution)/shard_map/ppermute | solution.py:169
  62.7 0.1 add_convert_fusion.2
  62.8 0.2 collective-permute-start.2
  63.0 0.1 add_convert_fusion.1
  63.1 3.2 %collective-permute-start.6 = (bf16[40,32,128]{2,1,0:T(8,128)(2,1)S(1)}, bf16[40,32,128]{2,1,0:T(8,128)(2,1)S(1)}, u32[]{:S(2)}, u32[]{:S(2)}) collective-permute-start(bf16[40,32,128]{2,1,0:T(8,128)(2,1)S(1)} %add_convert_fusion.1), channel_id=1, source_target_pairs={{0,6},{2,0},{4,2},{6,4},{1,7},{3,1},{5,3},{7,5},{8,14},{10,8},{12,... | collective-permute-start | bytes 983048 | tf_op jit(solution)/shard_map/ppermute | solution.py:169
  66.3 3.5 %collective-permute-done.3 = bf16[40,32,128]{2,1,0:T(8,128)(2,1)S(1)} collective-permute-done((bf16[40,32,128]{2,1,0:T(8,128)(2,1)S(1)}, bf16[40,32,128]{2,1,0:T(8,128)(2,1)S(1)}, u32[]{:S(2)}, u32[]{:S(2)}) %collective-permute-start.3) | collective-permute-done | bytes 327712 | tf_op jit(solution)/shard_map/ppermute | solution.py:169
  69.8 0.2 collective-permute-done.4
  69.9 6.0 %collective-permute-done.2 = bf16[40,32,128]{2,1,0:T(8,128)(2,1)S(1)} collective-permute-done((bf16[40,32,128]{2,1,0:T(8,128)(2,1)S(1)}, bf16[40,32,128]{2,1,0:T(8,128)(2,1)S(1)}, u32[]{:S(2)}, u32[]{:S(2)}) %collective-permute-start.2) | collective-permute-done | bytes 327712 | tf_op jit(solution)/shard_map/ppermute | solution.py:169
  75.9 0.1 collective-permute-done.6
  76.0 0.3 add_convert_fusion
  76.3 0.8 collective-permute-start.8
  77.1 1.3 collective-permute-start.7
  78.4 0.7 collective-permute-start.9
  79.1 3.4 %collective-permute-start.10 = (bf16[1280,128]{1,0:T(8,128)(2,1)S(1)}, bf16[1280,128]{1,0:T(8,128)(2,1)S(1)}, u32[]{:S(2)}, u32[]{:S(2)}) collective-permute-start(bf16[1280,128]{1,0:T(8,128)(2,1)S(1)} %bitcast.121), channel_id=1, source_target_pairs={{0,2},{1,7},{2,4},{3,1},{4,6},{5,3},{6,0},{7,5},{8,10},{9,15},{10,... | collective-permute-start | bytes 983048 | tf_op jit(solution)/shard_map/ppermute | solution.py:222
  82.5 0.0 collective-permute-done.9
  82.5 7.5 %collective-permute-done.10 = bf16[1280,128]{1,0:T(8,128)(2,1)S(1)} collective-permute-done((bf16[1280,128]{1,0:T(8,128)(2,1)S(1)}, bf16[1280,128]{1,0:T(8,128)(2,1)S(1)}, u32[]{:S(2)}, u32[]{:S(2)}) %collective-permute-start.10) | collective-permute-done | bytes 327712 | tf_op jit(solution)/shard_map/ppermute | solution.py:222
  90.0 0.0 collective-permute-done.8
  90.0 0.0 collective-permute-done.7
  90.0 0.7 collective-permute-start.15
  90.7 0.1 pad_maximum_fusion.refs_5_
  90.8 4.8 %collective-permute-start.12 = (bf16[2,2560,128]{2,1,0:T(8,128)(2,1)S(1)}, bf16[2,2560,128]{2,1,0:T(8,128)(2,1)S(1)}, u32[]{:S(2)}, u32[]{:S(2)}) collective-permute-start(bf16[2,2560,128]{2,1,0:T(8,128)(2,1)S(1)} %pad_maximum_fusion.refs_5_), channel_id=1, source_target_pairs={{0,24},{1,97},{2,26},{3,99},{4,28},{5,101},{6,30},{7,103},{8,0},{9... | collective-permute-start | bytes 3932168 | tf_op jit(solution)/shard_map/ppermute | solution.py:198
  95.6 3.8 %collective-permute-start.16 = (bf16[1280,128]{1,0:T(8,128)(2,1)S(1)}, bf16[1280,128]{1,0:T(8,128)(2,1)S(1)}, u32[]{:S(2)}, u32[]{:S(2)}) collective-permute-start(bf16[1280,128]{1,0:T(8,128)(2,1)S(1)} %collective-permute-done.10), channel_id=1, source_target_pairs={{2,10},{7,30},{4,44},{1,56},{6,78},{3,90},{0,104},{5,124},{10,11},... | collective-permute-start | bytes 983048 | tf_op jit(solution)/shard_map/ppermute | solution.py:228
  99.5 0.6 collective-permute-start.13
  100.1 7.5 %collective-permute-start.14 = (bf16[1280,128]{1,0:T(8,128)(2,1)S(1)}, bf16[1280,128]{1,0:T(8,128)(2,1)S(1)}, u32[]{:S(2)}, u32[]{:S(2)}) collective-permute-start(bf16[1280,128]{1,0:T(8,128)(2,1)S(1)} %slice.31), channel_id=1, source_target_pairs={{0,32},{1,9},{2,34},{3,11},{4,36},{5,13},{6,38},{7,15},{8,40},{9,1... | collective-permute-start | bytes 983048 | tf_op jit(solution)/shard_map/ppermute | solution.py:198
  107.6 14.9 %collective-permute-done.16 = bf16[1280,128]{1,0:T(8,128)(2,1)S(1)} collective-permute-done((bf16[1280,128]{1,0:T(8,128)(2,1)S(1)}, bf16[1280,128]{1,0:T(8,128)(2,1)S(1)}, u32[]{:S(2)}, u32[]{:S(2)}) %collective-permute-start.16) | collective-permute-done | bytes 327712 | tf_op jit(solution)/shard_map/ppermute | solution.py:228
  122.5 0.1 pad_maximum_fusion.4
  122.6 0.0 collective-permute-done.13
  122.7 0.1 pad_maximum_fusion.1.refs_6_
  122.8 0.0 collective-permute-done.11.refs_7_
  122.8 2.1 %collective-permute-start.18 = (bf16[2,2560,128]{2,1,0:T(8,128)(2,1)S(1)}, bf16[2,2560,128]{2,1,0:T(8,128)(2,1)S(1)}, u32[]{:S(2)}, u32[]{:S(2)}) collective-permute-start(bf16[2,2560,128]{2,1,0:T(8,128)(2,1)S(1)} %pad_maximum_fusion.1.refs_6_), channel_id=1, source_target_pairs={{0,24},{1,97},{2,26},{3,99},{4,28},{5,101},{6,30},{7,103},{8,0},{9... | collective-permute-start | bytes 3932168 | tf_op jit(solution)/shard_map/ppermute | solution.py:198
  125.0 0.0 collective-permute-start.17
  125.0 2.9 %collective-permute-start.20 = (bf16[2,1280,128]{2,1,0:T(8,128)(2,1)S(1)}, bf16[2,1280,128]{2,1,0:T(8,128)(2,1)S(1)}, u32[]{:S(2)}, u32[]{:S(2)}) collective-permute-start(bf16[2,1280,128]{2,1,0:T(8,128)(2,1)S(1)} %pad_maximum_fusion.4), channel_id=1, source_target_pairs={{0,6},{2,0},{4,2},{6,4},{1,7},{3,1},{5,3},{7,5},{8,14},{10,8},{12,... | collective-permute-start | bytes 1966088 | tf_op jit(solution)/shard_map/ppermute | solution.py:169
  127.9 10.2 %collective-permute-done.20 = bf16[2,1280,128]{2,1,0:T(8,128)(2,1)S(1)} collective-permute-done((bf16[2,1280,128]{2,1,0:T(8,128)(2,1)S(1)}, bf16[2,1280,128]{2,1,0:T(8,128)(2,1)S(1)}, u32[]{:S(2)}, u32[]{:S(2)}) %collective-permute-start.20) | collective-permute-done | bytes 655392 | tf_op jit(solution)/shard_map/ppermute | solution.py:169
  138.0 3.9 %collective-permute-done.19 = bf16[2,1280,128]{2,1,0:T(8,128)(2,1)S(1)} collective-permute-done((bf16[2,1280,128]{2,1,0:T(8,128)(2,1)S(1)}, bf16[2,1280,128]{2,1,0:T(8,128)(2,1)S(1)}, u32[]{:S(2)}, u32[]{:S(2)}) %collective-permute-start.19) | collective-permute-done | bytes 655392 | tf_op jit(solution)/shard_map/ppermute | solution.py:169
  141.9 5.5 %collective-permute-done.17.refs_8_ = bf16[2,2560,128]{2,1,0:T(8,128)(2,1)S(1)} collective-permute-done((bf16[2,2560,128]{2,1,0:T(8,128)(2,1)S(1)}, bf16[2,2560,128]{2,1,0:T(8,128)(2,1)S(1)}, u32[]{:S(2)}, u32[]{:S(2)}) %collective-permute-start.17) | collective-permute-done | bytes 1310752 | tf_op jit(solution)/shard_map/ppermute | solution.py:198
  147.5 0.1 collective-permute-start.21
  147.5 2.0 %collective-permute-start.22 = (bf16[1280,128]{1,0:T(8,128)(2,1)S(1)}, bf16[1280,128]{1,0:T(8,128)(2,1)S(1)}, u32[]{:S(2)}, u32[]{:S(2)}) collective-permute-start(bf16[1280,128]{1,0:T(8,128)(2,1)S(1)} %slice_bitcast_fusion), channel_id=1, source_target_pairs={{0,2},{2,4},{4,6},{6,0},{1,3},{3,5},{5,7},{7,1},{8,10},{10,12},{12... | collective-permute-start | bytes 983048 | tf_op jit(solution)/shard_map/ppermute | solution.py:169
  149.5 2.0 %collective-permute-start.25 = (bf16[2,2560,128]{2,1,0:T(8,128)(2,1)S(1)}, bf16[2,2560,128]{2,1,0:T(8,128)(2,1)S(1)}, u32[]{:S(2)}, u32[]{:S(2)}) collective-permute-start(bf16[2,2560,128]{2,1,0:T(8,128)(2,1)S(1)} %collective-permute-done.12.refs_9_), channel_id=1, source_target_pairs={{0,24},{1,97},{2,26},{3,99},{4,28},{5,101},{6,30},{7,103},{8,0},{9... | collective-permute-start | bytes 3932168 | tf_op jit(solution)/shard_map/ppermute | solution.py:198
  151.6 0.1 pad_maximum_fusion.2.refs_1_
  151.7 0.1 collective-permute-start.23
  151.8 0.2 collective-permute-start.26
  152.0 5.8 %collective-permute-done.21 = bf16[1280,128]{1,0:T(8,128)(2,1)S(1)} collective-permute-done((bf16[1280,128]{1,0:T(8,128)(2,1)S(1)}, bf16[1280,128]{1,0:T(8,128)(2,1)S(1)}, u32[]{:S(2)}, u32[]{:S(2)}) %collective-permute-start.21) | collective-permute-done | bytes 327712 | tf_op jit(solution)/shard_map/ppermute | solution.py:169
  157.8 0.1 maximum_bitcast_fusion.1
  157.9 0.1 pad_maximum_fusion.3.refs_2_
  158.0 1.8 collective-permute-start.24
  159.8 0.1 pad_add_fusion.refs_0_
  159.9 7.4 %collective-permute-done.25.refs_11_ = bf16[2,2560,128]{2,1,0:T(8,128)(2,1)S(1)} collective-permute-done((bf16[2,2560,128]{2,1,0:T(8,128)(2,1)S(1)}, bf16[2,2560,128]{2,1,0:T(8,128)(2,1)S(1)}, u32[]{:S(2)}, u32[]{:S(2)}) %collective-permute-start.25) | collective-permute-done | bytes 1310752 | tf_op jit(solution)/shard_map/ppermute | solution.py:198
  167.3 3.4 %collective-permute-done.26.refs_12_ = bf16[2,2560,128]{2,1,0:T(8,128)(2,1)S(1)} collective-permute-done((bf16[2,2560,128]{2,1,0:T(8,128)(2,1)S(1)}, bf16[2,2560,128]{2,1,0:T(8,128)(2,1)S(1)}, u32[]{:S(2)}, u32[]{:S(2)}) %collective-permute-start.26) | collective-permute-done | bytes 1310752 | tf_op jit(solution)/shard_map/ppermute | solution.py:198
  170.7 20.5 %exchange.1 = f32[1280,2560]{1,0:T(8,128)} custom-call(s32[4]{0:T(128)S(1)} %pad_add_fusion.refs_0_, bf16[2,2,1280,128]{3,2,1,0:T(8,128)(2,1)S(1)} %pad_maximum_fusion.2.refs_1_, bf16[2,2,1280,128]{3,2,1,0:T(8,128)(2,1)S(1)} %pad_maximum_fusion.3.refs_2_, bf16[2,2,1280,128]{3,2,1,0:T(8,128)(2,1)S(1)} %collective-permute-done.23.refs_3_, ...), custom_call_target="tpu_custom_call" | custom-call | tf_op jit(solution)/shard_map/exchange/pallas_call | solution.py:321
  (24 shorter events, 0.3 us)
Async XLA Ops:
  0.0 43.3 %copy-start = (s32[16384]{0:T(1024)S(1)}, s32[16384]{0:T(1024)}, u32[]{:S(2)}) copy-start(s32[16384]{0:T(1024)} %param.8) | copy-start | bytes 196612
  43.3 4.3 %collective-permute-start = (bf16[256,32,128]{2,1,0:T(8,128)(2,1)S(1)}, bf16[256,32,128]{2,1,0:T(8,128)(2,1)}, u32[]{:S(2)}, u32[]{:S(2)}) collective-permute-start(bf16[256,32,128]{2,1,0:T(8,128)(2,1)S(1)} %all_to_all.5.own_ref), channel_id=1, source_target_pairs={{0,1},{1,0},{2,3},{3,2},{4,5},{5,4},{6,7},{7,6},{8,9},{9,8},{10,11... | collective-permute-start | bytes 6291464 | tf_op jit(solution)/shard_map/ppermute | solution.py:373
  50.9 11.8 %collective-permute-start.1 = (bf16[40,32,128]{2,1,0:T(8,128)(2,1)S(1)}, bf16[40,32,128]{2,1,0:T(8,128)(2,1)S(1)}, u32[]{:S(2)}, u32[]{:S(2)}) collective-permute-start(bf16[40,32,128]{2,1,0:T(8,128)(2,1)S(1)} %get-tuple-element.26), channel_id=1, source_target_pairs={{0,2},{2,4},{4,6},{6,0},{1,3},{3,5},{5,7},{7,1},{8,10},{10,12},{12... | collective-permute-start | bytes 983048 | tf_op jit(solution)/shard_map/ppermute | solution.py:169
  52.3 10.7 %collective-permute-start.5 = (bf16[40,32,128]{2,1,0:T(8,128)(2,1)S(1)}, bf16[40,32,128]{2,1,0:T(8,128)(2,1)S(1)}, u32[]{:S(2)}, u32[]{:S(2)}) collective-permute-start(bf16[40,32,128]{2,1,0:T(8,128)(2,1)S(1)} %get-tuple-element.30), channel_id=1, source_target_pairs={{0,6},{2,0},{4,2},{6,4},{1,7},{3,1},{5,3},{7,5},{8,14},{10,8},{12,... | collective-permute-start | bytes 983048 | tf_op jit(solution)/shard_map/ppermute | solution.py:169
  54.2 15.6 %collective-permute-start.3 = (bf16[40,32,128]{2,1,0:T(8,128)(2,1)S(1)}, bf16[40,32,128]{2,1,0:T(8,128)(2,1)S(1)}, u32[]{:S(2)}, u32[]{:S(2)}) collective-permute-start(bf16[40,32,128]{2,1,0:T(8,128)(2,1)S(1)} %get-tuple-element.27), channel_id=1, source_target_pairs={{0,2},{2,4},{4,6},{6,0},{1,3},{3,5},{5,7},{7,1},{8,10},{10,12},{12... | collective-permute-start | bytes 983048 | tf_op jit(solution)/shard_map/ppermute | solution.py:169
  54.4 15.6 %collective-permute-start.4 = (bf16[40,32,128]{2,1,0:T(8,128)(2,1)S(1)}, bf16[40,32,128]{2,1,0:T(8,128)(2,1)S(1)}, u32[]{:S(2)}, u32[]{:S(2)}) collective-permute-start(bf16[40,32,128]{2,1,0:T(8,128)(2,1)S(1)} %get-tuple-element.28), channel_id=1, source_target_pairs={{0,6},{2,0},{4,2},{6,4},{1,7},{3,1},{5,3},{7,5},{8,14},{10,8},{12,... | collective-permute-start | bytes 983048 | tf_op jit(solution)/shard_map/ppermute | solution.py:169
  62.8 13.1 %collective-permute-start.2 = (bf16[40,32,128]{2,1,0:T(8,128)(2,1)S(1)}, bf16[40,32,128]{2,1,0:T(8,128)(2,1)S(1)}, u32[]{:S(2)}, u32[]{:S(2)}) collective-permute-start(bf16[40,32,128]{2,1,0:T(8,128)(2,1)S(1)} %add_convert_fusion.2), channel_id=1, source_target_pairs={{0,2},{2,4},{4,6},{6,0},{1,3},{3,5},{5,7},{7,1},{8,10},{10,12},{12... | collective-permute-start | bytes 983048 | tf_op jit(solution)/shard_map/ppermute | solution.py:169
  63.1 12.9 %collective-permute-start.6 = (bf16[40,32,128]{2,1,0:T(8,128)(2,1)S(1)}, bf16[40,32,128]{2,1,0:T(8,128)(2,1)S(1)}, u32[]{:S(2)}, u32[]{:S(2)}) collective-permute-start(bf16[40,32,128]{2,1,0:T(8,128)(2,1)S(1)} %add_convert_fusion.1), channel_id=1, source_target_pairs={{0,6},{2,0},{4,2},{6,4},{1,7},{3,1},{5,3},{7,5},{8,14},{10,8},{12,... | collective-permute-start | bytes 983048 | tf_op jit(solution)/shard_map/ppermute | solution.py:169
  76.3 13.8 %collective-permute-start.8 = (bf16[2560,128]{1,0:T(8,128)(2,1)S(1)}, bf16[2560,128]{1,0:T(8,128)(2,1)S(1)}, u32[]{:S(2)}, u32[]{:S(2)}) collective-permute-start(bf16[2560,128]{1,0:T(8,128)(2,1)S(1)} %bitcast.109), channel_id=1, source_target_pairs={{0,96},{1,25},{2,98},{3,27},{4,100},{5,29},{6,102},{7,31},{8,104},... | collective-permute-start | bytes 1966088 | tf_op jit(solution)/shard_map/ppermute | solution.py:198
  77.1 12.9 %collective-permute-start.7 = (bf16[2560,128]{1,0:T(8,128)(2,1)S(1)}, bf16[2560,128]{1,0:T(8,128)(2,1)S(1)}, u32[]{:S(2)}, u32[]{:S(2)}) collective-permute-start(bf16[2560,128]{1,0:T(8,128)(2,1)S(1)} %bitcast.110), channel_id=1, source_target_pairs={{0,32},{1,9},{2,34},{3,11},{4,36},{5,13},{6,38},{7,15},{8,40},{9,1... | collective-permute-start | bytes 1966088 | tf_op jit(solution)/shard_map/ppermute | solution.py:198
  78.4 4.1 %collective-permute-start.9 = (bf16[1280,128]{1,0:T(8,128)(2,1)S(1)}, bf16[1280,128]{1,0:T(8,128)(2,1)S(1)}, u32[]{:S(2)}, u32[]{:S(2)}) collective-permute-start(bf16[1280,128]{1,0:T(8,128)(2,1)S(1)} %bitcast.122), channel_id=1, source_target_pairs={{0,0},{1,5},{2,2},{3,7},{4,4},{5,1},{6,6},{7,3},{8,8},{9,13},{10,1... | collective-permute-start | bytes 983048 | tf_op jit(solution)/shard_map/ppermute | solution.py:222
  79.1 10.9 %collective-permute-start.10 = (bf16[1280,128]{1,0:T(8,128)(2,1)S(1)}, bf16[1280,128]{1,0:T(8,128)(2,1)S(1)}, u32[]{:S(2)}, u32[]{:S(2)}) collective-permute-start(bf16[1280,128]{1,0:T(8,128)(2,1)S(1)} %bitcast.121), channel_id=1, source_target_pairs={{0,2},{1,7},{2,4},{3,1},{4,6},{5,3},{6,0},{7,5},{8,10},{9,15},{10,... | collective-permute-start | bytes 983048 | tf_op jit(solution)/shard_map/ppermute | solution.py:222
  90.0 10.1 %collective-permute-start.15 = (bf16[1280,128]{1,0:T(8,128)(2,1)S(1)}, bf16[1280,128]{1,0:T(8,128)(2,1)S(1)}, u32[]{:S(2)}, u32[]{:S(2)}) collective-permute-start(bf16[1280,128]{1,0:T(8,128)(2,1)S(1)} %collective-permute-done.9), channel_id=1, source_target_pairs={{0,0},{5,20},{2,34},{7,54},{4,68},{1,80},{6,102},{3,114},{8,1},{13... | collective-permute-start | bytes 983048 | tf_op jit(solution)/shard_map/ppermute | solution.py:228
  90.8 32.0 %collective-permute-start.12 = (bf16[2,2560,128]{2,1,0:T(8,128)(2,1)S(1)}, bf16[2,2560,128]{2,1,0:T(8,128)(2,1)S(1)}, u32[]{:S(2)}, u32[]{:S(2)}) collective-permute-start(bf16[2,2560,128]{2,1,0:T(8,128)(2,1)S(1)} %pad_maximum_fusion.refs_5_), channel_id=1, source_target_pairs={{0,24},{1,97},{2,26},{3,99},{4,28},{5,101},{6,30},{7,103},{8,0},{9... | collective-permute-start | bytes 3932168 | tf_op jit(solution)/shard_map/ppermute | solution.py:198
  95.6 27.2 %collective-permute-start.11 = (bf16[2,2560,128]{2,1,0:T(8,128)(2,1)S(1)}, bf16[2,2560,128]{2,1,0:T(8,128)(2,1)S(1)}, u32[]{:S(2)}, u32[]{:S(2)}) collective-permute-start(bf16[2,2560,128]{2,1,0:T(8,128)(2,1)S(1)} %pad_maximum_fusion.refs_5_), channel_id=1, source_target_pairs={{0,8},{1,33},{2,10},{3,35},{4,12},{5,37},{6,14},{7,39},{8,16},{9,4... | collective-permute-start | bytes 3932168 | tf_op jit(solution)/shard_map/ppermute | solution.py:198
  95.6 26.9 %collective-permute-start.16 = (bf16[1280,128]{1,0:T(8,128)(2,1)S(1)}, bf16[1280,128]{1,0:T(8,128)(2,1)S(1)}, u32[]{:S(2)}, u32[]{:S(2)}) collective-permute-start(bf16[1280,128]{1,0:T(8,128)(2,1)S(1)} %collective-permute-done.10), channel_id=1, source_target_pairs={{2,10},{7,30},{4,44},{1,56},{6,78},{3,90},{0,104},{5,124},{10,11},... | collective-permute-start | bytes 983048 | tf_op jit(solution)/shard_map/ppermute | solution.py:228
  99.5 23.1 %collective-permute-start.13 = (bf16[1280,128]{1,0:T(8,128)(2,1)S(1)}, bf16[1280,128]{1,0:T(8,128)(2,1)S(1)}, u32[]{:S(2)}, u32[]{:S(2)}) collective-permute-start(bf16[1280,128]{1,0:T(8,128)(2,1)S(1)} %slice.30), channel_id=1, source_target_pairs={{0,96},{1,25},{2,98},{3,27},{4,100},{5,29},{6,102},{7,31},{8,104},... | collective-permute-start | bytes 983048 | tf_op jit(solution)/shard_map/ppermute | solution.py:198
  100.1 22.5 %collective-permute-start.14 = (bf16[1280,128]{1,0:T(8,128)(2,1)S(1)}, bf16[1280,128]{1,0:T(8,128)(2,1)S(1)}, u32[]{:S(2)}, u32[]{:S(2)}) collective-permute-start(bf16[1280,128]{1,0:T(8,128)(2,1)S(1)} %slice.31), channel_id=1, source_target_pairs={{0,32},{1,9},{2,34},{3,11},{4,36},{5,13},{6,38},{7,15},{8,40},{9,1... | collective-permute-start | bytes 983048 | tf_op jit(solution)/shard_map/ppermute | solution.py:198
  122.8 19.1 %collective-permute-start.18 = (bf16[2,2560,128]{2,1,0:T(8,128)(2,1)S(1)}, bf16[2,2560,128]{2,1,0:T(8,128)(2,1)S(1)}, u32[]{:S(2)}, u32[]{:S(2)}) collective-permute-start(bf16[2,2560,128]{2,1,0:T(8,128)(2,1)S(1)} %pad_maximum_fusion.1.refs_6_), channel_id=1, source_target_pairs={{0,24},{1,97},{2,26},{3,99},{4,28},{5,101},{6,30},{7,103},{8,0},{9... | collective-permute-start | bytes 3932168 | tf_op jit(solution)/shard_map/ppermute | solution.py:198
  125.0 22.4 %collective-permute-start.17 = (bf16[2,2560,128]{2,1,0:T(8,128)(2,1)S(1)}, bf16[2,2560,128]{2,1,0:T(8,128)(2,1)S(1)}, u32[]{:S(2)}, u32[]{:S(2)}) collective-permute-start(bf16[2,2560,128]{2,1,0:T(8,128)(2,1)S(1)} %pad_maximum_fusion.1.refs_6_), channel_id=1, source_target_pairs={{0,8},{1,33},{2,10},{3,35},{4,12},{5,37},{6,14},{7,39},{8,16},{9,4... | collective-permute-start | bytes 3932168 | tf_op jit(solution)/shard_map/ppermute | solution.py:198
  125.0 13.1 %collective-permute-start.20 = (bf16[2,1280,128]{2,1,0:T(8,128)(2,1)S(1)}, bf16[2,1280,128]{2,1,0:T(8,128)(2,1)S(1)}, u32[]{:S(2)}, u32[]{:S(2)}) collective-permute-start(bf16[2,1280,128]{2,1,0:T(8,128)(2,1)S(1)} %pad_maximum_fusion.4), channel_id=1, source_target_pairs={{0,6},{2,0},{4,2},{6,4},{1,7},{3,1},{5,3},{7,5},{8,14},{10,8},{12,... | collective-permute-start | bytes 1966088 | tf_op jit(solution)/shard_map/ppermute | solution.py:169
  127.9 14.1 %collective-permute-start.19 = (bf16[2,1280,128]{2,1,0:T(8,128)(2,1)S(1)}, bf16[2,1280,128]{2,1,0:T(8,128)(2,1)S(1)}, u32[]{:S(2)}, u32[]{:S(2)}) collective-permute-start(bf16[2,1280,128]{2,1,0:T(8,128)(2,1)S(1)} %pad_maximum_fusion.4), channel_id=1, source_target_pairs={{0,2},{2,4},{4,6},{6,0},{1,3},{3,5},{5,7},{7,1},{8,10},{10,12},{12... | collective-permute-start | bytes 1966088 | tf_op jit(solution)/shard_map/ppermute | solution.py:169
  147.5 10.4 %collective-permute-start.21 = (bf16[1280,128]{1,0:T(8,128)(2,1)S(1)}, bf16[1280,128]{1,0:T(8,128)(2,1)S(1)}, u32[]{:S(2)}, u32[]{:S(2)}) collective-permute-start(bf16[1280,128]{1,0:T(8,128)(2,1)S(1)} %slice_bitcast_fusion.1), channel_id=1, source_target_pairs={{0,6},{2,0},{4,2},{6,4},{1,7},{3,1},{5,3},{7,5},{8,14},{10,8},{12,... | collective-permute-start | bytes 983048 | tf_op jit(solution)/shard_map/ppermute | solution.py:169
  147.5 10.3 %collective-permute-start.22 = (bf16[1280,128]{1,0:T(8,128)(2,1)S(1)}, bf16[1280,128]{1,0:T(8,128)(2,1)S(1)}, u32[]{:S(2)}, u32[]{:S(2)}) collective-permute-start(bf16[1280,128]{1,0:T(8,128)(2,1)S(1)} %slice_bitcast_fusion), channel_id=1, source_target_pairs={{0,2},{2,4},{4,6},{6,0},{1,3},{3,5},{5,7},{7,1},{8,10},{10,12},{12... | collective-permute-start | bytes 983048 | tf_op jit(solution)/shard_map/ppermute | solution.py:169
  149.5 17.8 %collective-permute-start.25 = (bf16[2,2560,128]{2,1,0:T(8,128)(2,1)S(1)}, bf16[2,2560,128]{2,1,0:T(8,128)(2,1)S(1)}, u32[]{:S(2)}, u32[]{:S(2)}) collective-permute-start(bf16[2,2560,128]{2,1,0:T(8,128)(2,1)S(1)} %collective-permute-done.12.refs_9_), channel_id=1, source_target_pairs={{0,24},{1,97},{2,26},{3,99},{4,28},{5,101},{6,30},{7,103},{8,0},{9... | collective-permute-start | bytes 3932168 | tf_op jit(solution)/shard_map/ppermute | solution.py:198
  151.7 15.6 %collective-permute-start.23 = (bf16[2,2,1280,128]{3,2,1,0:T(8,128)(2,1)S(1)}, bf16[2,2,1280,128]{3,2,1,0:T(8,128)(2,1)S(1)}, u32[]{:S(2)}, u32[]{:S(2)}) collective-permute-start(bf16[2,2,1280,128]{3,2,1,0:T(8,128)(2,1)S(1)} %pad_maximum_fusion.2.refs_1_), channel_id=1, source_target_pairs={{0,1},{1,0},{2,3},{3,2},{4,5},{5,4},{6,7},{7,6},{8,9},{9,8},{10,11... | collective-permute-start | bytes 3932168 | tf_op jit(solution)/shard_map/ppermute | solution.py:239
  151.8 18.9 %collective-permute-start.26 = (bf16[2,2560,128]{2,1,0:T(8,128)(2,1)S(1)}, bf16[2,2560,128]{2,1,0:T(8,128)(2,1)S(1)}, u32[]{:S(2)}, u32[]{:S(2)}) collective-permute-start(bf16[2,2560,128]{2,1,0:T(8,128)(2,1)S(1)} %collective-permute-done.17.refs_8_), channel_id=1, source_target_pairs={{0,8},{1,33},{2,10},{3,35},{4,12},{5,37},{6,14},{7,39},{8,16},{9,4... | collective-permute-start | bytes 3932168 | tf_op jit(solution)/shard_map/ppermute | solution.py:198
  158.0 12.7 %collective-permute-start.24 = (bf16[2,2,1280,128]{3,2,1,0:T(8,128)(2,1)S(1)}, bf16[2,2,1280,128]{3,2,1,0:T(8,128)(2,1)S(1)}, u32[]{:S(2)}, u32[]{:S(2)}) collective-permute-start(bf16[2,2,1280,128]{3,2,1,0:T(8,128)(2,1)S(1)} %pad_maximum_fusion.3.refs_2_), channel_id=1, source_target_pairs={{0,1},{1,0},{2,3},{3,2},{4,5},{5,4},{6,7},{7,6},{8,9},{9,8},{10,11... | collective-permute-start | bytes 3932168 | tf_op jit(solution)/shard_map/ppermute | solution.py:239
